TPU v7x, 512 devices: a whole 4x8x8 slice. The times are simulated.
512 devices in a mesh: seq: 64 (over y_lo, z, core), head: 8 (over y_hi, x).
Axes of the slice: x: 4, y: 8 (y_hi: 2, y_lo: 4; y = y_hi * 4 + y_lo), z: 8, core: 2. Of those that a mesh axis runs over, the one named last changes fastest.
Arguments:
- layer_input: bfloat16 [8192, 2048], P('seq', 'head'), may hold values from -6 to 6
- w_input: bfloat16 [2048, 4096], P('seq', 'head'), may hold values from -0.125 to 0.125
- w_gate: bfloat16 [2048, 4096], P('seq', 'head'), may hold values from -0.125 to 0.125
- w_maps: bfloat16 [2048, 256], P('seq'), may hold values from -0.125 to 0.125
- w_step: bfloat16 [2048, 64], P('seq', 'head'), may hold values from -0.125 to 0.125
- step_bias: float32 [64], P('head'), may hold values from -6 to -3
- decay_log: float32 [64], P('head'), may hold values from -8 to 0
- skip_gain: float32 [64], P('head'), may hold values from 0.5 to 1.5
- conv_input: float32 [4, 4096], P(None, 'head'), may hold values from -3 to 3
- conv_maps: float32 [4, 256], replicated, may hold values from -3 to 3
- norm_gain: float32 [4096], P('head'), may hold values from 0.1 to 1.9
- w_out: bfloat16 [4096, 2048], P('head', 'seq'), may hold values from -0.09375 to 0.09375
Outputs:
- mixed: bfloat16 [8192, 2048], P('seq', 'head')
All inputs are finite; a program needn't handle non-finite values.
Results may differ from a plain program's by a relative error of at most 0.015.
Values may be sent and summed in bfloat16 or wider, within the bound.
No kernel may reach another device: no remote copies, remote signals or barrier semaphores. Data moves between devices by JAX's collectives and lax.ppermute only.
A program may use at most 128 MiB of HBM per device.

v0:
```python
import jax
import jax.numpy as jnp
from jax import lax
from jax.sharding import PartitionSpec as P

HEAD_DIM = 64
SPAN = 128
CONV = 4
GROUP_HEADS = 8


def partner(block, axis, bit):
    count = lax.axis_size(axis)
    route = []
    for low in range(count):
        high = low | 1 << bit
        if high != low and high < count:
            route += [(low, high), (high, low)]
    return lax.ppermute(block, axis, route)


def shifted(value, axis, steps):
    count = lax.axis_size(axis)
    initial, last = (max(0, -steps), min(count, count - steps))
    return lax.ppermute(value, axis, [(source, source + steps) for source in range(initial, last)])


def carried_in(part, axis, combine, identity):
    place = lax.axis_index(axis)
    gathered = jax.tree.map(lambda a: lax.all_gather(a, axis), part)
    state = jax.tree.map(lambda a, e: jnp.zeros_like(a) + jnp.asarray(e, a.dtype), part, identity)

    def one(lap, state):
        return combine(
            state, jax.tree.map(lambda a: lax.dynamic_index_in_dim(a, lap, 0, False), gathered)
        )

    return lax.fori_loop(0, place, one, state)


def join_states(earlier, later):
    state_one, gain_one = earlier
    state_two, gain_two = later
    return (state_one * gain_two[..., None, None] + state_two, gain_one * gain_two)


def local(
    layer_input,
    w_input,
    w_gate,
    w_maps,
    w_step,
    step_bias,
    decay_log,
    skip_gain,
    conv_input,
    conv_maps,
    norm_gain,
    w_out,
):
    seq_rows = layer_input.shape[0]
    bit_count = lax.axis_size("seq").bit_length() - 1
    mirrored = layer_input
    for bit_index in range(bit_count):
        mirrored = partner(mirrored, "seq", bit_index)
    forward_in, mirror_full = (
        lax.all_gather(layer_input, "head", axis=1, tiled=True),
        lax.all_gather(mirrored, "head", axis=1, tiled=True),
    )
    reversed_in = mirror_full[::-1, ::-1]
    inputs = jnp.concatenate([forward_in, reversed_in], 0)
    width_x = w_input.shape[1]
    head_count = w_step.shape[1]
    state_size = w_maps.shape[1] // 2
    full_x, full_z, full_bc, full_dt = (
        lax.all_gather(w_input, "seq", axis=0, tiled=True),
        lax.all_gather(w_gate, "seq", axis=0, tiled=True),
        lax.all_gather(w_maps, "seq", axis=0, tiled=True),
        lax.all_gather(w_step, "seq", axis=0, tiled=True),
    )
    proj_x = jnp.dot(inputs, full_x, preferred_element_type=jnp.float32)
    proj_z = jnp.dot(inputs, full_z, preferred_element_type=jnp.float32)
    proj_bc = jnp.dot(inputs, full_bc, preferred_element_type=jnp.float32)
    proj_dt = jnp.dot(inputs, full_dt, preferred_element_type=jnp.float32)
    joined = jnp.concatenate([proj_x, proj_bc], 1).astype(jnp.bfloat16).reshape(2, seq_rows, -1)
    gate_rows = proj_z.astype(jnp.bfloat16).reshape(2, seq_rows, width_x)
    step_size = jax.nn.softplus(proj_dt + step_bias).reshape(2, seq_rows, head_count)
    decay_rate = step_size * -jnp.exp(decay_log)
    tail_rows = joined[:, seq_rows - (CONV - 1) :]
    rim_rows = shifted(tail_rows, "seq", 1)
    extended = jnp.concatenate([rim_rows, joined], 1).astype(jnp.float32)
    tap_table = jnp.concatenate([conv_input, conv_maps], 1)
    running = tap_table[0] * extended[:, 0:seq_rows]
    for tap_index in range(1, CONV):
        running = running + tap_table[tap_index] * extended[:, tap_index : tap_index + seq_rows]
    convolved = jax.nn.silu(running).astype(jnp.bfloat16)
    blocks = seq_rows // SPAN
    x_heads = convolved[..., :width_x].reshape(2, blocks, SPAN, head_count, HEAD_DIM)
    in_maps = convolved[..., width_x : width_x + state_size].reshape(2, blocks, SPAN, state_size)
    out_maps = convolved[..., width_x + state_size :].reshape(2, blocks, SPAN, state_size)
    step_blocks = step_size.reshape(2, blocks, SPAN, head_count)
    rate_blocks = decay_rate.reshape(2, blocks, SPAN, head_count)
    cumulated = jnp.cumsum(rate_blocks, axis=2)
    scores = jnp.einsum("bcln,bcsn->bcls", out_maps, in_maps, preferred_element_type=jnp.float32)
    cum_heads = jnp.moveaxis(cumulated, 3, 2)
    differ = cum_heads[..., :, None] - cum_heads[..., None, :]
    lower_mask = lax.broadcasted_iota(jnp.int32, (SPAN, SPAN), 0) >= lax.broadcasted_iota(
        jnp.int32, (SPAN, SPAN), 1
    )
    decay_mat = jnp.where(lower_mask, jnp.exp(jnp.where(lower_mask, differ, 0.0)), 0.0)
    weights_m = (
        scores[:, :, None] * decay_mat * jnp.moveaxis(step_blocks, 3, 2)[..., None, :]
    ).astype(jnp.bfloat16)
    inner_out = jnp.einsum(
        "bchls,bcshp->bclhp", weights_m, x_heads, preferred_element_type=jnp.float32
    )
    end_weight = jnp.exp(cumulated[:, :, -1:, :] - cumulated) * step_blocks
    input_weighted = (x_heads.astype(jnp.float32) * end_weight[..., None]).astype(jnp.bfloat16)
    block_states = jnp.einsum(
        "bcshp,bcsn->bchpn", input_weighted, in_maps, preferred_element_type=jnp.float32
    )
    block_gain = jnp.exp(cumulated[:, :, -1, :])
    local_state = jnp.zeros_like(block_states[:, 0])
    local_state = block_gain[:, 0][..., None, None] * local_state + block_states[:, 0]
    local_gain = jnp.prod(block_gain, axis=1)
    entering, gain_in = carried_in(
        (local_state, local_gain),
        "seq",
        join_states,
        (jnp.zeros_like(local_state), jnp.ones_like(local_gain)),
    )
    entries = [entering]
    entry_states = jnp.stack(entries, 1)
    state_out = (
        jnp.einsum(
            "bcln,bchpn->bclhp",
            out_maps.astype(jnp.float32),
            entry_states,
            precision=lax.Precision.HIGHEST,
        )
        * jnp.exp(cumulated)[..., None]
    )
    skip_local = skip_gain[:, None]
    ssd_out = inner_out + state_out + skip_local * x_heads.astype(jnp.float32)
    gated_out = ssd_out.reshape(2, seq_rows, width_x) * jax.nn.silu(gate_rows.astype(jnp.float32))
    grouped = gated_out.reshape(2, seq_rows, -1, GROUP_HEADS * HEAD_DIM)
    mean_square = jnp.mean(grouped * grouped, axis=-1, keepdims=True)
    normed = (grouped * lax.rsqrt(mean_square + 1e-05)).reshape(2, seq_rows, width_x)
    outputs = (normed * norm_gain).astype(jnp.bfloat16)
    forward_mix = outputs[0]
    mirror_mix = outputs[1]
    for bit_index in range(bit_count):
        mirror_mix = partner(mirror_mix, "seq", bit_index)
    mirror_mix = mirror_mix[::-1]
    weight_piece = lax.all_gather(w_out, "seq", axis=1, tiled=True)
    term_pair = jnp.stack(
        [
            jnp.dot(forward_mix, weight_piece, preferred_element_type=jnp.float32),
            jnp.dot(mirror_mix, weight_piece, preferred_element_type=jnp.float32),
        ]
    )
    partial_sum = term_pair[0] + term_pair[1][:, ::-1]
    return lax.psum_scatter(partial_sum, "head", scatter_dimension=1, tiled=True).astype(
        jnp.bfloat16
    )


def solution(mesh):
    placed = (
        P("seq", "head"),
        P("seq", "head"),
        P("seq", "head"),
        P("seq", None),
        P("seq", "head"),
        P("head"),
        P("head"),
        P("head"),
        P(None, "head"),
        P(),
        P("head"),
        P("head", "seq"),
    )
    return jax.shard_map(
        local, mesh=mesh, in_specs=placed, out_specs=P("seq", "head"), check_vma=False
    )
```

profile of v0, /device:TPU:1, one launch (start us, length us, event | category | flops | bytes accessed | tf_op | source)
XLA Modules:
  0.0 796.9 jit_solution(16857249031667318250)
XLA Ops:
  8.8 8.8 %collective-permute-start = (bf16[128,256]{1,0:T(8,128)(2,1)}, bf16[128,256]{1,0:T(8,128)(2,1)S(1)}, u32[]{:S(2)}, u32[]{:S(2)}) collective-permute-start(bf16[128,256]{1,0:T(8,128)(2,1)} %param.14), channel_id=1, source_target_pairs={{0,8},{8,0},{16,24},{24,16},{32,40},{40,32},{48,56},{56,48},{64,72... | collective-permute-start | bytes 196616 | tf_op jit(solution)/shard_map/ppermute | solution.py:19
  20.6 41.1 %all_gather.29 = bf16[128,2048]{1,0:T(8,128)(2,1)S(1)} all-gather(bf16[128,256]{1,0:T(8,128)(2,1)} %param.14), channel_id=1, replica_groups=mesh['seq'=64,'head'=8] {'head'}, dimensions={1}, use_global_device_ids=true | all-gather | bytes 589824 | tf_op jit(solution)/shard_map/all_gather | solution.py:67
  61.7 2.3 collective-permute-start.2
  64.7 85.4 %all-gather.2 = bf16[64,32,8]{1,2,0:T(8,128)(2,1)S(1)} all-gather(bf16[1,32,8]{1,2,0:T(8,128)(2,1)} %bitcast.87), channel_id=1, replica_groups=mesh['seq'=64,'head'=8] {'seq'}, dimensions={0}, use_global_device_ids=true | all-gather | bytes 33280 | tf_op jit(solution)/shard_map/all_gather | solution.py:79
  150.3 1.9 collective-permute-start.3
  152.9 6.8 collective-permute-done.3
  159.8 1.9 collective-permute-start.4
  162.4 2.6 collective-permute-done.4
  164.9 1.9 collective-permute-start.5
  166.9 4.7 collective-permute-done.5
  171.6 38.6 %all_gather.30 = bf16[128,2048]{1,0:T(8,128)(2,1)S(1)} all-gather(bf16[128,256]{1,0:T(8,128)(2,1)S(1)} %collective-permute-done.5), channel_id=1, replica_groups=mesh['seq'=64,'head'=8] {'head'}, dimensions={1}, use_global_device_ids=true | all-gather | bytes 589824 | tf_op jit(solution)/shard_map/all_gather | solution.py:68
  214.6 35.1 %all-gather.9.cloned.1.call-done = bf16[2048,512]{1,0:T(8,128)(2,1)} async-done(((bf16[32,512]{1,0:T(8,128)(2,1)}), bf16[2048,512]{1,0:T(8,128)(2,1)}) %all-gather.9.cloned.1.call-update) | async-done | bytes 2097168 | tf_op jit(solution)/shard_map/all_gather | solution.py:76
  249.6 2.3 convolution_convert_fusion.1
  252.0 3.1 collective-permute-start.6
  258.5 77.8 %all-gather = f32[128,1,1,8]{3,2,1,0:T(1,128)S(1)} all-gather(f32[2,1,1,8]{3,2,1,0:T(1,128)S(1)} %get-tuple-element.67), channel_id=2, replica_groups=mesh['seq'=64,'head'=8] {'seq'}, dimensions={0}, use_global_device_ids=true | all-gather | bytes 4160 | tf_op jit(solution)/shard_map/all_gather | solution.py:30
  336.3 31.5 %all-gather.13.cloned.1.call-done = bf16[2048,512]{1,0:T(8,128)(2,1)} async-done(((bf16[32,512]{1,0:T(8,128)(2,1)}), bf16[2048,512]{1,0:T(8,128)(2,1)}) %all-gather.13.cloned.1.call-update) | async-done | bytes 2097168 | tf_op jit(solution)/shard_map/all_gather | solution.py:77
  367.8 2.3 fusion.3
  371.2 190.3 %all-gather.17.cloned.1.call-done = f32[128,8,64,128]{3,2,1,0:T(8,128)} async-done(((f32[2,8,64,128]{3,2,1,0:T(8,128)}), f32[128,8,64,128]{3,2,1,0:T(8,128)}) %all-gather.17.cloned.1.call-update) | async-done | bytes 33554448 | tf_op jit(solution)/shard_map/all_gather | solution.py:30
  564.2 1.9 collective-permute-start.7
  567.5 5.7 collective-permute-start.8
  573.2 3.7 collective-permute-done.8
  576.9 11.0 %collective-permute-start.9 = (bf16[128,512]{0,1:T(8,128)(2,1)S(1)}, bf16[128,512]{0,1:T(8,128)(2,1)S(1)}, u32[]{:S(2)}, u32[]{:S(2)}) collective-permute-start(bf16[128,512]{0,1:T(8,128)(2,1)S(1)} %collective-permute-done.8), channel_id=1, source_target_pairs={{0,32},{32,0},{8,40},{40,8},{16,48},{48,16},{24,56},{56,24},{64,96... | collective-permute-start | bytes 393224 | tf_op jit(solution)/shard_map/ppermute | solution.py:19
  587.9 7.0 collective-permute-done.9
  594.9 13.3 %collective-permute-start.10 = (bf16[128,512]{0,1:T(8,128)(2,1)S(1)}, bf16[128,512]{0,1:T(8,128)(2,1)S(1)}, u32[]{:S(2)}, u32[]{:S(2)}) collective-permute-start(bf16[128,512]{0,1:T(8,128)(2,1)S(1)} %collective-permute-done.9), channel_id=1, source_target_pairs={{0,64},{64,0},{8,72},{72,8},{16,80},{80,16},{24,88},{88,24},{32,96... | collective-permute-start | bytes 393224 | tf_op jit(solution)/shard_map/ppermute | solution.py:19
  608.2 3.2 collective-permute-done.10
  611.4 22.2 %collective-permute-start.11 = (bf16[128,512]{0,1:T(8,128)(2,1)S(1)}, bf16[128,512]{0,1:T(8,128)(2,1)}, u32[]{:S(2)}, u32[]{:S(2)}) collective-permute-start(bf16[128,512]{0,1:T(8,128)(2,1)S(1)} %collective-permute-done.10), channel_id=1, source_target_pairs={{0,128},{128,0},{8,136},{136,8},{16,144},{144,16},{24,152},{152,24... | collective-permute-start | bytes 393224 | tf_op jit(solution)/shard_map/ppermute | solution.py:19
  633.7 2.5 collective-permute-done.11
  636.2 43.5 %collective-permute-start.12 = (bf16[128,512]{0,1:T(8,128)(2,1)}, bf16[128,512]{0,1:T(8,128)(2,1)S(1)}, u32[]{:S(2)}, u32[]{:S(2)}) collective-permute-start(bf16[128,512]{0,1:T(8,128)(2,1)} %collective-permute-done.11), channel_id=1, source_target_pairs={{0,256},{256,0},{8,264},{264,8},{16,272},{272,16},{24,280},{280,24... | collective-permute-start | bytes 393224 | tf_op jit(solution)/shard_map/ppermute | solution.py:19
  679.7 6.9 all-gather.15.cloned.1.call-done
  686.6 2.6 fusion.14
  691.4 7.5 rev.11
  700.0 88.5 %reduce-scatter.2.cloned.1.call-done = f32[128,256]{1,0:T(8,128)} async-done(((f32[128,2048]{1,0:T(8,128)}), f32[128,256]{1,0:T(8,128)}) %reduce-scatter.2.cloned.1.call-update) | async-done | bytes 131088 | tf_op jit(solution)/shard_map/reduce_scatter | solution.py:163
  (71 shorter events, 26.3 us)
Async XLA Ops:
  6.5 205.4 %copy-start.2 = (f32[8]{0:T(128)S(1)}, f32[8]{0:T(128)}, u32[]{:S(2)}) copy-start(f32[8]{0:T(128)} %param.19) | copy-start | bytes 100
  6.5 206.3 %all-gather.11.cloned.1.call-start = ((), (), s32[]{:S(2)}) async-start(), calls=%async_computation.2 | async-start | bytes 1064960 | tf_op jit(solution)/shard_map/all_gather | solution.py:78
  7.3 242.4 %all-gather.9.cloned.1.call-start = ((), (), s32[]{:S(2)}) async-start(), calls=%async_computation.1 | async-start | bytes 2129920 | tf_op jit(solution)/shard_map/all_gather | solution.py:76
  8.0 359.8 %all-gather.13.cloned.1.call-start = ((), (), s32[]{:S(2)}) async-start(), calls=%async_computation.3 | async-start | bytes 2129920 | tf_op jit(solution)/shard_map/all_gather | solution.py:77
  8.7 552.7 %all-gather.17.cloned.1.call-start = ((), (), s32[]{:S(2)}) async-start(), calls=%async_computation.6 | async-start | bytes 34078720 | tf_op jit(solution)/shard_map/all_gather | solution.py:30
  8.8 9.9 %collective-permute-start = (bf16[128,256]{1,0:T(8,128)(2,1)}, bf16[128,256]{1,0:T(8,128)(2,1)S(1)}, u32[]{:S(2)}, u32[]{:S(2)}) collective-permute-start(bf16[128,256]{1,0:T(8,128)(2,1)} %param.14), channel_id=1, source_target_pairs={{0,8},{8,0},{16,24},{24,16},{32,40},{40,32},{48,56},{56,48},{64,72... | collective-permute-start | bytes 196616 | tf_op jit(solution)/shard_map/ppermute | solution.py:19
  18.7 43.0 %collective-permute-start.1 = (bf16[128,256]{1,0:T(8,128)(2,1)S(1)}, bf16[128,256]{1,0:T(8,128)(2,1)S(1)}, u32[]{:S(2)}, u32[]{:S(2)}) collective-permute-start(bf16[128,256]{1,0:T(8,128)(2,1)S(1)} %collective-permute-done), channel_id=1, source_target_pairs={{0,16},{16,0},{8,24},{24,8},{32,48},{48,32},{40,56},{56,40},{64,80... | collective-permute-start | bytes 196616 | tf_op jit(solution)/shard_map/ppermute | solution.py:19
  61.7 88.6 %collective-permute-start.2 = (bf16[128,256]{1,0:T(8,128)(2,1)S(1)}, bf16[128,256]{1,0:T(8,128)(2,1)S(1)}, u32[]{:S(2)}, u32[]{:S(2)}) collective-permute-start(bf16[128,256]{1,0:T(8,128)(2,1)S(1)} %collective-permute-done.1), channel_id=1, source_target_pairs={{0,32},{32,0},{8,40},{40,8},{16,48},{48,16},{24,56},{56,24},{64,96... | collective-permute-start | bytes 196616 | tf_op jit(solution)/shard_map/ppermute | solution.py:19
  150.3 9.5 %collective-permute-start.3 = (bf16[128,256]{1,0:T(8,128)(2,1)S(1)}, bf16[128,256]{1,0:T(8,128)(2,1)S(1)}, u32[]{:S(2)}, u32[]{:S(2)}) collective-permute-start(bf16[128,256]{1,0:T(8,128)(2,1)S(1)} %collective-permute-done.2), channel_id=1, source_target_pairs={{0,64},{64,0},{8,72},{72,8},{16,80},{80,16},{24,88},{88,24},{32,96... | collective-permute-start | bytes 196616 | tf_op jit(solution)/shard_map/ppermute | solution.py:19
  159.8 5.2 collective-permute-start.4
  164.9 6.6 collective-permute-start.5
  252.0 3.9 collective-permute-start.6
  257.8 428.8 %all-gather.15.cloned.1.call-start = ((), (), s32[]{:S(2)}) async-start(), calls=%async_computation.4 | async-start | bytes 2129920 | tf_op jit(solution)/shard_map/all_gather | solution.py:155
  258.4 530.1 %reduce-scatter.2.cloned.1.call-start = ((), (), s32[]{:S(2)}) async-start(), calls=%async_computation.5 | async-start | bytes 1179648 | tf_op jit(solution)/shard_map/reduce_scatter | solution.py:163
  561.5 1.7 copy-start.3
  563.2 0.8 copy-start.1
  564.2 3.2 collective-permute-start.7
  567.5 9.5 %collective-permute-start.8 = (bf16[128,512]{0,1:T(8,128)(2,1)S(1)}, bf16[128,512]{0,1:T(8,128)(2,1)S(1)}, u32[]{:S(2)}, u32[]{:S(2)}) collective-permute-start(bf16[128,512]{0,1:T(8,128)(2,1)S(1)} %collective-permute-done.7), channel_id=1, source_target_pairs={{0,16},{16,0},{8,24},{24,8},{32,48},{48,32},{40,56},{56,40},{64,80... | collective-permute-start | bytes 393224 | tf_op jit(solution)/shard_map/ppermute | solution.py:19
  576.9 18.0 %collective-permute-start.9 = (bf16[128,512]{0,1:T(8,128)(2,1)S(1)}, bf16[128,512]{0,1:T(8,128)(2,1)S(1)}, u32[]{:S(2)}, u32[]{:S(2)}) collective-permute-start(bf16[128,512]{0,1:T(8,128)(2,1)S(1)} %collective-permute-done.8), channel_id=1, source_target_pairs={{0,32},{32,0},{8,40},{40,8},{16,48},{48,16},{24,56},{56,24},{64,96... | collective-permute-start | bytes 393224 | tf_op jit(solution)/shard_map/ppermute | solution.py:19
  594.9 16.5 %collective-permute-start.10 = (bf16[128,512]{0,1:T(8,128)(2,1)S(1)}, bf16[128,512]{0,1:T(8,128)(2,1)S(1)}, u32[]{:S(2)}, u32[]{:S(2)}) collective-permute-start(bf16[128,512]{0,1:T(8,128)(2,1)S(1)} %collective-permute-done.9), channel_id=1, source_target_pairs={{0,64},{64,0},{8,72},{72,8},{16,80},{80,16},{24,88},{88,24},{32,96... | collective-permute-start | bytes 393224 | tf_op jit(solution)/shard_map/ppermute | solution.py:19
  611.4 24.7 %collective-permute-start.11 = (bf16[128,512]{0,1:T(8,128)(2,1)S(1)}, bf16[128,512]{0,1:T(8,128)(2,1)}, u32[]{:S(2)}, u32[]{:S(2)}) collective-permute-start(bf16[128,512]{0,1:T(8,128)(2,1)S(1)} %collective-permute-done.10), channel_id=1, source_target_pairs={{0,128},{128,0},{8,136},{136,8},{16,144},{144,16},{24,152},{152,24... | collective-permute-start | bytes 393224 | tf_op jit(solution)/shard_map/ppermute | solution.py:19
  636.2 53.0 %collective-permute-start.12 = (bf16[128,512]{0,1:T(8,128)(2,1)}, bf16[128,512]{0,1:T(8,128)(2,1)S(1)}, u32[]{:S(2)}, u32[]{:S(2)}) collective-permute-start(bf16[128,512]{0,1:T(8,128)(2,1)} %collective-permute-done.11), channel_id=1, source_target_pairs={{0,256},{256,0},{8,264},{264,8},{16,272},{272,16},{24,280},{280,24... | collective-permute-start | bytes 393224 | tf_op jit(solution)/shard_map/ppermute | solution.py:19
  686.6 3.0 copy-start
Sparse Core Ops, SparseCore 0:
  9.5 121.5 all-gather.10
  133.3 116.3 all-gather.8
  251.8 115.9 all-gather.12
  369.8 191.6 all-gather.16
  563.5 123.0 all-gather.14
  700.1 88.3 reduce-scatter.1
where the time goes:
time: 801 us; the launch traced here: 797 us
  waiting for transfers between devices  389 us (49%)
  blocking collectives  243 us (30%)
  starting transfers between devices  120 us (15%)
  between operations  13.9 us (2%)
  matrix products  13.1 us (2%)
  local copies, waits for them, and re-layouts  12.7 us (2%)
    all_gather x1, waiting for transfers between devices, carried_in(): gathered = jax.tree.map(lambda a: lax.all_gather(a, axis), part)  190 us
    ppermute x12, starting transfers between devices, partner(): return lax.ppermute(block, axis, route)  116 us
    reduce_scatter x1, waiting for transfers between devices, local(): lax.psum_scatter(partial_sum, 'head', scatter_dimension=1, tiled=True)  88.5 us
    all_gather x1, blocking collectives, local(): lax.all_gather(w_step, 'seq', axis=0, tiled=True)  85.4 us
    all_gather x1, blocking collectives, carried_in(): gathered = jax.tree.map(lambda a: lax.all_gather(a, axis), part)  77.8 us
    all_gather x1, blocking collectives, local(): lax.all_gather(layer_input, 'head', axis=1, tiled=True)  41.1 us
    all_gather x1, blocking collectives, local(): lax.all_gather(mirrored, 'head', axis=1, tiled=True)  38.6 us
    all_gather x1, waiting for transfers between devices, local(): lax.all_gather(w_input, 'seq', axis=0, tiled=True)  35.1 us
  transfers between devices with their start and end apart: 19, of which 15 were waited for; matrix products, arithmetic and copies ran while one was open for 2% of the time, Pallas kernels for 0%

commit v1 on v0

v1 whole, which is shorter than its diff:
```python
import jax
import jax.numpy as jnp
from jax import lax
from jax.experimental import pallas as pl
from jax.experimental.pallas import tpu as pltpu
from jax.sharding import Mesh
from jax.sharding import PartitionSpec as P

HEAD_DIM = 64
SPAN = 128
CONV = 4
STATE = 128
HALO = 16
EXT = SPAN + HALO
AXES = ("y_lo", "z_pair", "z_bit", "core", "y_hi", "x")
SEQ = ("y_lo", "z_pair", "z_bit", "core")
Z = ("z_pair", "z_bit")
HEAD = ("y_hi", "x")
F32 = jnp.float32
BF16 = jnp.bfloat16


def iota(shape, axis):
    return lax.broadcasted_iota(jnp.int32, shape, axis)


def ones_where(mask):
    return jnp.where(mask, 1.0, 0.0).astype(BF16)


def mm(a, b):
    return jnp.dot(a, b, preferred_element_type=F32)


def mm_t(a, b):
    return lax.dot_general(a, b, (((1,), (1,)), ((), ())), preferred_element_type=F32)


def t_mm(a, b):
    return lax.dot_general(a, b, (((0,), (0,)), ((), ())), preferred_element_type=F32)


def split(value, parts):
    pieces = []
    for _ in range(parts):
        piece = value.astype(BF16)
        pieces.append(piece)
        value = value - piece.astype(F32)
    return pieces


def silu(value):
    return value * (1.0 / (1.0 + jnp.exp(-value)))


def reversal(size):
    return ones_where(iota((size, size), 0) + iota((size, size), 1) == size - 1)


def spread(value, width):
    table = ones_where(iota((128, width), 0) == iota((128, width), 1) // HEAD_DIM)
    return sum(mm(piece, table) for piece in split(value, 2))


def running_sum(rate):
    lower = ones_where(iota((SPAN, SPAN), 0) >= iota((SPAN, SPAN), 1))
    return sum(mm(lower, piece) for piece in split(rate, 3))


def assemble(place_ref, pieces, full_ref):
    bit, core = place_ref[1], place_ref[2]
    for side in range(2):
        near, left, right = pieces[3 * side : 3 * side + 3]
        column = core + side - 2 * core * side
        for block in range(16):
            far = left.at[block] if block < 8 else right.at[block - 8]
            start = 128 * block + 32 * column
            full_ref[pl.ds(pl.multiple_of(start + 64 * bit, 32), 32)] = near[block]
            full_ref[pl.ds(pl.multiple_of(start + 64 * (1 - bit), 32), 32)] = far[...]


def assemble_ring(place_ref, pieces, full_ref):
    core, y_lo = place_ref[2], place_ref[3]
    for side in range(2):
        column = core + side - 2 * core * side
        for step in range(4):
            y = (y_lo + 4 - step) % 4
            for z in range(8):
                start = 512 * y + 64 * z + 32 * column
                full_ref[pl.ds(pl.multiple_of(start, 32), 32)] = pieces[side][z, step]


def front_kernel(
    place_ref, x_ref, n0, l0, r0, n1, l1, r1, bias_ref, decay_ref, taps_ref,
    send_ref, stream_ref, conv_ref, step_ref, rows_ref, full_ref,
):
    assemble(place_ref, (n0, l0, r0, n1, l1, r1), full_ref)
    flip_rows, flip_columns = reversal(EXT), reversal(256)
    for block in range(8):
        columns = slice(block * 256, (block + 1) * 256)
        stream_ref[:EXT, columns] = x_ref[block, :EXT]
        turned = mm(x_ref[7 - block, HALO:], flip_columns).astype(BF16)
        stream_ref[EXT:, columns] = mm(flip_rows, turned).astype(BF16)
    proj = mm(stream_ref[...], full_ref[...])
    conv_width = conv_ref.shape[2]
    rows_ref[...] = proj[:, :conv_width].astype(BF16).astype(F32)
    for branch in range(2):
        base = branch * EXT + HALO - (CONV - 1)
        running = taps_ref[0:1] * rows_ref[base : base + SPAN]
        for tap in range(1, CONV):
            running = running + taps_ref[tap : tap + 1] * rows_ref[base + tap : base + tap + SPAN]
        convolved = silu(running).astype(BF16)
        conv_ref[branch] = convolved
        raw = proj[branch * EXT + HALO : (branch + 1) * EXT, conv_width:] + bias_ref[...]
        step = jnp.maximum(raw, 0.0) + jnp.log1p(jnp.exp(-jnp.abs(raw)))
        cum = running_sum(step * -jnp.exp(decay_ref[...]))
        step_ref[branch] = step
        end = cum[SPAN - 1 : SPAN]
        x_width = conv_width - STATE
        weighted = (
            convolved[:, :x_width].astype(F32) * spread(jnp.exp(end - cum) * step, x_width)
        ).astype(BF16)
        state = t_mm(weighted, convolved[:, x_width:])
        high, low = (piece.astype(F32) for piece in split(jnp.exp(end), 2))
        row = iota((8, 128), 0)
        tiles = []
        for head in range(x_width // HEAD_DIM):
            tile = jnp.where(row == 0, high[:, head : head + 1], jnp.where(row == 1, low[:, head : head + 1], 0.0))
            tiles += [tile[None]] * 4
        count = x_width // 16
        send_ref[branch * count : (branch + 1) * count] = jnp.concatenate(
            [state.reshape(count, 16, STATE), jnp.concatenate(tiles, 0)], 1
        ).astype(BF16)


def scan_kernel(place_ref, got_ref, entry_ref):
    blocks = got_ref.shape[0]
    backward = jnp.where(place_ref[0] >= blocks // 2, 1, 0)

    def one(lap, state):
        block = lap + backward * (blocks - 1 - 2 * lap)
        entry_ref[block] = state.astype(BF16)
        got = got_ref[block].astype(F32)
        return state * (got[16:17] + got[17:18]) + got[:16]

    lax.fori_loop(0, blocks, one, jnp.zeros((16, STATE), F32), unroll=4)


def back_kernel(
    place_ref, stream_ref, own_ref, other_ref, conv_ref, step_ref, entry_ref, decay_ref, taps_ref, skip_ref, gain_ref,
    out_ref, rows_ref, inner_ref, full_ref,
):
    assemble_ring(place_ref, (own_ref, other_ref), full_ref)
    width = inner_ref.shape[1]
    proj = mm(stream_ref[...], full_ref[:, width:])
    rows_ref[...] = proj[:, width:].astype(BF16).astype(F32)
    causal = iota((SPAN, SPAN), 0) >= iota((SPAN, SPAN), 1)
    normed = []
    for branch in range(2):
        gate = silu(proj[branch * EXT + HALO : (branch + 1) * EXT, :width].astype(BF16).astype(F32))
        base = branch * EXT + HALO - (CONV - 1)
        running = taps_ref[0:1] * rows_ref[base : base + SPAN]
        for tap in range(1, CONV):
            running = running + taps_ref[tap : tap + 1] * rows_ref[base + tap : base + tap + SPAN]
        out_map = silu(running).astype(BF16)
        scores = mm_t(out_map, conv_ref[branch, :, width:])
        step = step_ref[branch]
        cum = running_sum(step * -jnp.exp(decay_ref[...]))
        cum_t, step_t = cum.T, step.T
        for head in range(width // HEAD_DIM):
            channels = slice(head * HEAD_DIM, (head + 1) * HEAD_DIM)
            differ = cum[:, head : head + 1] - cum_t[head : head + 1]
            decay = jnp.where(causal, jnp.exp(jnp.where(causal, differ, 0.0)), 0.0)
            weights = (scores * decay * step_t[head : head + 1]).astype(BF16)
            x_head = conv_ref[branch, :, channels]
            inner_ref[:, channels] = mm(weights, x_head) + skip_ref[:, channels] * x_head.astype(F32)
        entry = entry_ref[branch * width : (branch + 1) * width]
        carried = mm_t(out_map, entry) * spread(jnp.exp(cum), width)
        gated = (inner_ref[...] + carried) * gate
        square = jnp.mean(gated * gated, axis=-1, keepdims=True)
        normed.append((gated * lax.rsqrt(square + 1e-05) * gain_ref[...]).astype(BF16))
    forward, mirror = normed[0], mm(reversal(SPAN), normed[1]).astype(BF16)
    flip = reversal(256)
    for block in range(8):
        near, far = (slice(part * 256, (part + 1) * 256) for part in (block, 7 - block))
        turned = mm(flip, full_ref[far, :width]).astype(BF16)
        out_ref[block] = (mm_t(forward, full_ref[near, :width]) + mm_t(mirror, turned)).astype(BF16)


def kernel_call(body, outs, scratch, in_specs=None):
    extra = {} if in_specs is None else {"in_specs": in_specs}
    return pl.pallas_call(
        body,
        out_shape=outs,
        scratch_shapes=scratch,
        compiler_params=pltpu.CompilerParams(vmem_limit_bytes=20 << 20),
        **extra,
    )


def copies(block, axis):
    count = lax.axis_size(axis)
    return lax.all_to_all(jnp.broadcast_to(block[None], (count, *block.shape)), axis, 0, 0, tiled=True)


def shifted(value, steps):
    count = lax.axis_size(SEQ)
    route = [(source, source + steps) for source in range(count) if 0 <= source + steps < count]
    return lax.ppermute(value, SEQ, route)


def swapped(block):
    return lax.ppermute(block, "core", [(0, 1), (1, 0)])


def neighbours(near):
    count, half = lax.axis_size(Z), near.shape[0] // 2
    left = lax.ppermute(near[:half], Z, [(z, (z + 1) % count) for z in range(count)])
    right = lax.ppermute(near[half:], Z, [(z, (z - 1) % count) for z in range(count)])
    return left, right


def around(block, axis):
    count = lax.axis_size(axis)
    steps = [
        lax.ppermute(block, axis, [(place, (place + step) % count) for place in range(count)])
        for step in range(1, count)
    ]
    return jnp.stack([block, *steps])


def together(*values):
    return lax.optimization_barrier(values)


def local(
    layer_input, w_input, w_gate, w_maps, w_step, step_bias, decay_log, skip_gain, conv_input, conv_maps, norm_gain, w_out,
):
    rows, features = layer_input.shape
    width, heads = w_input.shape[1], w_step.shape[1]
    wide = 128 - heads
    place = jnp.stack([lax.axis_index(SEQ), lax.axis_index("z_bit"), lax.axis_index("core"), lax.axis_index("y_lo")])
    first = jnp.concatenate(
        [w_input, w_maps[:, :STATE], w_step, jnp.zeros((w_step.shape[0], wide), BF16)], 1
    )
    second = jnp.concatenate([w_out.T, w_gate, w_maps[:, STATE:]], 1)
    near = copies(first, ("y_lo", "z_pair"))
    before = shifted(layer_input[rows - HALO :], 1)
    after = shifted(layer_input[:HALO], -1)
    second_y = around(second, "y_lo")
    near, second_y, extended = together(near, second_y, jnp.concatenate([before, layer_input, after]))
    second_z = lax.all_gather(second_y, Z)
    left, right = neighbours(near)
    blocks = copies(extended, HEAD)
    first_pieces = (near, left, right, swapped(near), swapped(left), swapped(right))
    smem = pl.BlockSpec(memory_space=pltpu.SMEM)
    vmem = pl.BlockSpec(memory_space=pltpu.VMEM)
    struct = jax.ShapeDtypeStruct
    places = 2 * width // 16
    send, stream, conv, step = kernel_call(
        front_kernel,
        (
            struct((places, 24, STATE), BF16),
            struct((2 * EXT, 8 * features), BF16),
            struct((2, SPAN, width + STATE), BF16),
            struct((2, SPAN, 128), F32),
        ),
        [pltpu.VMEM((2 * EXT, width + STATE), F32), pltpu.VMEM((8 * features, width + 2 * STATE), BF16)],
        [smem] + [vmem] * 10,
    )(
        place, blocks, *first_pieces,
        jnp.pad(step_bias, (0, wide))[None], jnp.pad(decay_log, (0, wide))[None],
        jnp.concatenate([conv_input, conv_maps[:, :STATE]], 1),
    )
    got = lax.all_to_all(send, SEQ, 0, 0, tiled=True)
    second_own, got = together(second_z, got)
    second_other = swapped(second_own)
    entries = kernel_call(scan_kernel, struct((places, 16, STATE), BF16), [], [smem, vmem])(place, got)
    entry = lax.all_to_all(entries, SEQ, 0, 0, tiled=True).reshape(2 * width, STATE)
    partial = kernel_call(
        back_kernel,
        struct((8, SPAN, features), BF16),
        [
            pltpu.VMEM((2 * EXT, STATE), F32),
            pltpu.VMEM((SPAN, width), F32),
            pltpu.VMEM((8 * features, 2 * width + STATE), BF16),
        ],
        [smem] + [vmem] * 10,
    )(
        place, stream, second_own, second_other, conv, step, entry, jnp.pad(decay_log, (0, wide))[None], conv_maps[:, STATE:],
        jnp.repeat(skip_gain, HEAD_DIM)[None], norm_gain[None],
    )
    parts = lax.all_to_all(partial, HEAD, 0, 0, tiled=True)
    return jnp.sum(parts.astype(F32), 0).astype(BF16)


def solution(mesh):
    fine = Mesh(mesh.devices.reshape(4, 4, 2, 2, 2, 4), AXES)
    placed = (
        P(SEQ, HEAD), P(SEQ, HEAD), P(SEQ, HEAD), P(SEQ, None), P(SEQ, HEAD), P(HEAD), P(HEAD), P(HEAD), P(None, HEAD), P(), P(HEAD), P(HEAD, SEQ),
    )
    return jax.shard_map(local, mesh=fine, in_specs=placed, out_specs=P(SEQ, HEAD), check_vma=False)
```

time: 801 us -> 191 us (0.24)
  the two profiles are of different devices: /device:TPU:1 before, /device:TPU:8 now
where the time goes in v1:
time: 191 us; the launch traced here: 190 us
  starting transfers between devices  59.7 us (31%)
  blocking collectives  53.5 us (28%)
  waiting for transfers between devices  32.2 us (17%)
  local copies, waits for them, and re-layouts  16.8 us (9%)
  between operations  13.7 us (7%)
  Pallas kernels  11.2 us (6%)
  other arithmetic  2.36 us (1%)
    all_to_all x1, blocking collectives, local(): parts = lax.all_to_all(partial, HEAD, 0, 0, tiled=True)  29.4 us
    all_to_all x1, blocking collectives, local(): got = lax.all_to_all(send, SEQ, 0, 0, tiled=True)  24.2 us
    all_to_all x2, starting transfers between devices, copies(): lax.all_to_all(jnp.broadcast_to(block[None], (count, *block.shape)), axis...  20.7 us
    unnamed x39, local copies, waits for them, and re-layouts  11.4 us
    all_to_all x1, waiting for transfers between devices, local(): lax.all_to_all(entries, SEQ, 0, 0, tiled=True).reshape(2 * width, STATE)  11.2 us
    ppermute x1, waiting for transfers between devices, neighbours(): lax.ppermute(near[:half], Z, [(z, (z + 1) % count) for z in range(count)])  10.7 us
    ppermute x3, starting transfers between devices, around(): lax.ppermute(block, axis, [(place, (place + step) % count) for place in r...  10.2 us
    ppermute x4, starting transfers between devices, swapped(): return lax.ppermute(block, 'core', [(0, 1), (1, 0)])  7.98 us
  transfers between devices with their start and end apart: 15, of which 7 were waited for; matrix products, arithmetic and copies ran while one was open for 2% of the time, Pallas kernels for 3%

profile of v1, /device:TPU:8, one launch (start us, length us, event | category | flops | bytes accessed | tf_op | source)
XLA Modules:
  0.0 189.5 jit_solution(14902817972839404515)
XLA Ops:
  8.9 1.0 broadcast_in_dim.29
  9.9 13.8 %all-to-all-start = ((bf16[16,32,768]{2,1,0:T(8,128)(2,1)}), bf16[16,32,768]{2,1,0:T(8,128)(2,1)S(1)}, u32[]{:S(2)}, u32[]{:S(2)}) async-start(bf16[16,32,768]{2,1,0:T(8,128)(2,1)} %broadcast_in_dim.29), calls=%async_computation | async-start | bytes 1572864 | tf_op jit(solution)/shard_map/all_to_all | solution.py:203
  23.8 1.9 %collective-permute-start.3 = (bf16[16,256]{1,0:T(8,128)(2,1)S(1)}, bf16[16,256]{1,0:T(8,128)(2,1)S(1)}, u32[]{:S(2)}, u32[]{:S(2)}) collective-permute-start(bf16[16,256]{1,0:T(8,128)(2,1)S(1)} %get-tuple-element.27), channel_id=1, source_target_pairs={{0,8},{8,16},{16,24},{24,32},{32,40},{40,48},{48,56},{56,64},{64,7... | collective-permute-start | bytes 24584 | tf_op jit(solution)/shard_map/ppermute | solution.py:209
  25.7 5.8 %collective-permute-start.4 = (bf16[16,256]{1,0:T(8,128)(2,1)S(1)}, bf16[16,256]{1,0:T(8,128)(2,1)S(1)}, u32[]{:S(2)}, u32[]{:S(2)}) collective-permute-start(bf16[16,256]{1,0:T(8,128)(2,1)S(1)} %get-tuple-element.28), channel_id=1, source_target_pairs={{8,0},{16,8},{24,16},{32,24},{40,32},{48,40},{56,48},{64,56},{72,6... | collective-permute-start | bytes 24584 | tf_op jit(solution)/shard_map/ppermute | solution.py:209
  31.5 3.5 %collective-permute-start = (bf16[32,1152]{1,0:T(8,128)(2,1)S(1)}, bf16[32,1152]{1,0:T(8,128)(2,1)S(1)}, u32[]{:S(2)}, u32[]{:S(2)}) collective-permute-start(bf16[32,1152]{1,0:T(8,128)(2,1)S(1)} %get-tuple-element.26), channel_id=1, source_target_pairs={{0,128},{128,256},{256,384},{384,0},{1,129},{129,257},{257,385},{3... | collective-permute-start | bytes 221192 | tf_op jit(solution)/shard_map/ppermute | solution.py:226
  35.1 2.8 %collective-permute-start.1 = (bf16[32,1152]{1,0:T(8,128)(2,1)S(1)}, bf16[32,1152]{1,0:T(8,128)(2,1)S(1)}, u32[]{:S(2)}, u32[]{:S(2)}) collective-permute-start(bf16[32,1152]{1,0:T(8,128)(2,1)S(1)} %get-tuple-element.26), channel_id=1, source_target_pairs={{0,256},{128,384},{256,0},{384,128},{1,257},{129,385},{257,1},{385... | collective-permute-start | bytes 221192 | tf_op jit(solution)/shard_map/ppermute | solution.py:226
  37.9 3.9 %collective-permute-start.2 = (bf16[32,1152]{1,0:T(8,128)(2,1)S(1)}, bf16[32,1152]{1,0:T(8,128)(2,1)S(1)}, u32[]{:S(2)}, u32[]{:S(2)}) collective-permute-start(bf16[32,1152]{1,0:T(8,128)(2,1)S(1)} %get-tuple-element.26), channel_id=1, source_target_pairs={{0,384},{128,0},{256,128},{384,256},{1,385},{129,1},{257,129},{385... | collective-permute-start | bytes 221192 | tf_op jit(solution)/shard_map/ppermute | solution.py:226
  41.9 4.1 %collective-permute-done = bf16[32,1152]{1,0:T(8,128)(2,1)S(1)} collective-permute-done((bf16[32,1152]{1,0:T(8,128)(2,1)S(1)}, bf16[32,1152]{1,0:T(8,128)(2,1)S(1)}, u32[]{:S(2)}, u32[]{:S(2)}) %collective-permute-start) | collective-permute-done | bytes 73760 | tf_op jit(solution)/shard_map/ppermute | solution.py:226
  46.7 2.1 %collective-permute-done.2 = bf16[32,1152]{1,0:T(8,128)(2,1)S(1)} collective-permute-done((bf16[32,1152]{1,0:T(8,128)(2,1)S(1)}, bf16[32,1152]{1,0:T(8,128)(2,1)S(1)}, u32[]{:S(2)}, u32[]{:S(2)}) %collective-permute-start.2) | collective-permute-done | bytes 73760 | tf_op jit(solution)/shard_map/ppermute | solution.py:226
  49.6 0.9 broadcast_in_dim.30
  50.5 6.9 %all-to-all-start.1 = ((bf16[8,160,256]{2,1,0:T(8,128)(2,1)}), bf16[8,160,256]{2,1,0:T(8,128)(2,1)S(1)}, u32[]{:S(2)}, u32[]{:S(2)}) async-start(bf16[8,160,256]{2,1,0:T(8,128)(2,1)} %broadcast_in_dim.30), calls=%async_computation.1 | async-start | bytes 1310720 | tf_op jit(solution)/shard_map/all_to_all | solution.py:203
  58.2 3.3 %collective-permute-start.5 = (bf16[8,32,768]{2,1,0:T(8,128)(2,1)S(1)}, bf16[8,32,768]{2,1,0:T(8,128)(2,1)S(1)}, u32[]{:S(2)}, u32[]{:S(2)}) collective-permute-start(bf16[8,32,768]{2,1,0:T(8,128)(2,1)S(1)} %get-tuple-element.24), channel_id=1, source_target_pairs={{0,16},{16,32},{32,48},{48,64},{64,80},{80,96},{96,112},{112,0},{1... | collective-permute-start | bytes 1179656 | tf_op jit(solution)/shard_map/ppermute | solution.py:218
  61.5 4.0 %collective-permute-start.6 = (bf16[8,32,768]{2,1,0:T(8,128)(2,1)}, bf16[8,32,768]{2,1,0:T(8,128)(2,1)S(1)}, u32[]{:S(2)}, u32[]{:S(2)}) collective-permute-start(bf16[8,32,768]{2,1,0:T(8,128)(2,1)} %get-tuple-element.23), channel_id=1, source_target_pairs={{0,112},{16,0},{32,16},{48,32},{64,48},{80,64},{96,80},{112,96},{1... | collective-permute-start | bytes 1179656 | tf_op jit(solution)/shard_map/ppermute | solution.py:219
  65.5 1.9 %collective-permute-start.7 = (bf16[16,32,768]{2,1,0:T(8,128)(2,1)S(1)}, bf16[16,32,768]{2,1,0:T(8,128)(2,1)S(1)}, u32[]{:S(2)}, u32[]{:S(2)}) collective-permute-start(bf16[16,32,768]{2,1,0:T(8,128)(2,1)S(1)} %all-to-all-done.n0), channel_id=1, source_target_pairs={{0,8},{8,0},{1,9},{9,1},{2,10},{10,2},{3,11},{11,3},{4,12},{12,4},... | collective-permute-start | bytes 2359304 | tf_op jit(solution)/shard_map/ppermute | solution.py:213
  68.0 10.7 %collective-permute-done.5.l0 = bf16[8,32,768]{2,1,0:T(8,128)(2,1)S(1)} collective-permute-done((bf16[8,32,768]{2,1,0:T(8,128)(2,1)S(1)}, bf16[8,32,768]{2,1,0:T(8,128)(2,1)S(1)}, u32[]{:S(2)}, u32[]{:S(2)}) %collective-permute-start.5) | collective-permute-done | bytes 393248 | tf_op jit(solution)/shard_map/ppermute | solution.py:218
  78.7 1.9 %collective-permute-start.8 = (bf16[8,32,768]{2,1,0:T(8,128)(2,1)S(1)}, bf16[8,32,768]{2,1,0:T(8,128)(2,1)S(1)}, u32[]{:S(2)}, u32[]{:S(2)}) collective-permute-start(bf16[8,32,768]{2,1,0:T(8,128)(2,1)S(1)} %collective-permute-done.5.l0), channel_id=1, source_target_pairs={{0,8},{8,0},{1,9},{9,1},{2,10},{10,2},{3,11},{11,3},{4,12},{12,4},... | collective-permute-start | bytes 1179656 | tf_op jit(solution)/shard_map/ppermute | solution.py:213
  80.6 2.4 %collective-permute-done.6.r0 = bf16[8,32,768]{2,1,0:T(8,128)(2,1)S(1)} collective-permute-done((bf16[8,32,768]{2,1,0:T(8,128)(2,1)}, bf16[8,32,768]{2,1,0:T(8,128)(2,1)S(1)}, u32[]{:S(2)}, u32[]{:S(2)}) %collective-permute-start.6) | collective-permute-done | bytes 393248 | tf_op jit(solution)/shard_map/ppermute | solution.py:219
  83.0 1.9 %collective-permute-start.9 = (bf16[8,32,768]{2,1,0:T(8,128)(2,1)S(1)}, bf16[8,32,768]{2,1,0:T(8,128)(2,1)S(1)}, u32[]{:S(2)}, u32[]{:S(2)}) collective-permute-start(bf16[8,32,768]{2,1,0:T(8,128)(2,1)S(1)} %collective-permute-done.6.r0), channel_id=1, source_target_pairs={{0,8},{8,0},{1,9},{9,1},{2,10},{10,2},{3,11},{11,3},{4,12},{12,4},... | collective-permute-start | bytes 1179656 | tf_op jit(solution)/shard_map/ppermute | solution.py:213
  85.6 1.0 collective-permute-done.9.r1
  87.4 1.0 copy-done.4
  89.6 3.7 %shard_map.118 = (bf16[64,24,128]{2,1,0:T(8,128)(2,1)S(1)}, bf16[288,2048]{1,0:T(8,128)(2,1)S(1)}, bf16[2,128,640]{2,1,0:T(8,128)(2,1)S(1)}, f32[2,128,128]{2,1,0:T(8,128)S(1)}) custom-call(s32[4]{0:T(128)S(1)} %pad_add_fusion.place_ref, bf16[8,160,256]{2,1,0:T(8,128)(2,1)S(1)} %all-to-all-done.1.x_ref, bf16[16,32,768]{2,1,0:T(8,128)(2,1)S(1)} %all-to-all-done.n0, ...), custom_call_target="tpu_custom_call" | custom-call | tf_op jit(solution)/shard_map/pallas_call | solution.py:260
  93.3 1.0 copy-done.1
  95.0 24.2 %all_to_all.25.got_ref = bf16[64,24,128]{2,1,0:T(8,128)(2,1)S(1)} all-to-all(bf16[64,24,128]{2,1,0:T(8,128)(2,1)S(1)} %get-tuple-element.18), channel_id=1, replica_groups=mesh['y_lo'=4,'z_pair'=4,'z_bit'=2,'core'=2,'y_hi'=2,'x'=4] {'y_lo','z_p..., dimensions={0} | all-to-all | bytes 786432 | tf_op jit(solution)/shard_map/all_to_all | solution.py:275
  119.2 2.2 %collective-permute-start.10 = (bf16[8,4,32,1152]{3,2,1,0:T(8,128)(2,1)}, bf16[8,4,32,1152]{3,2,1,0:T(8,128)(2,1)S(1)}, u32[]{:S(2)}, u32[]{:S(2)}) collective-permute-start(bf16[8,4,32,1152]{3,2,1,0:T(8,128)(2,1)} %bitcast.17), channel_id=1, source_target_pairs={{0,8},{8,0},{1,9},{9,1},{2,10},{10,2},{3,11},{11,3},{4,12},{12,4},... | collective-permute-start | bytes 7077896 | tf_op jit(solution)/shard_map/ppermute | solution.py:213
  121.4 1.5 shard_map.119
  123.0 5.8 %all-to-all-start.3 = ((bf16[64,16,128]{2,1,0:T(8,128)(2,1)}), bf16[64,16,128]{2,1,0:T(8,128)(2,1)S(1)}, u32[]{:S(2)}, u32[]{:S(2)}) async-start(bf16[64,16,128]{2,1,0:T(8,128)(2,1)} %shard_map.119), calls=%async_computation.3 | async-start | bytes 524288 | tf_op jit(solution)/shard_map/all_to_all | solution.py:279
  129.5 11.2 %all-to-all-done.3 = bf16[64,16,128]{2,1,0:T(8,128)(2,1)S(1)} async-done(((bf16[64,16,128]{2,1,0:T(8,128)(2,1)}), bf16[64,16,128]{2,1,0:T(8,128)(2,1)S(1)}, u32[]{:S(2)}, u32[]{:S(2)}) %all-to-all-start.3) | async-done | bytes 262176 | tf_op jit(solution)/shard_map/all_to_all | solution.py:279
  140.7 1.7 copy-done
  142.4 1.3 copy-done.2
  143.6 1.0 copy-done.6
  146.6 6.1 %shard_map.120 = bf16[8,128,256]{2,1,0:T(8,128)(2,1)S(1)} custom-call(s32[4]{0:T(128)S(1)} %pad_add_fusion.place_ref, bf16[288,2048]{1,0:T(8,128)(2,1)S(1)} %copy-done.2, bf16[8,4,32,1152]{3,2,1,0:T(8,128)(2,1)S(1)} %bitcast.18, bf16[8,4,32,1152]{3,2,1,0:T(8,128)(2,1)S(1)} %collective-permute-done.10.other_ref, bf16[2,128,640]{2,1,0:T(8,128)(2,1)S(1)} %copy-done.6, ...), custom_call_target="tpu_custom_call" | custom-call | tf_op jit(solution)/shard_map/pallas_call | solution.py:280
  152.6 29.4 %all_to_all.26 = bf16[8,128,256]{2,1,0:T(8,128)(2,1)S(1)} all-to-all(bf16[8,128,256]{2,1,0:T(8,128)(2,1)S(1)} %shard_map.120), channel_id=1, replica_groups=mesh['y_lo'=4,'z_pair'=4,'z_bit'=2,'core'=2,'y_hi'=2,'x'=4] {'y_hi','x'}, dimensions={0} | all-to-all | bytes 1048576 | tf_op jit(solution)/shard_map/all_to_all | solution.py:293
  (61 shorter events, 12.3 us)
Async XLA Ops:
  6.5 17.2 %copy-start.12 = (bf16[128,256]{1,0:T(8,128)(2,1)S(1)}, bf16[128,256]{1,0:T(8,128)(2,1)}, u32[]{:S(2)}) copy-start(bf16[128,256]{1,0:T(8,128)(2,1)} %param.12) | copy-start | bytes 196612
  6.5 24.9 %copy-start.14 = (bf16[512,32]{0,1:T(8,128)(2,1)S(1)}, bf16[512,32]{0,1:T(8,128)(2,1)}, u32[]{:S(2)}) copy-start(bf16[512,32]{0,1:T(8,128)(2,1)} %param.23) | copy-start | bytes 98308
  6.5 24.9 %copy-start.13 = (bf16[32,512]{1,0:T(8,128)(2,1)S(1)}, bf16[32,512]{1,0:T(8,128)(2,1)}, u32[]{:S(2)}) copy-start(bf16[32,512]{1,0:T(8,128)(2,1)} %param.14) | copy-start | bytes 98308
  9.9 39.7 %all-to-all-start = ((bf16[16,32,768]{2,1,0:T(8,128)(2,1)}), bf16[16,32,768]{2,1,0:T(8,128)(2,1)S(1)}, u32[]{:S(2)}, u32[]{:S(2)}) async-start(bf16[16,32,768]{2,1,0:T(8,128)(2,1)} %broadcast_in_dim.29), calls=%async_computation | async-start | bytes 1572864 | tf_op jit(solution)/shard_map/all_to_all | solution.py:203
  23.7 95.5 %all-gather.3.cloned.1.call-start = ((), (), s32[]{:S(2)}) async-start(), calls=%async_computation.5 | async-start | bytes 2654208 | tf_op jit(solution)/shard_map/all_gather | solution.py:252
  23.8 18.1 %collective-permute-start.3 = (bf16[16,256]{1,0:T(8,128)(2,1)S(1)}, bf16[16,256]{1,0:T(8,128)(2,1)S(1)}, u32[]{:S(2)}, u32[]{:S(2)}) collective-permute-start(bf16[16,256]{1,0:T(8,128)(2,1)S(1)} %get-tuple-element.27), channel_id=1, source_target_pairs={{0,8},{8,16},{16,24},{24,32},{32,40},{40,48},{48,56},{56,64},{64,7... | collective-permute-start | bytes 24584 | tf_op jit(solution)/shard_map/ppermute | solution.py:209
  25.7 16.1 %collective-permute-start.4 = (bf16[16,256]{1,0:T(8,128)(2,1)S(1)}, bf16[16,256]{1,0:T(8,128)(2,1)S(1)}, u32[]{:S(2)}, u32[]{:S(2)}) collective-permute-start(bf16[16,256]{1,0:T(8,128)(2,1)S(1)} %get-tuple-element.28), channel_id=1, source_target_pairs={{8,0},{16,8},{24,16},{32,24},{40,32},{48,40},{56,48},{64,56},{72,6... | collective-permute-start | bytes 24584 | tf_op jit(solution)/shard_map/ppermute | solution.py:209
  31.5 35.9 %copy-start.17 = (f32[8]{0:T(128)S(1)}, f32[8]{0:T(128)}, u32[]{:S(2)}) copy-start(f32[8]{0:T(128)} %param.18) | copy-start | bytes 100
  31.5 35.9 %copy-start.18 = (f32[8]{0:T(128)S(1)}, f32[8]{0:T(128)}, u32[]{:S(2)}) copy-start(f32[8]{0:T(128)} %param.17) | copy-start | bytes 100
  31.5 53.5 %copy-start.16 = (f32[4,256]{1,0:T(4,128)S(1)}, f32[4,256]{1,0:T(4,128)}, u32[]{:S(2)}) copy-start(f32[4,256]{1,0:T(4,128)} %param.21) | copy-start | bytes 12292
  31.5 54.1 %copy-start.15 = (f32[4,512]{1,0:T(4,128)S(1)}, f32[4,512]{1,0:T(4,128)}, u32[]{:S(2)}) copy-start(f32[4,512]{1,0:T(4,128)} %param.20) | copy-start | bytes 24580
  31.5 14.4 %collective-permute-start = (bf16[32,1152]{1,0:T(8,128)(2,1)S(1)}, bf16[32,1152]{1,0:T(8,128)(2,1)S(1)}, u32[]{:S(2)}, u32[]{:S(2)}) collective-permute-start(bf16[32,1152]{1,0:T(8,128)(2,1)S(1)} %get-tuple-element.26), channel_id=1, source_target_pairs={{0,128},{128,256},{256,384},{384,0},{1,129},{129,257},{257,385},{3... | collective-permute-start | bytes 221192 | tf_op jit(solution)/shard_map/ppermute | solution.py:226
  35.1 11.7 %collective-permute-start.1 = (bf16[32,1152]{1,0:T(8,128)(2,1)S(1)}, bf16[32,1152]{1,0:T(8,128)(2,1)S(1)}, u32[]{:S(2)}, u32[]{:S(2)}) collective-permute-start(bf16[32,1152]{1,0:T(8,128)(2,1)S(1)} %get-tuple-element.26), channel_id=1, source_target_pairs={{0,256},{128,384},{256,0},{384,128},{1,257},{129,385},{257,1},{385... | collective-permute-start | bytes 221192 | tf_op jit(solution)/shard_map/ppermute | solution.py:226
  37.9 10.9 %collective-permute-start.2 = (bf16[32,1152]{1,0:T(8,128)(2,1)S(1)}, bf16[32,1152]{1,0:T(8,128)(2,1)S(1)}, u32[]{:S(2)}, u32[]{:S(2)}) collective-permute-start(bf16[32,1152]{1,0:T(8,128)(2,1)S(1)} %get-tuple-element.26), channel_id=1, source_target_pairs={{0,384},{128,0},{256,128},{384,256},{1,385},{129,1},{257,129},{385... | collective-permute-start | bytes 221192 | tf_op jit(solution)/shard_map/ppermute | solution.py:226
  50.5 36.9 %all-to-all-start.1 = ((bf16[8,160,256]{2,1,0:T(8,128)(2,1)}), bf16[8,160,256]{2,1,0:T(8,128)(2,1)S(1)}, u32[]{:S(2)}, u32[]{:S(2)}) async-start(bf16[8,160,256]{2,1,0:T(8,128)(2,1)} %broadcast_in_dim.30), calls=%async_computation.1 | async-start | bytes 1310720 | tf_op jit(solution)/shard_map/all_to_all | solution.py:203
  58.2 20.5 %collective-permute-start.5 = (bf16[8,32,768]{2,1,0:T(8,128)(2,1)S(1)}, bf16[8,32,768]{2,1,0:T(8,128)(2,1)S(1)}, u32[]{:S(2)}, u32[]{:S(2)}) collective-permute-start(bf16[8,32,768]{2,1,0:T(8,128)(2,1)S(1)} %get-tuple-element.24), channel_id=1, source_target_pairs={{0,16},{16,32},{32,48},{48,64},{64,80},{80,96},{96,112},{112,0},{1... | collective-permute-start | bytes 1179656 | tf_op jit(solution)/shard_map/ppermute | solution.py:218
  61.5 21.6 %collective-permute-start.6 = (bf16[8,32,768]{2,1,0:T(8,128)(2,1)}, bf16[8,32,768]{2,1,0:T(8,128)(2,1)S(1)}, u32[]{:S(2)}, u32[]{:S(2)}) collective-permute-start(bf16[8,32,768]{2,1,0:T(8,128)(2,1)} %get-tuple-element.23), channel_id=1, source_target_pairs={{0,112},{16,0},{32,16},{48,32},{64,48},{80,64},{96,80},{112,96},{1... | collective-permute-start | bytes 1179656 | tf_op jit(solution)/shard_map/ppermute | solution.py:219
  65.5 21.9 %collective-permute-start.7 = (bf16[16,32,768]{2,1,0:T(8,128)(2,1)S(1)}, bf16[16,32,768]{2,1,0:T(8,128)(2,1)S(1)}, u32[]{:S(2)}, u32[]{:S(2)}) collective-permute-start(bf16[16,32,768]{2,1,0:T(8,128)(2,1)S(1)} %all-to-all-done.n0), channel_id=1, source_target_pairs={{0,8},{8,0},{1,9},{9,1},{2,10},{10,2},{3,11},{11,3},{4,12},{12,4},... | collective-permute-start | bytes 2359304 | tf_op jit(solution)/shard_map/ppermute | solution.py:213
  78.7 6.9 %collective-permute-start.8 = (bf16[8,32,768]{2,1,0:T(8,128)(2,1)S(1)}, bf16[8,32,768]{2,1,0:T(8,128)(2,1)S(1)}, u32[]{:S(2)}, u32[]{:S(2)}) collective-permute-start(bf16[8,32,768]{2,1,0:T(8,128)(2,1)S(1)} %collective-permute-done.5.l0), channel_id=1, source_target_pairs={{0,8},{8,0},{1,9},{9,1},{2,10},{10,2},{3,11},{11,3},{4,12},{12,4},... | collective-permute-start | bytes 1179656 | tf_op jit(solution)/shard_map/ppermute | solution.py:213
  83.0 3.6 %collective-permute-start.9 = (bf16[8,32,768]{2,1,0:T(8,128)(2,1)S(1)}, bf16[8,32,768]{2,1,0:T(8,128)(2,1)S(1)}, u32[]{:S(2)}, u32[]{:S(2)}) collective-permute-start(bf16[8,32,768]{2,1,0:T(8,128)(2,1)S(1)} %collective-permute-done.6.r0), channel_id=1, source_target_pairs={{0,8},{8,0},{1,9},{9,1},{2,10},{10,2},{3,11},{11,3},{4,12},{12,4},... | collective-permute-start | bytes 1179656 | tf_op jit(solution)/shard_map/ppermute | solution.py:213
  86.6 0.8 copy-start.3
  87.4 1.0 copy-start.4
  89.0 0.7 copy-start.10
  93.3 1.0 copy-start.1
  94.3 0.7 copy-start.5
  119.2 21.5 %collective-permute-start.10 = (bf16[8,4,32,1152]{3,2,1,0:T(8,128)(2,1)}, bf16[8,4,32,1152]{3,2,1,0:T(8,128)(2,1)S(1)}, u32[]{:S(2)}, u32[]{:S(2)}) collective-permute-start(bf16[8,4,32,1152]{3,2,1,0:T(8,128)(2,1)} %bitcast.17), channel_id=1, source_target_pairs={{0,8},{8,0},{1,9},{9,1},{2,10},{10,2},{3,11},{11,3},{4,12},{12,4},... | collective-permute-start | bytes 7077896 | tf_op jit(solution)/shard_map/ppermute | solution.py:213
  123.0 17.7 %all-to-all-start.3 = ((bf16[64,16,128]{2,1,0:T(8,128)(2,1)}), bf16[64,16,128]{2,1,0:T(8,128)(2,1)S(1)}, u32[]{:S(2)}, u32[]{:S(2)}) async-start(bf16[64,16,128]{2,1,0:T(8,128)(2,1)} %shard_map.119), calls=%async_computation.3 | async-start | bytes 524288 | tf_op jit(solution)/shard_map/all_to_all | solution.py:279
  140.7 1.7 copy-start
  142.4 1.3 copy-start.2
  143.6 1.0 copy-start.6
  144.6 0.7 copy-start.7
  145.9 0.7 copy-start.11
  (2 other events, 1.2 us)
Sparse Core Ops, SparseCore 0:
  49.7 49.7 all-gather.2

commit v2 on v1

--- a/solution.py
+++ b/solution.py
@@ -91,29 +91,32 @@
 
 
 def front_kernel(
-    place_ref, x_ref, n0, l0, r0, n1, l1, r1, bias_ref, decay_ref, taps_ref,
+    place_ref, x_ref, n0, l0, r0, n1, l1, r1, small_ref,
     send_ref, stream_ref, conv_ref, step_ref, rows_ref, full_ref,
 ):
     assemble(place_ref, (n0, l0, r0, n1, l1, r1), full_ref)
+    y_hi, x = place_ref[4], place_ref[5]
     flip_rows, flip_columns = reversal(EXT), reversal(256)
-    for block in range(8):
-        columns = slice(block * 256, (block + 1) * 256)
-        stream_ref[:EXT, columns] = x_ref[block, :EXT]
-        turned = mm(x_ref[7 - block, HALO:], flip_columns).astype(BF16)
-        stream_ref[EXT:, columns] = mm(flip_rows, turned).astype(BF16)
+    for step in range(4):
+        for side in range(2):
+            block = 4 * (y_hi + side - 2 * y_hi * side) + (x + 4 - step) % 4
+            stream_ref[:EXT, pl.ds(pl.multiple_of(block * 256, 256), 256)] = x_ref[step, side, :EXT]
+            turned = mm(x_ref[step, side, HALO:], flip_columns).astype(BF16)
+            stream_ref[EXT:, pl.ds(pl.multiple_of((7 - block) * 256, 256), 256)] = mm(flip_rows, turned).astype(BF16)
     proj = mm(stream_ref[...], full_ref[...])
     conv_width = conv_ref.shape[2]
+    taps, bias, decay = small_ref[:CONV], small_ref[4:5, :128], small_ref[5:6, :128]
     rows_ref[...] = proj[:, :conv_width].astype(BF16).astype(F32)
     for branch in range(2):
         base = branch * EXT + HALO - (CONV - 1)
-        running = taps_ref[0:1] * rows_ref[base : base + SPAN]
+        running = taps[0:1] * rows_ref[base : base + SPAN]
         for tap in range(1, CONV):
-            running = running + taps_ref[tap : tap + 1] * rows_ref[base + tap : base + tap + SPAN]
+            running = running + taps[tap : tap + 1] * rows_ref[base + tap : base + tap + SPAN]
         convolved = silu(running).astype(BF16)
         conv_ref[branch] = convolved
-        raw = proj[branch * EXT + HALO : (branch + 1) * EXT, conv_width:] + bias_ref[...]
+        raw = proj[branch * EXT + HALO : (branch + 1) * EXT, conv_width:] + bias
         step = jnp.maximum(raw, 0.0) + jnp.log1p(jnp.exp(-jnp.abs(raw)))
-        cum = running_sum(step * -jnp.exp(decay_ref[...]))
+        cum = running_sum(step * -jnp.exp(decay))
         step_ref[branch] = step
         end = cum[SPAN - 1 : SPAN]
         x_width = conv_width - STATE
@@ -147,25 +150,26 @@
 
 
 def back_kernel(
-    place_ref, stream_ref, own_ref, other_ref, conv_ref, step_ref, entry_ref, decay_ref, taps_ref, skip_ref, gain_ref,
+    place_ref, stream_ref, own_ref, other_ref, conv_ref, step_ref, entry_ref, small_ref,
     out_ref, rows_ref, inner_ref, full_ref,
 ):
     assemble_ring(place_ref, (own_ref, other_ref), full_ref)
     width = inner_ref.shape[1]
     proj = mm(stream_ref[...], full_ref[:, width:])
+    taps, log_rate = small_ref[:CONV, :STATE], small_ref[6:7, :128]
     rows_ref[...] = proj[:, width:].astype(BF16).astype(F32)
     causal = iota((SPAN, SPAN), 0) >= iota((SPAN, SPAN), 1)
     normed = []
     for branch in range(2):
         gate = silu(proj[branch * EXT + HALO : (branch + 1) * EXT, :width].astype(BF16).astype(F32))
         base = branch * EXT + HALO - (CONV - 1)
-        running = taps_ref[0:1] * rows_ref[base : base + SPAN]
+        running = taps[0:1] * rows_ref[base : base + SPAN]
         for tap in range(1, CONV):
-            running = running + taps_ref[tap : tap + 1] * rows_ref[base + tap : base + tap + SPAN]
+            running = running + taps[tap : tap + 1] * rows_ref[base + tap : base + tap + SPAN]
         out_map = silu(running).astype(BF16)
         scores = mm_t(out_map, conv_ref[branch, :, width:])
         step = step_ref[branch]
-        cum = running_sum(step * -jnp.exp(decay_ref[...]))
+        cum = running_sum(step * -jnp.exp(log_rate))
         cum_t, step_t = cum.T, step.T
         for head in range(width // HEAD_DIM):
             channels = slice(head * HEAD_DIM, (head + 1) * HEAD_DIM)
@@ -173,18 +177,18 @@
             decay = jnp.where(causal, jnp.exp(jnp.where(causal, differ, 0.0)), 0.0)
             weights = (scores * decay * step_t[head : head + 1]).astype(BF16)
             x_head = conv_ref[branch, :, channels]
-            inner_ref[:, channels] = mm(weights, x_head) + skip_ref[:, channels] * x_head.astype(F32)
+            inner_ref[:, channels] = mm(weights, x_head) + small_ref[4:5, channels] * x_head.astype(F32)
         entry = entry_ref[branch * width : (branch + 1) * width]
         carried = mm_t(out_map, entry) * spread(jnp.exp(cum), width)
         gated = (inner_ref[...] + carried) * gate
         square = jnp.mean(gated * gated, axis=-1, keepdims=True)
-        normed.append((gated * lax.rsqrt(square + 1e-05) * gain_ref[...]).astype(BF16))
+        normed.append((gated * lax.rsqrt(square + 1e-05) * small_ref[5:6]).astype(BF16))
     forward, mirror = normed[0], mm(reversal(SPAN), normed[1]).astype(BF16)
     flip = reversal(256)
     for block in range(8):
         near, far = (slice(part * 256, (part + 1) * 256) for part in (block, 7 - block))
         turned = mm(flip, full_ref[far, :width]).astype(BF16)
-        out_ref[block] = (mm_t(forward, full_ref[near, :width]) + mm_t(mirror, turned)).astype(BF16)
+        out_ref[block % 4, block // 4] = (mm_t(forward, full_ref[near, :width]) + mm_t(mirror, turned)).astype(BF16)
 
 
 def kernel_call(body, outs, scratch, in_specs=None):
@@ -193,7 +197,7 @@
         body,
         out_shape=outs,
         scratch_shapes=scratch,
-        compiler_params=pltpu.CompilerParams(vmem_limit_bytes=20 << 20),
+        compiler_params=pltpu.CompilerParams(vmem_limit_bytes=18 << 20),
         **extra,
     )
 
@@ -239,7 +243,7 @@
     rows, features = layer_input.shape
     width, heads = w_input.shape[1], w_step.shape[1]
     wide = 128 - heads
-    place = jnp.stack([lax.axis_index(SEQ), lax.axis_index("z_bit"), lax.axis_index("core"), lax.axis_index("y_lo")])
+    place = jnp.stack([lax.axis_index(SEQ), lax.axis_index("z_bit"), lax.axis_index("core")] + [lax.axis_index(axis) for axis in ("y_lo", "y_hi", "x")])
     first = jnp.concatenate(
         [w_input, w_maps[:, :STATE], w_step, jnp.zeros((w_step.shape[0], wide), BF16)], 1
     )
@@ -247,16 +251,30 @@
     near = copies(first, ("y_lo", "z_pair"))
     before = shifted(layer_input[rows - HALO :], 1)
     after = shifted(layer_input[:HALO], -1)
+    extended = jnp.concatenate([before, layer_input, after])
+    extended = jnp.stack([extended, lax.ppermute(extended, "y_hi", [(0, 1), (1, 0)])])
     second_y = around(second, "y_lo")
-    near, second_y, extended = together(near, second_y, jnp.concatenate([before, layer_input, after]))
+    near, second_y, extended = together(near, second_y, extended)
     second_z = lax.all_gather(second_y, Z)
     left, right = neighbours(near)
-    blocks = copies(extended, HEAD)
+    blocks = around(extended, "x")
     first_pieces = (near, left, right, swapped(near), swapped(left), swapped(right))
     smem = pl.BlockSpec(memory_space=pltpu.SMEM)
     vmem = pl.BlockSpec(memory_space=pltpu.VMEM)
     struct = jax.ShapeDtypeStruct
     places = 2 * width // 16
+    front_small = jnp.concatenate(
+        [jnp.concatenate([conv_input, conv_maps[:, :STATE]], 1)]
+        + [jnp.pad(value, (0, width + STATE - heads))[None] for value in (step_bias, decay_log)]
+    )
+    back_small = jnp.concatenate(
+        [
+            jnp.pad(conv_maps[:, STATE:], ((0, 0), (0, width - STATE))),
+            jnp.repeat(skip_gain, HEAD_DIM)[None],
+            norm_gain[None],
+            jnp.pad(decay_log, (0, width - heads))[None],
+        ]
+    )
     send, stream, conv, step = kernel_call(
         front_kernel,
         (
@@ -266,11 +284,9 @@
             struct((2, SPAN, 128), F32),
         ),
         [pltpu.VMEM((2 * EXT, width + STATE), F32), pltpu.VMEM((8 * features, width + 2 * STATE), BF16)],
-        [smem] + [vmem] * 10,
+        [smem] + [vmem] * 8,
     )(
-        place, blocks, *first_pieces,
-        jnp.pad(step_bias, (0, wide))[None], jnp.pad(decay_log, (0, wide))[None],
-        jnp.concatenate([conv_input, conv_maps[:, :STATE]], 1),
+        place, blocks, *first_pieces, front_small,
     )
     got = lax.all_to_all(send, SEQ, 0, 0, tiled=True)
     second_own, got = together(second_z, got)
@@ -279,19 +295,20 @@
     entry = lax.all_to_all(entries, SEQ, 0, 0, tiled=True).reshape(2 * width, STATE)
     partial = kernel_call(
         back_kernel,
-        struct((8, SPAN, features), BF16),
+        struct((4, 2, SPAN, features), BF16),
         [
             pltpu.VMEM((2 * EXT, STATE), F32),
             pltpu.VMEM((SPAN, width), F32),
             pltpu.VMEM((8 * features, 2 * width + STATE), BF16),
         ],
-        [smem] + [vmem] * 10,
+        [smem] + [vmem] * 7,
     )(
-        place, stream, second_own, second_other, conv, step, entry, jnp.pad(decay_log, (0, wide))[None], conv_maps[:, STATE:],
-        jnp.repeat(skip_gain, HEAD_DIM)[None], norm_gain[None],
-    )
-    parts = lax.all_to_all(partial, HEAD, 0, 0, tiled=True)
-    return jnp.sum(parts.astype(F32), 0).astype(BF16)
+        place, stream, second_own, second_other, conv, step, entry, back_small,
+    )
+    parts = jnp.sum(lax.all_to_all(partial, "x", 0, 0, tiled=True).astype(F32), 0)
+    low = lax.axis_index("y_hi") == 0
+    kept, sent = jnp.where(low, parts[0], parts[1]), jnp.where(low, parts[1], parts[0]).astype(BF16)
+    return (kept + lax.ppermute(sent, "y_hi", [(0, 1), (1, 0)]).astype(F32)).astype(BF16)
 
 
 def solution(mesh):

time: 191 us -> 177 us (0.927)
  blocking collectives: 53.5 us -> 20.9 us
  starting transfers between devices: 59.7 us -> 80.5 us
  local copies, waits for them, and re-layouts: 16.8 us -> 8.47 us
  waiting for transfers between devices: 32.2 us -> 36.6 us
    all_to_all x1 -> x0, blocking collectives: 29.4 us -> none  [local(): parts = lax.all_to_all(partial, HEAD, 0, 0, tiled=True)]
    ppermute x3 -> x6, starting transfers between devices: 10.2 us -> 24.3 us  [around(): lax.ppermute(block, axis, [(place, (place + step) % count) for place in r...]
    ppermute x0 -> x2, waiting for transfers between devices: none -> 10.8 us  [the longest x1 5.43 us: local(): lax.ppermute(sent, 'y_hi', [(0, 1), (1, 0)]).astype(F32)]
    ppermute x1, waiting for transfers between devices: 10.7 us -> 0.01 us  [neighbours(): lax.ppermute(near[:half], Z, [(z, (z + 1) % count) for z in range(count)])]
    all_to_all x0 -> x1, waiting for transfers between devices: none -> 10.1 us  [local(): lax.all_to_all(partial, 'x', 0, 0, tiled=True).astype(F32)]
    ppermute x0 -> x2, starting transfers between devices: none -> 10.1 us  [the longest x1 5.04 us: local(): lax.ppermute(sent, 'y_hi', [(0, 1), (1, 0)]).astype(F32)]
    all_to_all x2 -> x1, starting transfers between devices: 20.7 us -> 13.9 us  [copies(): lax.all_to_all(jnp.broadcast_to(block[None], (count, *block.shape)), axis...]
    unnamed x39 -> x31, local copies, waits for them, and re-layouts: 11.4 us -> 6.33 us
  transfers between devices with their start and end apart: 15 -> 20, of which waited for: 7 -> 8; matrix products, arithmetic and copies ran while one was open for 2% -> 1% of each run, Pallas kernels for 3% -> 3%
where the time goes in v2:
time: 177 us; the launch traced here: 176 us
  starting transfers between devices  80.5 us (45%)
  waiting for transfers between devices  36.6 us (21%)
  blocking collectives  20.9 us (12%)
  between operations  13.9 us (8%)
  Pallas kernels  12.3 us (7%)
  local copies, waits for them, and re-layouts  8.47 us (5%)
  other arithmetic  3.41 us (2%)
    ppermute x6, starting transfers between devices, around(): lax.ppermute(block, axis, [(place, (place + step) % count) for place in r...  24.3 us
    all_to_all x1, blocking collectives, local(): got = lax.all_to_all(send, SEQ, 0, 0, tiled=True)  20.9 us
    all_to_all x1, starting transfers between devices, copies(): lax.all_to_all(jnp.broadcast_to(block[None], (count, *block.shape)), axis...  13.9 us
    all_to_all x1, waiting for transfers between devices, local(): lax.all_to_all(entries, SEQ, 0, 0, tiled=True).reshape(2 * width, STATE)  11.8 us
    ppermute x4, starting transfers between devices, swapped(): return lax.ppermute(block, 'core', [(0, 1), (1, 0)])  10.8 us
    all_to_all x1, waiting for transfers between devices, local(): lax.all_to_all(partial, 'x', 0, 0, tiled=True).astype(F32)  10.1 us
    pallas_call x1, Pallas kernels, local(): kernel_call(back_kernel, struct((4, 2, SPAN, features), BF16), [pltpu.VME...  6.84 us
    unnamed x31, local copies, waits for them, and re-layouts  6.33 us
  transfers between devices with their start and end apart: 20, of which 8 were waited for; matrix products, arithmetic and copies ran while one was open for 1% of the time, Pallas kernels for 3%

profile of v2, /device:TPU:8, one launch (start us, length us, event | category | flops | bytes accessed | tf_op | source)
XLA Modules:
  0.0 176.1 jit_solution(14021774634496086143)
XLA Ops:
  9.9 13.9 %all-to-all-start = ((bf16[16,32,768]{2,1,0:T(8,128)(2,1)}), bf16[16,32,768]{2,1,0:T(8,128)(2,1)S(1)}, u32[]{:S(2)}, u32[]{:S(2)}) async-start(bf16[16,32,768]{2,1,0:T(8,128)(2,1)} %broadcast_in_dim.25), calls=%async_computation | async-start | bytes 1572864 | tf_op jit(solution)/shard_map/all_to_all | solution.py:207
  23.9 1.9 %collective-permute-start.3 = (bf16[16,256]{1,0:T(8,128)(2,1)S(1)}, bf16[16,256]{1,0:T(8,128)(2,1)S(1)}, u32[]{:S(2)}, u32[]{:S(2)}) collective-permute-start(bf16[16,256]{1,0:T(8,128)(2,1)S(1)} %get-tuple-element.28), channel_id=1, source_target_pairs={{0,8},{8,16},{16,24},{24,32},{32,40},{40,48},{48,56},{56,64},{64,7... | collective-permute-start | bytes 24584 | tf_op jit(solution)/shard_map/ppermute | solution.py:213
  25.9 1.9 %collective-permute-start.2 = (bf16[32,1152]{1,0:T(8,128)(2,1)S(1)}, bf16[32,1152]{1,0:T(8,128)(2,1)S(1)}, u32[]{:S(2)}, u32[]{:S(2)}) collective-permute-start(bf16[32,1152]{1,0:T(8,128)(2,1)S(1)} %get-tuple-element.26), channel_id=1, source_target_pairs={{0,384},{128,0},{256,128},{384,256},{1,385},{129,1},{257,129},{385... | collective-permute-start | bytes 221192 | tf_op jit(solution)/shard_map/ppermute | solution.py:230
  27.8 3.9 %collective-permute-start = (bf16[32,1152]{1,0:T(8,128)(2,1)S(1)}, bf16[32,1152]{1,0:T(8,128)(2,1)S(1)}, u32[]{:S(2)}, u32[]{:S(2)}) collective-permute-start(bf16[32,1152]{1,0:T(8,128)(2,1)S(1)} %get-tuple-element.26), channel_id=1, source_target_pairs={{0,128},{128,256},{256,384},{384,0},{1,129},{129,257},{257,385},{3... | collective-permute-start | bytes 221192 | tf_op jit(solution)/shard_map/ppermute | solution.py:230
  31.8 6.1 %collective-permute-start.1 = (bf16[32,1152]{1,0:T(8,128)(2,1)S(1)}, bf16[32,1152]{1,0:T(8,128)(2,1)S(1)}, u32[]{:S(2)}, u32[]{:S(2)}) collective-permute-start(bf16[32,1152]{1,0:T(8,128)(2,1)S(1)} %get-tuple-element.26), channel_id=1, source_target_pairs={{0,256},{128,384},{256,0},{384,128},{1,257},{129,385},{257,1},{385... | collective-permute-start | bytes 221192 | tf_op jit(solution)/shard_map/ppermute | solution.py:230
  37.8 3.1 %collective-permute-start.4 = (bf16[16,256]{1,0:T(8,128)(2,1)S(1)}, bf16[16,256]{1,0:T(8,128)(2,1)S(1)}, u32[]{:S(2)}, u32[]{:S(2)}) collective-permute-start(bf16[16,256]{1,0:T(8,128)(2,1)S(1)} %get-tuple-element.27), channel_id=1, source_target_pairs={{8,0},{16,8},{24,16},{32,24},{40,32},{48,40},{56,48},{64,56},{72,6... | collective-permute-start | bytes 24584 | tf_op jit(solution)/shard_map/ppermute | solution.py:213
  41.0 1.3 collective-permute-done.4
  42.3 5.0 %collective-permute-start.5 = (bf16[160,256]{1,0:T(8,128)(2,1)S(1)}, bf16[160,256]{1,0:T(8,128)(2,1)S(1)}, u32[]{:S(2)}, u32[]{:S(2)}) collective-permute-start(bf16[160,256]{1,0:T(8,128)(2,1)S(1)} %constant_dynamic-update-slice_fusion), channel_id=1, source_target_pairs={{0,4},{4,0},{1,5},{5,1},{2,6},{6,2},{3,7},{7,3},{8,12},{12,8},{9,1... | collective-permute-start | bytes 245768 | tf_op jit(solution)/shard_map/ppermute | solution.py:255
  49.4 5.4 %collective-permute-done.5 = bf16[160,256]{1,0:T(8,128)(2,1)S(1)} collective-permute-done((bf16[160,256]{1,0:T(8,128)(2,1)S(1)}, bf16[160,256]{1,0:T(8,128)(2,1)S(1)}, u32[]{:S(2)}, u32[]{:S(2)}) %collective-permute-start.5) | collective-permute-done | bytes 81952 | tf_op jit(solution)/shard_map/ppermute | solution.py:255
  54.9 3.4 %collective-permute-start.9 = (bf16[8,32,768]{2,1,0:T(8,128)(2,1)S(1)}, bf16[8,32,768]{2,1,0:T(8,128)(2,1)S(1)}, u32[]{:S(2)}, u32[]{:S(2)}) collective-permute-start(bf16[8,32,768]{2,1,0:T(8,128)(2,1)S(1)} %get-tuple-element.24), channel_id=1, source_target_pairs={{0,16},{16,32},{32,48},{48,64},{64,80},{80,96},{96,112},{112,0},{1... | collective-permute-start | bytes 1179656 | tf_op jit(solution)/shard_map/ppermute | solution.py:222
  58.4 3.6 %collective-permute-start.10 = (bf16[8,32,768]{2,1,0:T(8,128)(2,1)S(1)}, bf16[8,32,768]{2,1,0:T(8,128)(2,1)S(1)}, u32[]{:S(2)}, u32[]{:S(2)}) collective-permute-start(bf16[8,32,768]{2,1,0:T(8,128)(2,1)S(1)} %get-tuple-element.23), channel_id=1, source_target_pairs={{0,112},{16,0},{32,16},{48,32},{64,48},{80,64},{96,80},{112,96},{1... | collective-permute-start | bytes 1179656 | tf_op jit(solution)/shard_map/ppermute | solution.py:223
  62.0 4.3 %collective-permute-start.11 = (bf16[16,32,768]{2,1,0:T(8,128)(2,1)S(1)}, bf16[16,32,768]{2,1,0:T(8,128)(2,1)S(1)}, u32[]{:S(2)}, u32[]{:S(2)}) collective-permute-start(bf16[16,32,768]{2,1,0:T(8,128)(2,1)S(1)} %all-to-all-done.n0), channel_id=1, source_target_pairs={{0,8},{8,0},{1,9},{9,1},{2,10},{10,2},{3,11},{11,3},{4,12},{12,4},... | collective-permute-start | bytes 2359304 | tf_op jit(solution)/shard_map/ppermute | solution.py:217
  66.3 3.4 %collective-permute-start.6 = (bf16[2,160,256]{2,1,0:T(8,128)(2,1)S(1)}, bf16[2,160,256]{2,1,0:T(8,128)(2,1)S(1)}, u32[]{:S(2)}, u32[]{:S(2)}) collective-permute-start(bf16[2,160,256]{2,1,0:T(8,128)(2,1)S(1)} %pad_maximum_fusion.2), channel_id=1, source_target_pairs={{0,1},{1,2},{2,3},{3,0},{4,5},{5,6},{6,7},{7,4},{8,9},{9,10},{10,1... | collective-permute-start | bytes 491528 | tf_op jit(solution)/shard_map/ppermute | solution.py:230
  69.7 4.6 %collective-permute-start.7 = (bf16[2,160,256]{2,1,0:T(8,128)(2,1)S(1)}, bf16[2,160,256]{2,1,0:T(8,128)(2,1)}, u32[]{:S(2)}, u32[]{:S(2)}) collective-permute-start(bf16[2,160,256]{2,1,0:T(8,128)(2,1)S(1)} %pad_maximum_fusion.2), channel_id=1, source_target_pairs={{0,2},{1,3},{2,0},{3,1},{4,6},{5,7},{6,4},{7,5},{8,10},{9,11},{10,... | collective-permute-start | bytes 491528 | tf_op jit(solution)/shard_map/ppermute | solution.py:230
  74.3 1.2 collective-permute-done.6
  75.5 4.4 %collective-permute-start.8 = (bf16[2,160,256]{2,1,0:T(8,128)(2,1)S(1)}, bf16[2,160,256]{2,1,0:T(8,128)(2,1)}, u32[]{:S(2)}, u32[]{:S(2)}) collective-permute-start(bf16[2,160,256]{2,1,0:T(8,128)(2,1)S(1)} %pad_maximum_fusion.2), channel_id=1, source_target_pairs={{0,3},{1,0},{2,1},{3,2},{4,7},{5,4},{6,5},{7,6},{8,11},{9,8},{10,9... | collective-permute-start | bytes 491528 | tf_op jit(solution)/shard_map/ppermute | solution.py:230
  79.9 1.9 %collective-permute-start.12 = (bf16[8,32,768]{2,1,0:T(8,128)(2,1)S(1)}, bf16[8,32,768]{2,1,0:T(8,128)(2,1)S(1)}, u32[]{:S(2)}, u32[]{:S(2)}) collective-permute-start(bf16[8,32,768]{2,1,0:T(8,128)(2,1)S(1)} %collective-permute-done.9.l0), channel_id=1, source_target_pairs={{0,8},{8,0},{1,9},{9,1},{2,10},{10,2},{3,11},{11,3},{4,12},{12,4},... | collective-permute-start | bytes 1179656 | tf_op jit(solution)/shard_map/ppermute | solution.py:217
  81.8 2.4 %collective-permute-start.13 = (bf16[8,32,768]{2,1,0:T(8,128)(2,1)S(1)}, bf16[8,32,768]{2,1,0:T(8,128)(2,1)S(1)}, u32[]{:S(2)}, u32[]{:S(2)}) collective-permute-start(bf16[8,32,768]{2,1,0:T(8,128)(2,1)S(1)} %collective-permute-done.10.r0), channel_id=1, source_target_pairs={{0,8},{8,0},{1,9},{9,1},{2,10},{10,2},{3,11},{11,3},{4,12},{12,4},... | collective-permute-start | bytes 1179656 | tf_op jit(solution)/shard_map/ppermute | solution.py:217
  84.5 1.1 pad_maximum_fusion.x_ref
  85.7 4.0 %shard_map.118 = (bf16[64,24,128]{2,1,0:T(8,128)(2,1)S(1)}, bf16[288,2048]{1,0:T(8,128)(2,1)S(1)}, bf16[2,128,640]{2,1,0:T(8,128)(2,1)S(1)}, f32[2,128,128]{2,1,0:T(8,128)S(1)}) custom-call(s32[6]{0:T(128)S(1)} %stack.66.place_ref, bf16[4,2,160,256]{3,2,1,0:T(8,128)(2,1)S(1)} %pad_maximum_fusion.x_ref, bf16[16,32,768]{2,1,0:T(8,128)(2,1)S(1)} %all-to-all-done.n0, ...), custom_call_target="tpu_custom_call" | custom-call | tf_op jit(solution)/shard_map/pallas_call | solution.py:278
  91.3 20.9 %all_to_all.20.got_ref = bf16[64,24,128]{2,1,0:T(8,128)(2,1)S(1)} all-to-all(bf16[64,24,128]{2,1,0:T(8,128)(2,1)S(1)} %get-tuple-element.18), channel_id=1, replica_groups=mesh['y_lo'=4,'z_pair'=4,'z_bit'=2,'core'=2,'y_hi'=2,'x'=4] {'y_lo','z_p..., dimensions={0} | all-to-all | bytes 786432 | tf_op jit(solution)/shard_map/all_to_all | solution.py:291
  112.2 2.2 %collective-permute-start.14 = (bf16[8,4,32,1152]{3,2,1,0:T(8,128)(2,1)}, bf16[8,4,32,1152]{3,2,1,0:T(8,128)(2,1)S(1)}, u32[]{:S(2)}, u32[]{:S(2)}) collective-permute-start(bf16[8,4,32,1152]{3,2,1,0:T(8,128)(2,1)} %bitcast.28), channel_id=1, source_target_pairs={{0,8},{8,0},{1,9},{9,1},{2,10},{10,2},{3,11},{11,3},{4,12},{12,4},... | collective-permute-start | bytes 7077896 | tf_op jit(solution)/shard_map/ppermute | solution.py:217
  114.5 1.5 shard_map.119
  116.0 5.8 %all-to-all-start.2 = ((bf16[64,16,128]{2,1,0:T(8,128)(2,1)}), bf16[64,16,128]{2,1,0:T(8,128)(2,1)S(1)}, u32[]{:S(2)}, u32[]{:S(2)}) async-start(bf16[64,16,128]{2,1,0:T(8,128)(2,1)} %shard_map.119), calls=%async_computation.2 | async-start | bytes 524288 | tf_op jit(solution)/shard_map/all_to_all | solution.py:295
  122.0 11.8 %all-to-all-done.2 = bf16[64,16,128]{2,1,0:T(8,128)(2,1)S(1)} async-done(((bf16[64,16,128]{2,1,0:T(8,128)(2,1)}), bf16[64,16,128]{2,1,0:T(8,128)(2,1)S(1)}, u32[]{:S(2)}, u32[]{:S(2)}) %all-to-all-start.2) | async-done | bytes 262176 | tf_op jit(solution)/shard_map/all_to_all | solution.py:295
  133.7 1.7 copy-done
  135.4 1.3 copy-done.2
  137.6 6.8 %shard_map.120 = bf16[4,2,128,256]{3,2,1,0:T(8,128)(2,1)} custom-call(s32[6]{0:T(128)S(1)} %stack.66.place_ref, bf16[288,2048]{1,0:T(8,128)(2,1)S(1)} %copy-done.2, bf16[8,4,32,1152]{3,2,1,0:T(8,128)(2,1)S(1)} %bitcast.29, bf16[8,4,32,1152]{3,2,1,0:T(8,128)(2,1)S(1)} %collective-permute-done.14.other_ref, ...), custom_call_target="tpu_custom_call" | custom-call | tf_op jit(solution)/shard_map/pallas_call | solution.py:296
  144.4 3.5 %all-to-all-start.3 = ((bf16[4,2,128,256]{3,2,1,0:T(8,128)(2,1)}), bf16[4,2,128,256]{3,2,1,0:T(8,128)(2,1)S(1)}, u32[]{:S(2)}, u32[]{:S(2)}) async-start(bf16[4,2,128,256]{3,2,1,0:T(8,128)(2,1)} %shard_map.120), calls=%async_computation.3 | async-start | bytes 1048576 | tf_op jit(solution)/shard_map/all_to_all | solution.py:308
  147.9 10.1 %all-to-all-done.3 = bf16[4,2,128,256]{3,2,1,0:T(8,128)(2,1)S(1)} async-done(((bf16[4,2,128,256]{3,2,1,0:T(8,128)(2,1)}), bf16[4,2,128,256]{3,2,1,0:T(8,128)(2,1)S(1)}, u32[]{:S(2)}, u32[]{:S(2)}) %all-to-all-start.3) | async-done | bytes 524320 | tf_op jit(solution)/shard_map/all_to_all | solution.py:308
  158.1 5.0 %collective-permute-start.15 = (bf16[128,256]{1,0:T(8,128)(2,1)S(1)}, bf16[128,256]{1,0:T(8,128)(2,1)S(1)}, u32[]{:S(2)}, u32[]{:S(2)}) collective-permute-start(bf16[128,256]{1,0:T(8,128)(2,1)S(1)} %fusion.1), channel_id=1, source_target_pairs={{0,4},{4,0},{1,5},{5,1},{2,6},{6,2},{3,7},{7,3},{8,12},{12,8},{9,1... | collective-permute-start | bytes 196616 | tf_op jit(solution)/shard_map/ppermute | solution.py:311
  163.2 5.4 %collective-permute-done.15 = bf16[128,256]{1,0:T(8,128)(2,1)S(1)} collective-permute-done((bf16[128,256]{1,0:T(8,128)(2,1)S(1)}, bf16[128,256]{1,0:T(8,128)(2,1)S(1)}, u32[]{:S(2)}, u32[]{:S(2)}) %collective-permute-start.15) | collective-permute-done | bytes 65568 | tf_op jit(solution)/shard_map/ppermute | solution.py:311
  (70 shorter events, 9.3 us)
Async XLA Ops:
  6.5 17.4 %copy-start.5 = (bf16[128,256]{1,0:T(8,128)(2,1)S(1)}, bf16[128,256]{1,0:T(8,128)(2,1)}, u32[]{:S(2)}) copy-start(bf16[128,256]{1,0:T(8,128)(2,1)} %param.12) | copy-start | bytes 196612
  6.5 19.3 %copy-start.7 = (bf16[512,32]{0,1:T(8,128)(2,1)S(1)}, bf16[512,32]{0,1:T(8,128)(2,1)}, u32[]{:S(2)}) copy-start(bf16[512,32]{0,1:T(8,128)(2,1)} %param.23) | copy-start | bytes 98308
  6.5 19.3 %copy-start.6 = (bf16[32,512]{1,0:T(8,128)(2,1)S(1)}, bf16[32,512]{1,0:T(8,128)(2,1)}, u32[]{:S(2)}) copy-start(bf16[32,512]{1,0:T(8,128)(2,1)} %param.14) | copy-start | bytes 98308
  9.9 74.4 %copy-start.9 = (f32[4,256]{1,0:T(4,128)S(1)}, f32[4,256]{1,0:T(4,128)}, u32[]{:S(2)}) copy-start(f32[4,256]{1,0:T(4,128)} %param.21) | copy-start | bytes 12292
  9.9 74.4 %copy-start.12 = (f32[8]{0:T(128)S(1)}, f32[8]{0:T(128)}, u32[]{:S(2)}) copy-start(f32[8]{0:T(128)} %param.17) | copy-start | bytes 100
  9.9 74.4 %copy-start.11 = (f32[8]{0:T(128)S(1)}, f32[8]{0:T(128)}, u32[]{:S(2)}) copy-start(f32[8]{0:T(128)} %param.18) | copy-start | bytes 100
  9.9 74.6 %copy-start.8 = (f32[4,512]{1,0:T(4,128)S(1)}, f32[4,512]{1,0:T(4,128)}, u32[]{:S(2)}) copy-start(f32[4,512]{1,0:T(4,128)} %param.20) | copy-start | bytes 24580
  9.9 44.9 %all-to-all-start = ((bf16[16,32,768]{2,1,0:T(8,128)(2,1)}), bf16[16,32,768]{2,1,0:T(8,128)(2,1)S(1)}, u32[]{:S(2)}, u32[]{:S(2)}) async-start(bf16[16,32,768]{2,1,0:T(8,128)(2,1)} %broadcast_in_dim.25), calls=%async_computation | async-start | bytes 1572864 | tf_op jit(solution)/shard_map/all_to_all | solution.py:207
  23.9 88.4 %all-gather.3.cloned.1.call-start = ((), (), s32[]{:S(2)}) async-start(), calls=%async_computation.4 | async-start | bytes 2654208 | tf_op jit(solution)/shard_map/all_gather | solution.py:258
  23.9 17.0 %collective-permute-start.3 = (bf16[16,256]{1,0:T(8,128)(2,1)S(1)}, bf16[16,256]{1,0:T(8,128)(2,1)S(1)}, u32[]{:S(2)}, u32[]{:S(2)}) collective-permute-start(bf16[16,256]{1,0:T(8,128)(2,1)S(1)} %get-tuple-element.28), channel_id=1, source_target_pairs={{0,8},{8,16},{16,24},{24,32},{32,40},{40,48},{48,56},{56,64},{64,7... | collective-permute-start | bytes 24584 | tf_op jit(solution)/shard_map/ppermute | solution.py:213
  25.9 22.2 %collective-permute-start.2 = (bf16[32,1152]{1,0:T(8,128)(2,1)S(1)}, bf16[32,1152]{1,0:T(8,128)(2,1)S(1)}, u32[]{:S(2)}, u32[]{:S(2)}) collective-permute-start(bf16[32,1152]{1,0:T(8,128)(2,1)S(1)} %get-tuple-element.26), channel_id=1, source_target_pairs={{0,384},{128,0},{256,128},{384,256},{1,385},{129,1},{257,129},{385... | collective-permute-start | bytes 221192 | tf_op jit(solution)/shard_map/ppermute | solution.py:230
  27.8 20.3 %collective-permute-start = (bf16[32,1152]{1,0:T(8,128)(2,1)S(1)}, bf16[32,1152]{1,0:T(8,128)(2,1)S(1)}, u32[]{:S(2)}, u32[]{:S(2)}) collective-permute-start(bf16[32,1152]{1,0:T(8,128)(2,1)S(1)} %get-tuple-element.26), channel_id=1, source_target_pairs={{0,128},{128,256},{256,384},{384,0},{1,129},{129,257},{257,385},{3... | collective-permute-start | bytes 221192 | tf_op jit(solution)/shard_map/ppermute | solution.py:230
  31.8 16.9 %collective-permute-start.1 = (bf16[32,1152]{1,0:T(8,128)(2,1)S(1)}, bf16[32,1152]{1,0:T(8,128)(2,1)S(1)}, u32[]{:S(2)}, u32[]{:S(2)}) collective-permute-start(bf16[32,1152]{1,0:T(8,128)(2,1)S(1)} %get-tuple-element.26), channel_id=1, source_target_pairs={{0,256},{128,384},{256,0},{384,128},{1,257},{129,385},{257,1},{385... | collective-permute-start | bytes 221192 | tf_op jit(solution)/shard_map/ppermute | solution.py:230
  37.8 4.5 %collective-permute-start.4 = (bf16[16,256]{1,0:T(8,128)(2,1)S(1)}, bf16[16,256]{1,0:T(8,128)(2,1)S(1)}, u32[]{:S(2)}, u32[]{:S(2)}) collective-permute-start(bf16[16,256]{1,0:T(8,128)(2,1)S(1)} %get-tuple-element.27), channel_id=1, source_target_pairs={{8,0},{16,8},{24,16},{32,24},{40,32},{48,40},{56,48},{64,56},{72,6... | collective-permute-start | bytes 24584 | tf_op jit(solution)/shard_map/ppermute | solution.py:213
  42.3 12.5 %collective-permute-start.5 = (bf16[160,256]{1,0:T(8,128)(2,1)S(1)}, bf16[160,256]{1,0:T(8,128)(2,1)S(1)}, u32[]{:S(2)}, u32[]{:S(2)}) collective-permute-start(bf16[160,256]{1,0:T(8,128)(2,1)S(1)} %constant_dynamic-update-slice_fusion), channel_id=1, source_target_pairs={{0,4},{4,0},{1,5},{5,1},{2,6},{6,2},{3,7},{7,3},{8,12},{12,8},{9,1... | collective-permute-start | bytes 245768 | tf_op jit(solution)/shard_map/ppermute | solution.py:255
  54.9 25.0 %collective-permute-start.9 = (bf16[8,32,768]{2,1,0:T(8,128)(2,1)S(1)}, bf16[8,32,768]{2,1,0:T(8,128)(2,1)S(1)}, u32[]{:S(2)}, u32[]{:S(2)}) collective-permute-start(bf16[8,32,768]{2,1,0:T(8,128)(2,1)S(1)} %get-tuple-element.24), channel_id=1, source_target_pairs={{0,16},{16,32},{32,48},{48,64},{64,80},{80,96},{96,112},{112,0},{1... | collective-permute-start | bytes 1179656 | tf_op jit(solution)/shard_map/ppermute | solution.py:222
  58.4 23.5 %collective-permute-start.10 = (bf16[8,32,768]{2,1,0:T(8,128)(2,1)S(1)}, bf16[8,32,768]{2,1,0:T(8,128)(2,1)S(1)}, u32[]{:S(2)}, u32[]{:S(2)}) collective-permute-start(bf16[8,32,768]{2,1,0:T(8,128)(2,1)S(1)} %get-tuple-element.23), channel_id=1, source_target_pairs={{0,112},{16,0},{32,16},{48,32},{64,48},{80,64},{96,80},{112,96},{1... | collective-permute-start | bytes 1179656 | tf_op jit(solution)/shard_map/ppermute | solution.py:223
  62.0 23.6 %collective-permute-start.11 = (bf16[16,32,768]{2,1,0:T(8,128)(2,1)S(1)}, bf16[16,32,768]{2,1,0:T(8,128)(2,1)S(1)}, u32[]{:S(2)}, u32[]{:S(2)}) collective-permute-start(bf16[16,32,768]{2,1,0:T(8,128)(2,1)S(1)} %all-to-all-done.n0), channel_id=1, source_target_pairs={{0,8},{8,0},{1,9},{9,1},{2,10},{10,2},{3,11},{11,3},{4,12},{12,4},... | collective-permute-start | bytes 2359304 | tf_op jit(solution)/shard_map/ppermute | solution.py:217
  66.3 9.2 %collective-permute-start.6 = (bf16[2,160,256]{2,1,0:T(8,128)(2,1)S(1)}, bf16[2,160,256]{2,1,0:T(8,128)(2,1)S(1)}, u32[]{:S(2)}, u32[]{:S(2)}) collective-permute-start(bf16[2,160,256]{2,1,0:T(8,128)(2,1)S(1)} %pad_maximum_fusion.2), channel_id=1, source_target_pairs={{0,1},{1,2},{2,3},{3,0},{4,5},{5,6},{6,7},{7,4},{8,9},{9,10},{10,1... | collective-permute-start | bytes 491528 | tf_op jit(solution)/shard_map/ppermute | solution.py:230
  69.7 14.8 %collective-permute-start.7 = (bf16[2,160,256]{2,1,0:T(8,128)(2,1)S(1)}, bf16[2,160,256]{2,1,0:T(8,128)(2,1)}, u32[]{:S(2)}, u32[]{:S(2)}) collective-permute-start(bf16[2,160,256]{2,1,0:T(8,128)(2,1)S(1)} %pad_maximum_fusion.2), channel_id=1, source_target_pairs={{0,2},{1,3},{2,0},{3,1},{4,6},{5,7},{6,4},{7,5},{8,10},{9,11},{10,... | collective-permute-start | bytes 491528 | tf_op jit(solution)/shard_map/ppermute | solution.py:230
  75.5 9.0 %collective-permute-start.8 = (bf16[2,160,256]{2,1,0:T(8,128)(2,1)S(1)}, bf16[2,160,256]{2,1,0:T(8,128)(2,1)}, u32[]{:S(2)}, u32[]{:S(2)}) collective-permute-start(bf16[2,160,256]{2,1,0:T(8,128)(2,1)S(1)} %pad_maximum_fusion.2), channel_id=1, source_target_pairs={{0,3},{1,0},{2,1},{3,2},{4,7},{5,4},{6,5},{7,6},{8,11},{9,8},{10,9... | collective-permute-start | bytes 491528 | tf_op jit(solution)/shard_map/ppermute | solution.py:230
  79.9 5.7 %collective-permute-start.12 = (bf16[8,32,768]{2,1,0:T(8,128)(2,1)S(1)}, bf16[8,32,768]{2,1,0:T(8,128)(2,1)S(1)}, u32[]{:S(2)}, u32[]{:S(2)}) collective-permute-start(bf16[8,32,768]{2,1,0:T(8,128)(2,1)S(1)} %collective-permute-done.9.l0), channel_id=1, source_target_pairs={{0,8},{8,0},{1,9},{9,1},{2,10},{10,2},{3,11},{11,3},{4,12},{12,4},... | collective-permute-start | bytes 1179656 | tf_op jit(solution)/shard_map/ppermute | solution.py:217
  81.8 3.8 %collective-permute-start.13 = (bf16[8,32,768]{2,1,0:T(8,128)(2,1)S(1)}, bf16[8,32,768]{2,1,0:T(8,128)(2,1)S(1)}, u32[]{:S(2)}, u32[]{:S(2)}) collective-permute-start(bf16[8,32,768]{2,1,0:T(8,128)(2,1)S(1)} %collective-permute-done.10.r0), channel_id=1, source_target_pairs={{0,8},{8,0},{1,9},{9,1},{2,10},{10,2},{3,11},{11,3},{4,12},{12,4},... | collective-permute-start | bytes 1179656 | tf_op jit(solution)/shard_map/ppermute | solution.py:217
  85.6 36.2 %copy-start.13 = (f32[8]{0:T(128)S(1)}, f32[8]{0:T(128)}, u32[]{:S(2)}) copy-start(f32[8]{0:T(128)} %param.19) | copy-start | bytes 100
  85.6 36.3 %copy-start.10 = (f32[512]{0:T(512)S(1)}, f32[512]{0:T(512)}, u32[]{:S(2)}) copy-start(f32[512]{0:T(512)} %param.22) | copy-start | bytes 6148
  89.6 1.0 copy-start.1
  112.2 21.5 %collective-permute-start.14 = (bf16[8,4,32,1152]{3,2,1,0:T(8,128)(2,1)}, bf16[8,4,32,1152]{3,2,1,0:T(8,128)(2,1)S(1)}, u32[]{:S(2)}, u32[]{:S(2)}) collective-permute-start(bf16[8,4,32,1152]{3,2,1,0:T(8,128)(2,1)} %bitcast.28), channel_id=1, source_target_pairs={{0,8},{8,0},{1,9},{9,1},{2,10},{10,2},{3,11},{11,3},{4,12},{12,4},... | collective-permute-start | bytes 7077896 | tf_op jit(solution)/shard_map/ppermute | solution.py:217
  116.0 17.7 %all-to-all-start.2 = ((bf16[64,16,128]{2,1,0:T(8,128)(2,1)}), bf16[64,16,128]{2,1,0:T(8,128)(2,1)S(1)}, u32[]{:S(2)}, u32[]{:S(2)}) async-start(bf16[64,16,128]{2,1,0:T(8,128)(2,1)} %shard_map.119), calls=%async_computation.2 | async-start | bytes 524288 | tf_op jit(solution)/shard_map/all_to_all | solution.py:295
  133.7 1.7 copy-start
  135.4 1.3 copy-start.2
  144.4 13.6 %all-to-all-start.3 = ((bf16[4,2,128,256]{3,2,1,0:T(8,128)(2,1)}), bf16[4,2,128,256]{3,2,1,0:T(8,128)(2,1)S(1)}, u32[]{:S(2)}, u32[]{:S(2)}) async-start(bf16[4,2,128,256]{3,2,1,0:T(8,128)(2,1)} %shard_map.120), calls=%async_computation.3 | async-start | bytes 1048576 | tf_op jit(solution)/shard_map/all_to_all | solution.py:308
  158.1 10.5 %collective-permute-start.15 = (bf16[128,256]{1,0:T(8,128)(2,1)S(1)}, bf16[128,256]{1,0:T(8,128)(2,1)S(1)}, u32[]{:S(2)}, u32[]{:S(2)}) collective-permute-start(bf16[128,256]{1,0:T(8,128)(2,1)S(1)} %fusion.1), channel_id=1, source_target_pairs={{0,4},{4,0},{1,5},{5,1},{2,6},{6,2},{3,7},{7,3},{8,12},{12,8},{9,1... | collective-permute-start | bytes 196616 | tf_op jit(solution)/shard_map/ppermute | solution.py:311
  (2 other events, 1.6 us)
Sparse Core Ops, SparseCore 0:
  55.0 45.2 all-gather.2

commit v3 on v2

--- a/solution.py
+++ b/solution.py
@@ -79,15 +79,12 @@
             full_ref[pl.ds(pl.multiple_of(start + 64 * (1 - bit), 32), 32)] = far[...]
 
 
-def assemble_ring(place_ref, pieces, full_ref):
-    core, y_lo = place_ref[2], place_ref[3]
-    for side in range(2):
-        column = core + side - 2 * core * side
-        for step in range(4):
-            y = (y_lo + 4 - step) % 4
-            for z in range(8):
-                start = 512 * y + 64 * z + 32 * column
-                full_ref[pl.ds(pl.multiple_of(start, 32), 32)] = pieces[side][z, step]
+def pack_kernel(input_ref, maps_ref, step_ref, out_ref):
+    heads = step_ref.shape[0]
+    step = t_mm(step_ref[...], ones_where(iota((heads, 128), 0) == iota((heads, 128), 1))).astype(BF16)
+    block = jnp.concatenate([input_ref[...], maps_ref[:, :STATE], step], 1)
+    for copy in range(out_ref.shape[0]):
+        out_ref[copy] = block
 
 
 def front_kernel(
@@ -95,11 +92,11 @@
     send_ref, stream_ref, conv_ref, step_ref, rows_ref, full_ref,
 ):
     assemble(place_ref, (n0, l0, r0, n1, l1, r1), full_ref)
-    y_hi, x = place_ref[4], place_ref[5]
+    y_hi = place_ref[4]
     flip_rows, flip_columns = reversal(EXT), reversal(256)
     for step in range(4):
         for side in range(2):
-            block = 4 * (y_hi + side - 2 * y_hi * side) + (x + 4 - step) % 4
+            block = 4 * (y_hi + side - 2 * y_hi * side) + step
             stream_ref[:EXT, pl.ds(pl.multiple_of(block * 256, 256), 256)] = x_ref[step, side, :EXT]
             turned = mm(x_ref[step, side, HALO:], flip_columns).astype(BF16)
             stream_ref[EXT:, pl.ds(pl.multiple_of((7 - block) * 256, 256), 256)] = mm(flip_rows, turned).astype(BF16)
@@ -149,17 +146,24 @@
     lax.fori_loop(0, blocks, one, jnp.zeros((16, STATE), F32), unroll=4)
 
 
-def back_kernel(
-    place_ref, stream_ref, own_ref, other_ref, conv_ref, step_ref, entry_ref, small_ref,
-    out_ref, rows_ref, inner_ref, full_ref,
+def inner_kernel(
+    place_ref, stream_ref, own_ref, other_ref, conv_ref, step_ref, small_ref,
+    map_ref, inner_ref, gate_ref, weights_ref, rows_ref, full_ref,
 ):
-    assemble_ring(place_ref, (own_ref, other_ref), full_ref)
-    width = inner_ref.shape[1]
-    proj = mm(stream_ref[...], full_ref[:, width:])
+    core, y_lo = place_ref[2], place_ref[3]
+    width = inner_ref.shape[2]
+    for side, ref in enumerate((own_ref, other_ref)):
+        column = core + side - 2 * core * side
+        for step in range(4):
+            y = (y_lo + 4 - step) % 4
+            for z in range(8):
+                start = pl.ds(pl.multiple_of(512 * y + 64 * z + 32 * column, 32), 32)
+                weights_ref[0, start] = ref[z, step, :, :width]
+                full_ref[start] = ref[z, step, :, width:]
+    proj = mm(stream_ref[...], full_ref[...])
     taps, log_rate = small_ref[:CONV, :STATE], small_ref[6:7, :128]
     rows_ref[...] = proj[:, width:].astype(BF16).astype(F32)
     causal = iota((SPAN, SPAN), 0) >= iota((SPAN, SPAN), 1)
-    normed = []
     for branch in range(2):
         gate = silu(proj[branch * EXT + HALO : (branch + 1) * EXT, :width].astype(BF16).astype(F32))
         base = branch * EXT + HALO - (CONV - 1)
@@ -167,6 +171,7 @@
         for tap in range(1, CONV):
             running = running + taps[tap : tap + 1] * rows_ref[base + tap : base + tap + SPAN]
         out_map = silu(running).astype(BF16)
+        map_ref[branch] = out_map
         scores = mm_t(out_map, conv_ref[branch, :, width:])
         step = step_ref[branch]
         cum = running_sum(step * -jnp.exp(log_rate))
@@ -177,18 +182,29 @@
             decay = jnp.where(causal, jnp.exp(jnp.where(causal, differ, 0.0)), 0.0)
             weights = (scores * decay * step_t[head : head + 1]).astype(BF16)
             x_head = conv_ref[branch, :, channels]
-            inner_ref[:, channels] = mm(weights, x_head) + small_ref[4:5, channels] * x_head.astype(F32)
-        entry = entry_ref[branch * width : (branch + 1) * width]
-        carried = mm_t(out_map, entry) * spread(jnp.exp(cum), width)
-        gated = (inner_ref[...] + carried) * gate
+            inner_ref[branch, :, channels] = mm(weights, x_head) + small_ref[4:5, channels] * x_head.astype(F32)
+        inner_ref[branch] = inner_ref[branch] * gate
+        gate_ref[branch] = spread(jnp.exp(cum), width) * gate
+    flip = reversal(256)
+    for block in range(8):
+        near, far = (slice(part * 256, (part + 1) * 256) for part in (block, 7 - block))
+        weights_ref[1, near] = mm(flip, weights_ref[0, far]).astype(BF16)
+
+
+def out_kernel(entry_ref, map_ref, inner_ref, gate_ref, weights_ref, small_ref, out_ref):
+    width = inner_ref.shape[2]
+    normed = []
+    for branch in range(2):
+        carried = mm_t(map_ref[branch], entry_ref[branch * width : (branch + 1) * width])
+        gated = inner_ref[branch] + carried * gate_ref[branch]
         square = jnp.mean(gated * gated, axis=-1, keepdims=True)
         normed.append((gated * lax.rsqrt(square + 1e-05) * small_ref[5:6]).astype(BF16))
     forward, mirror = normed[0], mm(reversal(SPAN), normed[1]).astype(BF16)
-    flip = reversal(256)
     for block in range(8):
-        near, far = (slice(part * 256, (part + 1) * 256) for part in (block, 7 - block))
-        turned = mm(flip, full_ref[far, :width]).astype(BF16)
-        out_ref[block % 4, block // 4] = (mm_t(forward, full_ref[near, :width]) + mm_t(mirror, turned)).astype(BF16)
+        rows = slice(block * 256, (block + 1) * 256)
+        out_ref[block % 4, block // 4] = (
+            mm_t(forward, weights_ref[0, rows]) + mm_t(mirror, weights_ref[1, rows])
+        ).astype(BF16)
 
 
 def kernel_call(body, outs, scratch, in_specs=None):
@@ -197,7 +213,7 @@
         body,
         out_shape=outs,
         scratch_shapes=scratch,
-        compiler_params=pltpu.CompilerParams(vmem_limit_bytes=18 << 20),
+        compiler_params=pltpu.CompilerParams(vmem_limit_bytes=20 << 20),
         **extra,
     )
 
@@ -243,12 +259,15 @@
     rows, features = layer_input.shape
     width, heads = w_input.shape[1], w_step.shape[1]
     wide = 128 - heads
-    place = jnp.stack([lax.axis_index(SEQ), lax.axis_index("z_bit"), lax.axis_index("core")] + [lax.axis_index(axis) for axis in ("y_lo", "y_hi", "x")])
-    first = jnp.concatenate(
-        [w_input, w_maps[:, :STATE], w_step, jnp.zeros((w_step.shape[0], wide), BF16)], 1
+    place = jnp.stack([lax.axis_index(SEQ), lax.axis_index("z_bit"), lax.axis_index("core")] + [lax.axis_index(axis) for axis in ("y_lo", "y_hi")])
+    smem = pl.BlockSpec(memory_space=pltpu.SMEM)
+    vmem = pl.BlockSpec(memory_space=pltpu.VMEM)
+    struct = jax.ShapeDtypeStruct
+    first = kernel_call(pack_kernel, struct((16, w_input.shape[0], width + 2 * STATE), BF16), [])(
+        w_input, w_maps, w_step.T
     )
     second = jnp.concatenate([w_out.T, w_gate, w_maps[:, STATE:]], 1)
-    near = copies(first, ("y_lo", "z_pair"))
+    near = lax.all_to_all(first, ("y_lo", "z_pair"), 0, 0, tiled=True)
     before = shifted(layer_input[rows - HALO :], 1)
     after = shifted(layer_input[:HALO], -1)
     extended = jnp.concatenate([before, layer_input, after])
@@ -257,11 +276,8 @@
     near, second_y, extended = together(near, second_y, extended)
     second_z = lax.all_gather(second_y, Z)
     left, right = neighbours(near)
-    blocks = around(extended, "x")
+    blocks = copies(extended, "x")
     first_pieces = (near, left, right, swapped(near), swapped(left), swapped(right))
-    smem = pl.BlockSpec(memory_space=pltpu.SMEM)
-    vmem = pl.BlockSpec(memory_space=pltpu.VMEM)
-    struct = jax.ShapeDtypeStruct
     places = 2 * width // 16
     front_small = jnp.concatenate(
         [jnp.concatenate([conv_input, conv_maps[:, :STATE]], 1)]
@@ -293,17 +309,19 @@
     second_other = swapped(second_own)
     entries = kernel_call(scan_kernel, struct((places, 16, STATE), BF16), [], [smem, vmem])(place, got)
     entry = lax.all_to_all(entries, SEQ, 0, 0, tiled=True).reshape(2 * width, STATE)
-    partial = kernel_call(
-        back_kernel,
-        struct((4, 2, SPAN, features), BF16),
-        [
-            pltpu.VMEM((2 * EXT, STATE), F32),
-            pltpu.VMEM((SPAN, width), F32),
-            pltpu.VMEM((8 * features, 2 * width + STATE), BF16),
-        ],
-        [smem] + [vmem] * 7,
-    )(
-        place, stream, second_own, second_other, conv, step, entry, back_small,
+    out_map, inner, gate, weights = kernel_call(
+        inner_kernel,
+        (
+            struct((2, SPAN, STATE), BF16),
+            struct((2, SPAN, width), F32),
+            struct((2, SPAN, width), F32),
+            struct((2, 8 * features, width), BF16),
+        ),
+        [pltpu.VMEM((2 * EXT, STATE), F32), pltpu.VMEM((8 * features, width + STATE), BF16)],
+        [smem] + [vmem] * 6,
+    )(place, stream, second_own, second_other, conv, step, back_small)
+    partial = kernel_call(out_kernel, struct((4, 2, SPAN, features), BF16), [])(
+        entry, out_map, inner, gate, weights, back_small
     )
     parts = jnp.sum(lax.all_to_all(partial, "x", 0, 0, tiled=True).astype(F32), 0)
     low = lax.axis_index("y_hi") == 0

time: 177 us -> 172 us (0.972)
  waiting for transfers between devices: 36.6 us -> 26.2 us
  local copies, waits for them, and re-layouts: 8.47 us -> 17.2 us
  starting transfers between devices: 80.5 us -> 76.8 us
    ppermute x6 -> x3, starting transfers between devices: 24.3 us -> 10.1 us  [around(): lax.ppermute(block, axis, [(place, (place + step) % count) for place in r...]
    all_to_all x0 -> x1, starting transfers between devices: none -> 13.8 us  [local(): near = lax.all_to_all(first, ('y_lo', 'z_pair'), 0, 0, tiled=True)]
    all_to_all x1, waiting for transfers between devices: 11.8 us -> 0.24 us  [local(): lax.all_to_all(entries, SEQ, 0, 0, tiled=True).reshape(2 * width, STATE)]
    all_to_all x1, starting transfers between devices: 13.9 us -> 4.29 us  [copies(): lax.all_to_all(jnp.broadcast_to(block[None], (count, *block.shape)), axis...]
    unnamed x31 -> x44, local copies, waits for them, and re-layouts: 6.33 us -> 14.6 us
    all_to_all x1, waiting for transfers between devices: 0.01 us -> 4.14 us  [copies(): lax.all_to_all(jnp.broadcast_to(block[None], (count, *block.shape)), axis...]
    ppermute x4, starting transfers between devices: 10.8 us -> 14.8 us  [swapped(): return lax.ppermute(block, 'core', [(0, 1), (1, 0)])]
    ppermute x2, starting transfers between devices: 5.03 us -> 8.63 us  [shifted(): return lax.ppermute(value, SEQ, route)]
  transfers between devices with their start and end apart: 20 -> 18, of which waited for: 8 -> 6; matrix products, arithmetic and copies ran while one was open for 1% -> 2% of each run, Pallas kernels for 3% -> 6%
where the time goes in v3:
time: 172 us; the launch traced here: 171 us
  starting transfers between devices  76.8 us (45%)
  waiting for transfers between devices  26.2 us (15%)
  blocking collectives  20.5 us (12%)
  local copies, waits for them, and re-layouts  17.2 us (10%)
  Pallas kernels  13.9 us (8%)
  between operations  13.8 us (8%)
  other arithmetic  2.17 us (1%)
    all_to_all x1, blocking collectives, local(): got = lax.all_to_all(send, SEQ, 0, 0, tiled=True)  20.5 us
    ppermute x4, starting transfers between devices, swapped(): return lax.ppermute(block, 'core', [(0, 1), (1, 0)])  14.8 us
    unnamed x44, local copies, waits for them, and re-layouts  14.6 us
    all_to_all x1, starting transfers between devices, local(): near = lax.all_to_all(first, ('y_lo', 'z_pair'), 0, 0, tiled=True)  13.8 us
    all_to_all x1, waiting for transfers between devices, local(): lax.all_to_all(partial, 'x', 0, 0, tiled=True).astype(F32)  10.1 us
    ppermute x3, starting transfers between devices, around(): lax.ppermute(block, axis, [(place, (place + step) % count) for place in r...  10.1 us
    ppermute x2, starting transfers between devices, shifted(): return lax.ppermute(value, SEQ, route)  8.63 us
    all_to_all x1, starting transfers between devices, local(): lax.all_to_all(entries, SEQ, 0, 0, tiled=True).reshape(2 * width, STATE)  5.76 us
  transfers between devices with their start and end apart: 18, of which 6 were waited for; matrix products, arithmetic and copies ran while one was open for 2% of the time, Pallas kernels for 6%

profile of v3, /device:TPU:8, one launch (start us, length us, event | category | flops | bytes accessed | tf_op | source)
XLA Modules:
  0.0 170.5 jit_solution(3926466603059503529)
XLA Ops:
  8.7 1.1 shard_map.118
  9.8 13.8 %all-to-all-start = ((bf16[16,32,768]{2,1,0:T(8,128)(2,1)}), bf16[16,32,768]{2,1,0:T(8,128)(2,1)S(1)}, u32[]{:S(2)}, u32[]{:S(2)}) async-start(bf16[16,32,768]{2,1,0:T(8,128)(2,1)} %shard_map.118), calls=%async_computation | async-start | bytes 1572864 | tf_op jit(solution)/shard_map/all_to_all | solution.py:270
  23.7 1.9 %collective-permute-start.3 = (bf16[16,256]{1,0:T(8,128)(2,1)S(1)}, bf16[16,256]{1,0:T(8,128)(2,1)S(1)}, u32[]{:S(2)}, u32[]{:S(2)}) collective-permute-start(bf16[16,256]{1,0:T(8,128)(2,1)S(1)} %get-tuple-element.36), channel_id=1, source_target_pairs={{0,8},{8,16},{16,24},{24,32},{32,40},{40,48},{48,56},{56,64},{64,7... | collective-permute-start | bytes 24584 | tf_op jit(solution)/shard_map/ppermute | solution.py:229
  25.7 4.3 %collective-permute-start.1 = (bf16[32,1152]{1,0:T(8,128)(2,1)S(1)}, bf16[32,1152]{1,0:T(8,128)(2,1)S(1)}, u32[]{:S(2)}, u32[]{:S(2)}) collective-permute-start(bf16[32,1152]{1,0:T(8,128)(2,1)S(1)} %get-tuple-element.34), channel_id=1, source_target_pairs={{0,256},{128,384},{256,0},{384,128},{1,257},{129,385},{257,1},{385... | collective-permute-start | bytes 221192 | tf_op jit(solution)/shard_map/ppermute | solution.py:246
  29.9 1.9 %collective-permute-start = (bf16[32,1152]{1,0:T(8,128)(2,1)S(1)}, bf16[32,1152]{1,0:T(8,128)(2,1)S(1)}, u32[]{:S(2)}, u32[]{:S(2)}) collective-permute-start(bf16[32,1152]{1,0:T(8,128)(2,1)S(1)} %get-tuple-element.34), channel_id=1, source_target_pairs={{0,128},{128,256},{256,384},{384,0},{1,129},{129,257},{257,385},{3... | collective-permute-start | bytes 221192 | tf_op jit(solution)/shard_map/ppermute | solution.py:246
  31.9 3.9 %collective-permute-start.2 = (bf16[32,1152]{1,0:T(8,128)(2,1)S(1)}, bf16[32,1152]{1,0:T(8,128)(2,1)S(1)}, u32[]{:S(2)}, u32[]{:S(2)}) collective-permute-start(bf16[32,1152]{1,0:T(8,128)(2,1)S(1)} %get-tuple-element.34), channel_id=1, source_target_pairs={{0,384},{128,0},{256,128},{384,256},{1,385},{129,1},{257,129},{385... | collective-permute-start | bytes 221192 | tf_op jit(solution)/shard_map/ppermute | solution.py:246
  35.8 6.7 %collective-permute-start.4 = (bf16[16,256]{1,0:T(8,128)(2,1)S(1)}, bf16[16,256]{1,0:T(8,128)(2,1)S(1)}, u32[]{:S(2)}, u32[]{:S(2)}) collective-permute-start(bf16[16,256]{1,0:T(8,128)(2,1)S(1)} %get-tuple-element.35), channel_id=1, source_target_pairs={{8,0},{16,8},{24,16},{32,24},{40,32},{48,40},{56,48},{64,56},{72,6... | collective-permute-start | bytes 24584 | tf_op jit(solution)/shard_map/ppermute | solution.py:229
  42.5 1.3 collective-permute-done.4
  43.9 5.0 %collective-permute-start.5 = (bf16[160,256]{1,0:T(8,128)(2,1)S(1)}, bf16[160,256]{1,0:T(8,128)(2,1)S(1)}, u32[]{:S(2)}, u32[]{:S(2)}) collective-permute-start(bf16[160,256]{1,0:T(8,128)(2,1)S(1)} %constant_dynamic-update-slice_fusion), channel_id=1, source_target_pairs={{0,4},{4,0},{1,5},{5,1},{2,6},{6,2},{3,7},{7,3},{8,12},{12,8},{9,1... | collective-permute-start | bytes 245768 | tf_op jit(solution)/shard_map/ppermute | solution.py:274
  49.7 4.6 %collective-permute-done.5 = bf16[160,256]{1,0:T(8,128)(2,1)S(1)} collective-permute-done((bf16[160,256]{1,0:T(8,128)(2,1)S(1)}, bf16[160,256]{1,0:T(8,128)(2,1)S(1)}, u32[]{:S(2)}, u32[]{:S(2)}) %collective-permute-start.5) | collective-permute-done | bytes 81952 | tf_op jit(solution)/shard_map/ppermute | solution.py:274
  55.2 3.1 %collective-permute-start.7 = (bf16[8,32,768]{2,1,0:T(8,128)(2,1)S(1)}, bf16[8,32,768]{2,1,0:T(8,128)(2,1)S(1)}, u32[]{:S(2)}, u32[]{:S(2)}) collective-permute-start(bf16[8,32,768]{2,1,0:T(8,128)(2,1)S(1)} %get-tuple-element.31), channel_id=1, source_target_pairs={{0,112},{16,0},{32,16},{48,32},{64,48},{80,64},{96,80},{112,96},{1... | collective-permute-start | bytes 1179656 | tf_op jit(solution)/shard_map/ppermute | solution.py:239
  58.2 2.8 %collective-permute-start.6 = (bf16[8,32,768]{2,1,0:T(8,128)(2,1)}, bf16[8,32,768]{2,1,0:T(8,128)(2,1)S(1)}, u32[]{:S(2)}, u32[]{:S(2)}) collective-permute-start(bf16[8,32,768]{2,1,0:T(8,128)(2,1)} %get-tuple-element.32), channel_id=1, source_target_pairs={{0,16},{16,32},{32,48},{48,64},{64,80},{80,96},{96,112},{112,0},{1... | collective-permute-start | bytes 1179656 | tf_op jit(solution)/shard_map/ppermute | solution.py:238
  61.0 6.5 %collective-permute-start.8 = (bf16[16,32,768]{2,1,0:T(8,128)(2,1)S(1)}, bf16[16,32,768]{2,1,0:T(8,128)(2,1)S(1)}, u32[]{:S(2)}, u32[]{:S(2)}) collective-permute-start(bf16[16,32,768]{2,1,0:T(8,128)(2,1)S(1)} %all-to-all-done.n0), channel_id=1, source_target_pairs={{0,8},{8,0},{1,9},{9,1},{2,10},{10,2},{3,11},{11,3},{4,12},{12,4},... | collective-permute-start | bytes 2359304 | tf_op jit(solution)/shard_map/ppermute | solution.py:233
  68.4 4.3 %all-to-all-start.1 = ((bf16[4,2,160,256]{3,2,1,0:T(8,128)(2,1)}), bf16[4,2,160,256]{3,2,1,0:T(8,128)(2,1)S(1)}, u32[]{:S(2)}, u32[]{:S(2)}) async-start(bf16[4,2,160,256]{3,2,1,0:T(8,128)(2,1)} %broadcast_in_dim.21), calls=%async_computation.1 | async-start | bytes 1310720 | tf_op jit(solution)/shard_map/all_to_all | solution.py:223
  72.7 1.9 %collective-permute-start.10 = (bf16[8,32,768]{2,1,0:T(8,128)(2,1)S(1)}, bf16[8,32,768]{2,1,0:T(8,128)(2,1)S(1)}, u32[]{:S(2)}, u32[]{:S(2)}) collective-permute-start(bf16[8,32,768]{2,1,0:T(8,128)(2,1)S(1)} %collective-permute-done.7.r0), channel_id=1, source_target_pairs={{0,8},{8,0},{1,9},{9,1},{2,10},{10,2},{3,11},{11,3},{4,12},{12,4},... | collective-permute-start | bytes 1179656 | tf_op jit(solution)/shard_map/ppermute | solution.py:233
  74.6 4.2 %collective-permute-start.9 = (bf16[8,32,768]{2,1,0:T(8,128)(2,1)S(1)}, bf16[8,32,768]{2,1,0:T(8,128)(2,1)}, u32[]{:S(2)}, u32[]{:S(2)}) collective-permute-start(bf16[8,32,768]{2,1,0:T(8,128)(2,1)S(1)} %collective-permute-done.6.l0), channel_id=1, source_target_pairs={{0,8},{8,0},{1,9},{9,1},{2,10},{10,2},{3,11},{11,3},{4,12},{12,4},... | collective-permute-start | bytes 1179656 | tf_op jit(solution)/shard_map/ppermute | solution.py:233
  79.6 4.1 %all-to-all-done.1.x_ref = bf16[4,2,160,256]{3,2,1,0:T(8,128)(2,1)S(1)} async-done(((bf16[4,2,160,256]{3,2,1,0:T(8,128)(2,1)}), bf16[4,2,160,256]{3,2,1,0:T(8,128)(2,1)S(1)}, u32[]{:S(2)}, u32[]{:S(2)}) %all-to-all-start.1) | async-done | bytes 655392 | tf_op jit(solution)/shard_map/all_to_all | solution.py:223
  84.5 4.4 %shard_map.119 = (bf16[64,24,128]{2,1,0:T(8,128)(2,1)S(1)}, bf16[288,2048]{1,0:T(8,128)(2,1)S(1)}, bf16[2,128,640]{2,1,0:T(8,128)(2,1)S(1)}, f32[2,128,128]{2,1,0:T(8,128)S(1)}) custom-call(s32[5]{0:T(128)S(1)} %stack.47.place_ref, bf16[4,2,160,256]{3,2,1,0:T(8,128)(2,1)S(1)} %all-to-all-done.1.x_ref, bf16[16,32,768]{2,1,0:T(8,128)(2,1)S(1)} %all-to-all-done.n0, ...), custom_call_target="tpu_custom_call" | custom-call | tf_op jit(solution)/shard_map/pallas_call | solution.py:294
  90.6 20.5 %all_to_all.25.got_ref = bf16[64,24,128]{2,1,0:T(8,128)(2,1)S(1)} all-to-all(bf16[64,24,128]{2,1,0:T(8,128)(2,1)S(1)} %get-tuple-element.21), channel_id=1, replica_groups=mesh['y_lo'=4,'z_pair'=4,'z_bit'=2,'core'=2,'y_hi'=2,'x'=4] {'y_lo','z_p..., dimensions={0} | all-to-all | bytes 786432 | tf_op jit(solution)/shard_map/all_to_all | solution.py:307
  111.1 2.2 %collective-permute-start.11 = (bf16[8,4,32,1152]{3,2,1,0:T(8,128)(2,1)}, bf16[8,4,32,1152]{3,2,1,0:T(8,128)(2,1)S(1)}, u32[]{:S(2)}, u32[]{:S(2)}) collective-permute-start(bf16[8,4,32,1152]{3,2,1,0:T(8,128)(2,1)} %bitcast.24), channel_id=1, source_target_pairs={{0,8},{8,0},{1,9},{9,1},{2,10},{10,2},{3,11},{11,3},{4,12},{12,4},... | collective-permute-start | bytes 7077896 | tf_op jit(solution)/shard_map/ppermute | solution.py:233
  113.4 1.6 shard_map.120
  114.9 5.8 %all-to-all-start.3 = ((bf16[64,16,128]{2,1,0:T(8,128)(2,1)}), bf16[64,16,128]{2,1,0:T(8,128)(2,1)S(1)}, u32[]{:S(2)}, u32[]{:S(2)}) async-start(bf16[64,16,128]{2,1,0:T(8,128)(2,1)} %shard_map.120), calls=%async_computation.3 | async-start | bytes 524288 | tf_op jit(solution)/shard_map/all_to_all | solution.py:311
  121.5 1.7 copy-done.2
  123.2 1.3 copy-done.4
  125.5 4.2 %shard_map.121 = (bf16[2,128,128]{2,1,0:T(8,128)(2,1)S(1)}, f32[2,128,512]{2,1,0:T(8,128)S(1)}, f32[2,128,512]{2,1,0:T(8,128)S(1)}, bf16[2,2048,512]{2,1,0:T(8,128)(2,1)S(1)}) custom-call(s32[5]{0:T(128)S(1)} %stack.47.place_ref, bf16[288,2048]{1,0:T(8,128)(2,1)S(1)} %copy-done.4, bf16[8,4,32,1152]{3,2,1,0:T(8,128)(2,1)S(1)} %bitcast.25, ...), custom_call_target="tpu_custom_call" | custom-call | tf_op jit(solution)/shard_map/pallas_call | solution.py:312
  129.7 1.9 %copy-done = bf16[2,2048,512]{2,1,0:T(8,128)(2,1)} copy-done((bf16[2,2048,512]{2,1,0:T(8,128)(2,1)}, bf16[2,2048,512]{2,1,0:T(8,128)(2,1)S(1)}, u32[]{:S(2)}) %copy-start) | copy-done | bytes 4194328
  132.7 2.2 %copy-done.1 = bf16[2,2048,512]{2,1,0:T(8,128)(2,1)S(1)} copy-done((bf16[2,2048,512]{2,1,0:T(8,128)(2,1)S(1)}, bf16[2,2048,512]{2,1,0:T(8,128)(2,1)}, u32[]{:S(2)}) %copy-start.1) | copy-done | bytes 4194328
  135.9 2.7 %shard_map.122 = bf16[4,2,128,256]{3,2,1,0:T(8,128)(2,1)} custom-call(bf16[1024,128]{1,0:T(8,128)(2,1)S(1)} %bitcast.26, bf16[2,128,128]{2,1,0:T(8,128)(2,1)S(1)} %get-tuple-element.27.map_ref, f32[2,128,512]{2,1,0:T(8,128)S(1)} %get-tuple-element.28.inner_ref, f32[2,128,512]{2,1,0:T(8,128)S(1)} %copy-done.6, bf16[2,2048,512]{2,1,0:T(8,128)(2,1)S(1)} %copy-done.1, ...), custom_call_target="tpu_custom_call" | custom-call | tf_op jit(solution)/shard_map/pallas_call | solution.py:323
  138.6 3.5 %all-to-all-start.4 = ((bf16[4,2,128,256]{3,2,1,0:T(8,128)(2,1)}), bf16[4,2,128,256]{3,2,1,0:T(8,128)(2,1)S(1)}, u32[]{:S(2)}, u32[]{:S(2)}) async-start(bf16[4,2,128,256]{3,2,1,0:T(8,128)(2,1)} %shard_map.122), calls=%async_computation.4 | async-start | bytes 1048576 | tf_op jit(solution)/shard_map/all_to_all | solution.py:326
  142.0 10.1 %all-to-all-done.4 = bf16[4,2,128,256]{3,2,1,0:T(8,128)(2,1)S(1)} async-done(((bf16[4,2,128,256]{3,2,1,0:T(8,128)(2,1)}), bf16[4,2,128,256]{3,2,1,0:T(8,128)(2,1)S(1)}, u32[]{:S(2)}, u32[]{:S(2)}) %all-to-all-start.4) | async-done | bytes 524320 | tf_op jit(solution)/shard_map/all_to_all | solution.py:326
  152.3 5.0 %collective-permute-start.12 = (bf16[128,256]{1,0:T(8,128)(2,1)S(1)}, bf16[128,256]{1,0:T(8,128)(2,1)S(1)}, u32[]{:S(2)}, u32[]{:S(2)}) collective-permute-start(bf16[128,256]{1,0:T(8,128)(2,1)S(1)} %fusion.1), channel_id=1, source_target_pairs={{0,4},{4,0},{1,5},{5,1},{2,6},{6,2},{3,7},{7,3},{8,12},{12,8},{9,1... | collective-permute-start | bytes 196616 | tf_op jit(solution)/shard_map/ppermute | solution.py:329
  157.3 5.7 %collective-permute-done.12 = bf16[128,256]{1,0:T(8,128)(2,1)S(1)} collective-permute-done((bf16[128,256]{1,0:T(8,128)(2,1)S(1)}, bf16[128,256]{1,0:T(8,128)(2,1)S(1)}, u32[]{:S(2)}, u32[]{:S(2)}) %collective-permute-start.12) | collective-permute-done | bytes 65568 | tf_op jit(solution)/shard_map/ppermute | solution.py:329
  (78 shorter events, 12.6 us)
Async XLA Ops:
  8.7 15.0 %copy-start.13 = (bf16[128,256]{1,0:T(8,128)(2,1)S(1)}, bf16[128,256]{1,0:T(8,128)(2,1)}, u32[]{:S(2)}) copy-start(bf16[128,256]{1,0:T(8,128)(2,1)} %param.12) | copy-start | bytes 196612
  8.7 16.9 %slice-start = ((bf16[32,256]{1,0:T(8,128)(2,1)}), bf16[32,128]{1,0:T(8,128)(2,1)S(1)}, s32[]{:S(2)}) async-start(bf16[32,256]{1,0:T(8,128)(2,1)} %maps_ref.1), calls=%async_computation.6 | async-start | bytes 16384 | tf_op jit(solution)/shard_map/slice | solution.py:269
  8.7 16.9 %copy-start.14 = (bf16[32,512]{1,0:T(8,128)(2,1)S(1)}, bf16[32,512]{1,0:T(8,128)(2,1)}, u32[]{:S(2)}) copy-start(bf16[32,512]{1,0:T(8,128)(2,1)} %param.14) | copy-start | bytes 98308
  8.7 16.9 %copy-start.15 = (bf16[512,32]{0,1:T(8,128)(2,1)S(1)}, bf16[512,32]{0,1:T(8,128)(2,1)}, u32[]{:S(2)}) copy-start(bf16[512,32]{0,1:T(8,128)(2,1)} %param.23) | copy-start | bytes 98308
  9.8 44.5 %all-to-all-start = ((bf16[16,32,768]{2,1,0:T(8,128)(2,1)}), bf16[16,32,768]{2,1,0:T(8,128)(2,1)S(1)}, u32[]{:S(2)}, u32[]{:S(2)}) async-start(bf16[16,32,768]{2,1,0:T(8,128)(2,1)} %shard_map.118), calls=%async_computation | async-start | bytes 1572864 | tf_op jit(solution)/shard_map/all_to_all | solution.py:270
  23.6 87.5 %all-gather.3.cloned.1.call-start = ((), (), s32[]{:S(2)}) async-start(), calls=%async_computation.5 | async-start | bytes 2654208 | tf_op jit(solution)/shard_map/all_gather | solution.py:277
  23.7 18.8 %collective-permute-start.3 = (bf16[16,256]{1,0:T(8,128)(2,1)S(1)}, bf16[16,256]{1,0:T(8,128)(2,1)S(1)}, u32[]{:S(2)}, u32[]{:S(2)}) collective-permute-start(bf16[16,256]{1,0:T(8,128)(2,1)S(1)} %get-tuple-element.36), channel_id=1, source_target_pairs={{0,8},{8,16},{16,24},{24,32},{32,40},{40,48},{48,56},{56,64},{64,7... | collective-permute-start | bytes 24584 | tf_op jit(solution)/shard_map/ppermute | solution.py:229
  25.7 23.2 %collective-permute-start.1 = (bf16[32,1152]{1,0:T(8,128)(2,1)S(1)}, bf16[32,1152]{1,0:T(8,128)(2,1)S(1)}, u32[]{:S(2)}, u32[]{:S(2)}) collective-permute-start(bf16[32,1152]{1,0:T(8,128)(2,1)S(1)} %get-tuple-element.34), channel_id=1, source_target_pairs={{0,256},{128,384},{256,0},{384,128},{1,257},{129,385},{257,1},{385... | collective-permute-start | bytes 221192 | tf_op jit(solution)/shard_map/ppermute | solution.py:246
  29.9 19.0 %collective-permute-start = (bf16[32,1152]{1,0:T(8,128)(2,1)S(1)}, bf16[32,1152]{1,0:T(8,128)(2,1)S(1)}, u32[]{:S(2)}, u32[]{:S(2)}) collective-permute-start(bf16[32,1152]{1,0:T(8,128)(2,1)S(1)} %get-tuple-element.34), channel_id=1, source_target_pairs={{0,128},{128,256},{256,384},{384,0},{1,129},{129,257},{257,385},{3... | collective-permute-start | bytes 221192 | tf_op jit(solution)/shard_map/ppermute | solution.py:246
  31.9 17.1 %collective-permute-start.2 = (bf16[32,1152]{1,0:T(8,128)(2,1)S(1)}, bf16[32,1152]{1,0:T(8,128)(2,1)S(1)}, u32[]{:S(2)}, u32[]{:S(2)}) collective-permute-start(bf16[32,1152]{1,0:T(8,128)(2,1)S(1)} %get-tuple-element.34), channel_id=1, source_target_pairs={{0,384},{128,0},{256,128},{384,256},{1,385},{129,1},{257,129},{385... | collective-permute-start | bytes 221192 | tf_op jit(solution)/shard_map/ppermute | solution.py:246
  35.8 8.1 %collective-permute-start.4 = (bf16[16,256]{1,0:T(8,128)(2,1)S(1)}, bf16[16,256]{1,0:T(8,128)(2,1)S(1)}, u32[]{:S(2)}, u32[]{:S(2)}) collective-permute-start(bf16[16,256]{1,0:T(8,128)(2,1)S(1)} %get-tuple-element.35), channel_id=1, source_target_pairs={{8,0},{16,8},{24,16},{32,24},{40,32},{48,40},{56,48},{64,56},{72,6... | collective-permute-start | bytes 24584 | tf_op jit(solution)/shard_map/ppermute | solution.py:229
  43.9 10.4 %collective-permute-start.5 = (bf16[160,256]{1,0:T(8,128)(2,1)S(1)}, bf16[160,256]{1,0:T(8,128)(2,1)S(1)}, u32[]{:S(2)}, u32[]{:S(2)}) collective-permute-start(bf16[160,256]{1,0:T(8,128)(2,1)S(1)} %constant_dynamic-update-slice_fusion), channel_id=1, source_target_pairs={{0,4},{4,0},{1,5},{5,1},{2,6},{6,2},{3,7},{7,3},{8,12},{12,8},{9,1... | collective-permute-start | bytes 245768 | tf_op jit(solution)/shard_map/ppermute | solution.py:274
  48.9 29.9 %copy-start.20 = (f32[8]{0:T(128)S(1)}, f32[8]{0:T(128)}, u32[]{:S(2)}) copy-start(f32[8]{0:T(128)} %param.17) | copy-start | bytes 100
  48.9 29.9 %copy-start.19 = (f32[8]{0:T(128)S(1)}, f32[8]{0:T(128)}, u32[]{:S(2)}) copy-start(f32[8]{0:T(128)} %param.18) | copy-start | bytes 100
  48.9 30.0 %copy-start.17 = (f32[4,256]{1,0:T(4,128)S(1)}, f32[4,256]{1,0:T(4,128)}, u32[]{:S(2)}) copy-start(f32[4,256]{1,0:T(4,128)} %param.21) | copy-start | bytes 12292
  49.7 29.2 %copy-start.16 = (f32[4,512]{1,0:T(4,128)S(1)}, f32[4,512]{1,0:T(4,128)}, u32[]{:S(2)}) copy-start(f32[4,512]{1,0:T(4,128)} %param.20) | copy-start | bytes 24580
  55.2 17.5 %collective-permute-start.7 = (bf16[8,32,768]{2,1,0:T(8,128)(2,1)S(1)}, bf16[8,32,768]{2,1,0:T(8,128)(2,1)S(1)}, u32[]{:S(2)}, u32[]{:S(2)}) collective-permute-start(bf16[8,32,768]{2,1,0:T(8,128)(2,1)S(1)} %get-tuple-element.31), channel_id=1, source_target_pairs={{0,112},{16,0},{32,16},{48,32},{64,48},{80,64},{96,80},{112,96},{1... | collective-permute-start | bytes 1179656 | tf_op jit(solution)/shard_map/ppermute | solution.py:239
  58.2 16.4 %collective-permute-start.6 = (bf16[8,32,768]{2,1,0:T(8,128)(2,1)}, bf16[8,32,768]{2,1,0:T(8,128)(2,1)S(1)}, u32[]{:S(2)}, u32[]{:S(2)}) collective-permute-start(bf16[8,32,768]{2,1,0:T(8,128)(2,1)} %get-tuple-element.32), channel_id=1, source_target_pairs={{0,16},{16,32},{32,48},{48,64},{64,80},{80,96},{96,112},{112,0},{1... | collective-permute-start | bytes 1179656 | tf_op jit(solution)/shard_map/ppermute | solution.py:238
  61.0 22.7 %collective-permute-start.8 = (bf16[16,32,768]{2,1,0:T(8,128)(2,1)S(1)}, bf16[16,32,768]{2,1,0:T(8,128)(2,1)S(1)}, u32[]{:S(2)}, u32[]{:S(2)}) collective-permute-start(bf16[16,32,768]{2,1,0:T(8,128)(2,1)S(1)} %all-to-all-done.n0), channel_id=1, source_target_pairs={{0,8},{8,0},{1,9},{9,1},{2,10},{10,2},{3,11},{11,3},{4,12},{12,4},... | collective-permute-start | bytes 2359304 | tf_op jit(solution)/shard_map/ppermute | solution.py:233
  68.4 15.4 %all-to-all-start.1 = ((bf16[4,2,160,256]{3,2,1,0:T(8,128)(2,1)}), bf16[4,2,160,256]{3,2,1,0:T(8,128)(2,1)S(1)}, u32[]{:S(2)}, u32[]{:S(2)}) async-start(bf16[4,2,160,256]{3,2,1,0:T(8,128)(2,1)} %broadcast_in_dim.21), calls=%async_computation.1 | async-start | bytes 1310720 | tf_op jit(solution)/shard_map/all_to_all | solution.py:223
  72.7 11.1 %collective-permute-start.10 = (bf16[8,32,768]{2,1,0:T(8,128)(2,1)S(1)}, bf16[8,32,768]{2,1,0:T(8,128)(2,1)S(1)}, u32[]{:S(2)}, u32[]{:S(2)}) collective-permute-start(bf16[8,32,768]{2,1,0:T(8,128)(2,1)S(1)} %collective-permute-done.7.r0), channel_id=1, source_target_pairs={{0,8},{8,0},{1,9},{9,1},{2,10},{10,2},{3,11},{11,3},{4,12},{12,4},... | collective-permute-start | bytes 1179656 | tf_op jit(solution)/shard_map/ppermute | solution.py:233
  74.6 9.1 %collective-permute-start.9 = (bf16[8,32,768]{2,1,0:T(8,128)(2,1)S(1)}, bf16[8,32,768]{2,1,0:T(8,128)(2,1)}, u32[]{:S(2)}, u32[]{:S(2)}) collective-permute-start(bf16[8,32,768]{2,1,0:T(8,128)(2,1)S(1)} %collective-permute-done.6.l0), channel_id=1, source_target_pairs={{0,8},{8,0},{1,9},{9,1},{2,10},{10,2},{3,11},{11,3},{4,12},{12,4},... | collective-permute-start | bytes 1179656 | tf_op jit(solution)/shard_map/ppermute | solution.py:233
  79.0 42.5 %copy-start.18 = (f32[512]{0:T(512)S(1)}, f32[512]{0:T(512)}, u32[]{:S(2)}) copy-start(f32[512]{0:T(512)} %param.22) | copy-start | bytes 6148
  111.1 10.4 %collective-permute-start.11 = (bf16[8,4,32,1152]{3,2,1,0:T(8,128)(2,1)}, bf16[8,4,32,1152]{3,2,1,0:T(8,128)(2,1)S(1)}, u32[]{:S(2)}, u32[]{:S(2)}) collective-permute-start(bf16[8,4,32,1152]{3,2,1,0:T(8,128)(2,1)} %bitcast.24), channel_id=1, source_target_pairs={{0,8},{8,0},{1,9},{9,1},{2,10},{10,2},{3,11},{11,3},{4,12},{12,4},... | collective-permute-start | bytes 7077896 | tf_op jit(solution)/shard_map/ppermute | solution.py:233
  114.9 17.7 %all-to-all-start.3 = ((bf16[64,16,128]{2,1,0:T(8,128)(2,1)}), bf16[64,16,128]{2,1,0:T(8,128)(2,1)S(1)}, u32[]{:S(2)}, u32[]{:S(2)}) async-start(bf16[64,16,128]{2,1,0:T(8,128)(2,1)} %shard_map.120), calls=%async_computation.3 | async-start | bytes 524288 | tf_op jit(solution)/shard_map/all_to_all | solution.py:311
  121.5 1.7 copy-start.2
  123.2 1.3 copy-start.4
  129.7 2.0 %copy-start = (bf16[2,2048,512]{2,1,0:T(8,128)(2,1)}, bf16[2,2048,512]{2,1,0:T(8,128)(2,1)S(1)}, u32[]{:S(2)}) copy-start(bf16[2,2048,512]{2,1,0:T(8,128)(2,1)S(1)} %get-tuple-element.30.weights_ref) | copy-start | bytes 12582916
  132.7 2.2 %copy-start.1 = (bf16[2,2048,512]{2,1,0:T(8,128)(2,1)S(1)}, bf16[2,2048,512]{2,1,0:T(8,128)(2,1)}, u32[]{:S(2)}) copy-start(bf16[2,2048,512]{2,1,0:T(8,128)(2,1)} %copy-done) | copy-start | bytes 12582916
  134.8 1.0 copy-start.6
  138.6 13.6 %all-to-all-start.4 = ((bf16[4,2,128,256]{3,2,1,0:T(8,128)(2,1)}), bf16[4,2,128,256]{3,2,1,0:T(8,128)(2,1)S(1)}, u32[]{:S(2)}, u32[]{:S(2)}) async-start(bf16[4,2,128,256]{3,2,1,0:T(8,128)(2,1)} %shard_map.122), calls=%async_computation.4 | async-start | bytes 1048576 | tf_op jit(solution)/shard_map/all_to_all | solution.py:326
  152.3 10.8 %collective-permute-start.12 = (bf16[128,256]{1,0:T(8,128)(2,1)S(1)}, bf16[128,256]{1,0:T(8,128)(2,1)S(1)}, u32[]{:S(2)}, u32[]{:S(2)}) collective-permute-start(bf16[128,256]{1,0:T(8,128)(2,1)S(1)} %fusion.1), channel_id=1, source_target_pairs={{0,4},{4,0},{1,5},{5,1},{2,6},{6,2},{3,7},{7,3},{8,12},{12,8},{9,1... | collective-permute-start | bytes 196616 | tf_op jit(solution)/shard_map/ppermute | solution.py:329
  (8 other events, 6.4 us)
Sparse Core Ops, SparseCore 0:
  54.5 44.8 all-gather.2

commit v4 on v3

--- a/solution.py
+++ b/solution.py
@@ -12,9 +12,9 @@
 STATE = 128
 HALO = 16
 EXT = SPAN + HALO
-AXES = ("y_lo", "z_pair", "z_bit", "core", "y_hi", "x")
-SEQ = ("y_lo", "z_pair", "z_bit", "core")
-Z = ("z_pair", "z_bit")
+AXES = ("y_pair", "y_bit", "z", "core", "y_hi", "x")
+SEQ = ("y_pair", "y_bit", "z", "core")
+Y_LO = ("y_pair", "y_bit")
 HEAD = ("y_hi", "x")
 F32 = jnp.float32
 BF16 = jnp.bfloat16
@@ -70,13 +70,12 @@
 def assemble(place_ref, pieces, full_ref):
     bit, core = place_ref[1], place_ref[2]
     for side in range(2):
-        near, left, right = pieces[3 * side : 3 * side + 3]
+        near, far = pieces[2 * side : 2 * side + 2]
         column = core + side - 2 * core * side
         for block in range(16):
-            far = left.at[block] if block < 8 else right.at[block - 8]
-            start = 128 * block + 32 * column
-            full_ref[pl.ds(pl.multiple_of(start + 64 * bit, 32), 32)] = near[block]
-            full_ref[pl.ds(pl.multiple_of(start + 64 * (1 - bit), 32), 32)] = far[...]
+            start = 1024 * (block // 8) + 64 * (block % 8) + 32 * column
+            full_ref[pl.ds(pl.multiple_of(start + 512 * bit, 32), 32)] = near[block]
+            full_ref[pl.ds(pl.multiple_of(start + 512 * (1 - bit), 32), 32)] = far[block]
 
 
 def pack_kernel(input_ref, maps_ref, step_ref, out_ref):
@@ -88,10 +87,10 @@
 
 
 def front_kernel(
-    place_ref, x_ref, n0, l0, r0, n1, l1, r1, small_ref,
+    place_ref, x_ref, n0, f0, n1, f1, small_ref,
     send_ref, stream_ref, conv_ref, step_ref, rows_ref, full_ref,
 ):
-    assemble(place_ref, (n0, l0, r0, n1, l1, r1), full_ref)
+    assemble(place_ref, (n0, f0, n1, f1), full_ref)
     y_hi = place_ref[4]
     flip_rows, flip_columns = reversal(EXT), reversal(256)
     for step in range(4):
@@ -146,20 +145,24 @@
     lax.fori_loop(0, blocks, one, jnp.zeros((16, STATE), F32), unroll=4)
 
 
+def order(place_ref, pieces, columns, full_ref):
+    core, y_lo = place_ref[2], place_ref[3]
+    for side, ref in enumerate(pieces):
+        column = core + side - 2 * core * side
+        for step in range(4):
+            y = (y_lo + 4 - step) % 4
+            for z in range(8):
+                start = 512 * y + 64 * z + 32 * column
+                full_ref[pl.ds(pl.multiple_of(start, 32), 32)] = ref[z, step, :, columns]
+
+
 def inner_kernel(
     place_ref, stream_ref, own_ref, other_ref, conv_ref, step_ref, small_ref,
     map_ref, inner_ref, gate_ref, weights_ref, rows_ref, full_ref,
 ):
-    core, y_lo = place_ref[2], place_ref[3]
     width = inner_ref.shape[2]
-    for side, ref in enumerate((own_ref, other_ref)):
-        column = core + side - 2 * core * side
-        for step in range(4):
-            y = (y_lo + 4 - step) % 4
-            for z in range(8):
-                start = pl.ds(pl.multiple_of(512 * y + 64 * z + 32 * column, 32), 32)
-                weights_ref[0, start] = ref[z, step, :, :width]
-                full_ref[start] = ref[z, step, :, width:]
+    order(place_ref, (own_ref, other_ref), slice(0, width), weights_ref)
+    order(place_ref, (own_ref, other_ref), slice(width, width + width + STATE), full_ref)
     proj = mm(stream_ref[...], full_ref[...])
     taps, log_rate = small_ref[:CONV, :STATE], small_ref[6:7, :128]
     rows_ref[...] = proj[:, width:].astype(BF16).astype(F32)
@@ -185,35 +188,46 @@
             inner_ref[branch, :, channels] = mm(weights, x_head) + small_ref[4:5, channels] * x_head.astype(F32)
         inner_ref[branch] = inner_ref[branch] * gate
         gate_ref[branch] = spread(jnp.exp(cum), width) * gate
-    flip = reversal(256)
-    for block in range(8):
-        near, far = (slice(part * 256, (part + 1) * 256) for part in (block, 7 - block))
-        weights_ref[1, near] = mm(flip, weights_ref[0, far]).astype(BF16)
-
-
-def out_kernel(entry_ref, map_ref, inner_ref, gate_ref, weights_ref, small_ref, out_ref):
+
+
+def out_kernel(
+    entry_ref, map_ref, inner_in, gate_in, weights_in, small_ref, out_ref, inner_ref, gate_ref, weights_ref, sems
+):
+    inner_copy, gate_copy, weights_copy = (
+        pltpu.make_async_copy(source, target, sems.at[place])
+        for place, (source, target) in enumerate(
+            ((inner_in, inner_ref), (gate_in, gate_ref), (weights_in, weights_ref))
+        )
+    )
+    for copy in (inner_copy, gate_copy, weights_copy):
+        copy.start()
     width = inner_ref.shape[2]
+    carried_in = [
+        mm_t(map_ref[branch], entry_ref[branch * width : (branch + 1) * width]) for branch in range(2)
+    ]
+    inner_copy.wait()
+    gate_copy.wait()
     normed = []
-    for branch in range(2):
-        carried = mm_t(map_ref[branch], entry_ref[branch * width : (branch + 1) * width])
+    for branch, carried in enumerate(carried_in):
         gated = inner_ref[branch] + carried * gate_ref[branch]
         square = jnp.mean(gated * gated, axis=-1, keepdims=True)
         normed.append((gated * lax.rsqrt(square + 1e-05) * small_ref[5:6]).astype(BF16))
     forward, mirror = normed[0], mm(reversal(SPAN), normed[1]).astype(BF16)
+    weights_copy.wait()
+    flip = reversal(256)
     for block in range(8):
-        rows = slice(block * 256, (block + 1) * 256)
-        out_ref[block % 4, block // 4] = (
-            mm_t(forward, weights_ref[0, rows]) + mm_t(mirror, weights_ref[1, rows])
-        ).astype(BF16)
-
-
-def kernel_call(body, outs, scratch, in_specs=None):
+        near, far = (slice(part * 256, (part + 1) * 256) for part in (block, 7 - block))
+        turned = mm(flip, weights_ref[far]).astype(BF16)
+        out_ref[block % 4, block // 4] = (mm_t(forward, weights_ref[near]) + mm_t(mirror, turned)).astype(BF16)
+
+
+def kernel_call(body, outs, scratch, in_specs=None, limit=20):
     extra = {} if in_specs is None else {"in_specs": in_specs}
     return pl.pallas_call(
         body,
         out_shape=outs,
         scratch_shapes=scratch,
-        compiler_params=pltpu.CompilerParams(vmem_limit_bytes=20 << 20),
+        compiler_params=pltpu.CompilerParams(vmem_limit_bytes=limit << 20),
         **extra,
     )
 
@@ -231,13 +245,6 @@
 
 def swapped(block):
     return lax.ppermute(block, "core", [(0, 1), (1, 0)])
-
-
-def neighbours(near):
-    count, half = lax.axis_size(Z), near.shape[0] // 2
-    left = lax.ppermute(near[:half], Z, [(z, (z + 1) % count) for z in range(count)])
-    right = lax.ppermute(near[half:], Z, [(z, (z - 1) % count) for z in range(count)])
-    return left, right
 
 
 def around(block, axis):
@@ -259,7 +266,7 @@
     rows, features = layer_input.shape
     width, heads = w_input.shape[1], w_step.shape[1]
     wide = 128 - heads
-    place = jnp.stack([lax.axis_index(SEQ), lax.axis_index("z_bit"), lax.axis_index("core")] + [lax.axis_index(axis) for axis in ("y_lo", "y_hi")])
+    place = jnp.stack([lax.axis_index(SEQ), lax.axis_index("y_bit"), lax.axis_index("core")] + [lax.axis_index(axis) for axis in (Y_LO, "y_hi")])
     smem = pl.BlockSpec(memory_space=pltpu.SMEM)
     vmem = pl.BlockSpec(memory_space=pltpu.VMEM)
     struct = jax.ShapeDtypeStruct
@@ -267,17 +274,18 @@
         w_input, w_maps, w_step.T
     )
     second = jnp.concatenate([w_out.T, w_gate, w_maps[:, STATE:]], 1)
-    near = lax.all_to_all(first, ("y_lo", "z_pair"), 0, 0, tiled=True)
+    near = lax.all_to_all(first, ("y_pair", "z"), 0, 0, tiled=True)
     before = shifted(layer_input[rows - HALO :], 1)
     after = shifted(layer_input[:HALO], -1)
     extended = jnp.concatenate([before, layer_input, after])
     extended = jnp.stack([extended, lax.ppermute(extended, "y_hi", [(0, 1), (1, 0)])])
-    second_y = around(second, "y_lo")
+    second_y = around(second, Y_LO)
     near, second_y, extended = together(near, second_y, extended)
-    second_z = lax.all_gather(second_y, Z)
-    left, right = neighbours(near)
+    second_z = lax.all_gather(second_y, "z")
+    far = lax.ppermute(near, "y_bit", [(0, 1), (1, 0)])
     blocks = copies(extended, "x")
-    first_pieces = (near, left, right, swapped(near), swapped(left), swapped(right))
+    far, blocks = together(far, blocks)
+    first_pieces = (near, far, swapped(near), swapped(far))
     places = 2 * width // 16
     front_small = jnp.concatenate(
         [jnp.concatenate([conv_input, conv_maps[:, :STATE]], 1)]
@@ -300,7 +308,7 @@
             struct((2, SPAN, 128), F32),
         ),
         [pltpu.VMEM((2 * EXT, width + STATE), F32), pltpu.VMEM((8 * features, width + 2 * STATE), BF16)],
-        [smem] + [vmem] * 8,
+        [smem] + [vmem] * 6,
     )(
         place, blocks, *first_pieces, front_small,
     )
@@ -315,14 +323,25 @@
             struct((2, SPAN, STATE), BF16),
             struct((2, SPAN, width), F32),
             struct((2, SPAN, width), F32),
-            struct((2, 8 * features, width), BF16),
+            struct((8 * features, width), BF16),
         ),
         [pltpu.VMEM((2 * EXT, STATE), F32), pltpu.VMEM((8 * features, width + STATE), BF16)],
         [smem] + [vmem] * 6,
+        60,
     )(place, stream, second_own, second_other, conv, step, back_small)
-    partial = kernel_call(out_kernel, struct((4, 2, SPAN, features), BF16), [])(
-        entry, out_map, inner, gate, weights, back_small
-    )
+    hbm = pl.BlockSpec(memory_space=pltpu.HBM)
+    partial = kernel_call(
+        out_kernel,
+        struct((4, 2, SPAN, features), BF16),
+        [
+            pltpu.VMEM((2, SPAN, width), F32),
+            pltpu.VMEM((2, SPAN, width), F32),
+            pltpu.VMEM((8 * features, width), BF16),
+            pltpu.SemaphoreType.DMA((3,)),
+        ],
+        [vmem, vmem, hbm, hbm, hbm, vmem],
+        60,
+    )(entry, out_map, inner, gate, weights, back_small)
     parts = jnp.sum(lax.all_to_all(partial, "x", 0, 0, tiled=True).astype(F32), 0)
     low = lax.axis_index("y_hi") == 0
     kept, sent = jnp.where(low, parts[0], parts[1]), jnp.where(low, parts[1], parts[0]).astype(BF16)
@@ -330,7 +349,7 @@
 
 
 def solution(mesh):
-    fine = Mesh(mesh.devices.reshape(4, 4, 2, 2, 2, 4), AXES)
+    fine = Mesh(mesh.devices.reshape(2, 2, 8, 2, 2, 4), AXES)
     placed = (
         P(SEQ, HEAD), P(SEQ, HEAD), P(SEQ, HEAD), P(SEQ, None), P(SEQ, HEAD), P(HEAD), P(HEAD), P(HEAD), P(None, HEAD), P(), P(HEAD), P(HEAD, SEQ),
     )

time: 172 us -> 173 us (level)
  local copies, waits for them, and re-layouts: 17.2 us -> 7.99 us
  waiting for transfers between devices: 26.2 us -> 34.7 us
  starting transfers between devices: 76.8 us -> 68.8 us
  Pallas kernels: 13.9 us -> 20.6 us
  blocking collectives: 20.5 us -> 23.9 us
    ppermute x4 -> x3, starting transfers between devices: 14.8 us -> 6.06 us  [swapped(): return lax.ppermute(block, 'core', [(0, 1), (1, 0)])]
    unnamed x44 -> x38, local copies, waits for them, and re-layouts: 14.6 us -> 6.83 us
    ppermute x2 -> x1, starting transfers between devices: 5.83 us -> 1.92 us  [local(): far = lax.ppermute(near, 'y_bit', [(0, 1), (1, 0)])]
    ppermute x2, waiting for transfers between devices: 1.31 us -> 4.92 us  [shifted(): return lax.ppermute(value, SEQ, route)]
    all_to_all x1, blocking collectives: 20.5 us -> 23.9 us  [local(): got = lax.all_to_all(send, SEQ, 0, 0, tiled=True)]
    pallas_call x1, Pallas kernels: 4.2 us -> 7.55 us  [local(): kernel_call(inner_kernel, (struct((2, SPAN, STATE), BF16), struct((2, SPA...]
    pallas_call x1, Pallas kernels: 2.67 us -> 5.86 us  [local(): kernel_call(out_kernel, struct((4, 2, SPAN, features), BF16), [pltpu.VMEM...]
    ppermute x1, waiting for transfers between devices: 4.56 us -> 1.67 us  [local(): lax.ppermute(extended, 'y_hi', [(0, 1), (1, 0)])]
  transfers between devices with their start and end apart: 18 -> 16, of which waited for: 6 -> 8; matrix products, arithmetic and copies ran while one was open for 2% -> 2% of each run, Pallas kernels for 6% -> 8%
where the time goes in v4:
time: 173 us; the launch traced here: 172 us
  starting transfers between devices  68.8 us (40%)
  waiting for transfers between devices  34.7 us (20%)
  blocking collectives  23.9 us (14%)
  Pallas kernels  20.6 us (12%)
  between operations  13.8 us (8%)
  local copies, waits for them, and re-layouts  7.99 us (5%)
  other arithmetic  2.17 us (1%)
    all_to_all x1, blocking collectives, local(): got = lax.all_to_all(send, SEQ, 0, 0, tiled=True)  23.9 us
    all_to_all x1, starting transfers between devices, local(): near = lax.all_to_all(first, ('y_pair', 'z'), 0, 0, tiled=True)  12.6 us
    ppermute x3, starting transfers between devices, around(): lax.ppermute(block, axis, [(place, (place + step) % count) for place in r...  10.6 us
    all_to_all x1, waiting for transfers between devices, local(): lax.all_to_all(partial, 'x', 0, 0, tiled=True).astype(F32)  9.9 us
    ppermute x2, starting transfers between devices, shifted(): return lax.ppermute(value, SEQ, route)  8.63 us
    ppermute x1, starting transfers between devices, local(): lax.ppermute(extended, 'y_hi', [(0, 1), (1, 0)])  7.78 us
    pallas_call x1, Pallas kernels, local(): kernel_call(inner_kernel, (struct((2, SPAN, STATE), BF16), struct((2, SPA...  7.55 us
    all_to_all x1, starting transfers between devices, local(): lax.all_to_all(entries, SEQ, 0, 0, tiled=True).reshape(2 * width, STATE)  7.22 us
  transfers between devices with their start and end apart: 16, of which 8 were waited for; matrix products, arithmetic and copies ran while one was open for 2% of the time, Pallas kernels for 8%

profile of v4, /device:TPU:8, one launch (start us, length us, event | category | flops | bytes accessed | tf_op | source)
XLA Modules:
  0.0 171.9 jit_solution(7561742772967387295)
XLA Ops:
  8.7 1.1 shard_map.118
  9.8 12.6 %all-to-all-start = ((bf16[16,32,768]{2,1,0:T(8,128)(2,1)}), bf16[16,32,768]{2,1,0:T(8,128)(2,1)S(1)}, u32[]{:S(2)}, u32[]{:S(2)}) async-start(bf16[16,32,768]{2,1,0:T(8,128)(2,1)} %shard_map.118), calls=%async_computation | async-start | bytes 1572864 | tf_op jit(solution)/shard_map/all_to_all | solution.py:277
  22.5 1.9 %collective-permute-start.3 = (bf16[16,256]{1,0:T(8,128)(2,1)S(1)}, bf16[16,256]{1,0:T(8,128)(2,1)S(1)}, u32[]{:S(2)}, u32[]{:S(2)}) collective-permute-start(bf16[16,256]{1,0:T(8,128)(2,1)S(1)} %get-tuple-element.38), channel_id=1, source_target_pairs={{0,8},{8,16},{16,24},{24,32},{32,40},{40,48},{48,56},{56,64},{64,7... | collective-permute-start | bytes 24584 | tf_op jit(solution)/shard_map/ppermute | solution.py:243
  24.5 4.7 %collective-permute-start.1 = (bf16[32,1152]{1,0:T(8,128)(2,1)S(1)}, bf16[32,1152]{1,0:T(8,128)(2,1)S(1)}, u32[]{:S(2)}, u32[]{:S(2)}) collective-permute-start(bf16[32,1152]{1,0:T(8,128)(2,1)S(1)} %get-tuple-element.36), channel_id=1, source_target_pairs={{0,256},{128,384},{256,0},{384,128},{1,257},{129,385},{257,1},{385... | collective-permute-start | bytes 221192 | tf_op jit(solution)/shard_map/ppermute | solution.py:253
  29.2 1.9 %collective-permute-start = (bf16[32,1152]{1,0:T(8,128)(2,1)S(1)}, bf16[32,1152]{1,0:T(8,128)(2,1)S(1)}, u32[]{:S(2)}, u32[]{:S(2)}) collective-permute-start(bf16[32,1152]{1,0:T(8,128)(2,1)S(1)} %get-tuple-element.36), channel_id=1, source_target_pairs={{0,128},{128,256},{256,384},{384,0},{1,129},{129,257},{257,385},{3... | collective-permute-start | bytes 221192 | tf_op jit(solution)/shard_map/ppermute | solution.py:253
  31.1 3.9 %collective-permute-start.2 = (bf16[32,1152]{1,0:T(8,128)(2,1)S(1)}, bf16[32,1152]{1,0:T(8,128)(2,1)S(1)}, u32[]{:S(2)}, u32[]{:S(2)}) collective-permute-start(bf16[32,1152]{1,0:T(8,128)(2,1)S(1)} %get-tuple-element.36), channel_id=1, source_target_pairs={{0,384},{128,0},{256,128},{384,256},{1,385},{129,1},{257,129},{385... | collective-permute-start | bytes 221192 | tf_op jit(solution)/shard_map/ppermute | solution.py:253
  35.1 6.7 %collective-permute-start.4 = (bf16[16,256]{1,0:T(8,128)(2,1)S(1)}, bf16[16,256]{1,0:T(8,128)(2,1)S(1)}, u32[]{:S(2)}, u32[]{:S(2)}) collective-permute-start(bf16[16,256]{1,0:T(8,128)(2,1)S(1)} %get-tuple-element.37), channel_id=1, source_target_pairs={{8,0},{16,8},{24,16},{32,24},{40,32},{48,40},{56,48},{64,56},{72,6... | collective-permute-start | bytes 24584 | tf_op jit(solution)/shard_map/ppermute | solution.py:243
  41.8 4.9 %collective-permute-done.4 = bf16[16,256]{1,0:T(8,128)(2,1)S(1)} collective-permute-done((bf16[16,256]{1,0:T(8,128)(2,1)S(1)}, bf16[16,256]{1,0:T(8,128)(2,1)S(1)}, u32[]{:S(2)}, u32[]{:S(2)}) %collective-permute-start.4) | collective-permute-done | bytes 8224 | tf_op jit(solution)/shard_map/ppermute | solution.py:243
  46.7 7.8 %collective-permute-start.5 = (bf16[160,256]{1,0:T(8,128)(2,1)S(1)}, bf16[160,256]{1,0:T(8,128)(2,1)S(1)}, u32[]{:S(2)}, u32[]{:S(2)}) collective-permute-start(bf16[160,256]{1,0:T(8,128)(2,1)S(1)} %constant_dynamic-update-slice_fusion), channel_id=1, source_target_pairs={{0,4},{4,0},{1,5},{5,1},{2,6},{6,2},{3,7},{7,3},{8,12},{12,8},{9,1... | collective-permute-start | bytes 245768 | tf_op jit(solution)/shard_map/ppermute | solution.py:281
  55.3 1.7 collective-permute-done.5
  57.1 1.9 %collective-permute-start.6 = (bf16[16,32,768]{2,1,0:T(8,128)(2,1)S(1)}, bf16[16,32,768]{2,1,0:T(8,128)(2,1)S(1)}, u32[]{:S(2)}, u32[]{:S(2)}) collective-permute-start(bf16[16,32,768]{2,1,0:T(8,128)(2,1)S(1)} %all-to-all-done.n0), channel_id=1, source_target_pairs={{0,128},{128,0},{1,129},{129,1},{2,130},{130,2},{3,131},{131,3},{4... | collective-permute-start | bytes 2359304 | tf_op jit(solution)/shard_map/ppermute | solution.py:285
  59.0 0.9 broadcast_in_dim.21
  59.9 4.3 %all-to-all-start.1 = ((bf16[4,2,160,256]{3,2,1,0:T(8,128)(2,1)}), bf16[4,2,160,256]{3,2,1,0:T(8,128)(2,1)S(1)}, u32[]{:S(2)}, u32[]{:S(2)}) async-start(bf16[4,2,160,256]{3,2,1,0:T(8,128)(2,1)} %broadcast_in_dim.21), calls=%async_computation.1 | async-start | bytes 1310720 | tf_op jit(solution)/shard_map/all_to_all | solution.py:237
  64.2 1.9 %collective-permute-start.7 = (bf16[16,32,768]{2,1,0:T(8,128)(2,1)S(1)}, bf16[16,32,768]{2,1,0:T(8,128)(2,1)S(1)}, u32[]{:S(2)}, u32[]{:S(2)}) collective-permute-start(bf16[16,32,768]{2,1,0:T(8,128)(2,1)S(1)} %all-to-all-done.n0), channel_id=1, source_target_pairs={{0,8},{8,0},{1,9},{9,1},{2,10},{10,2},{3,11},{11,3},{4,12},{12,4},... | collective-permute-start | bytes 2359304 | tf_op jit(solution)/shard_map/ppermute | solution.py:247
  66.1 6.9 %all-to-all-done.1.x_ref = bf16[4,2,160,256]{3,2,1,0:T(8,128)(2,1)S(1)} async-done(((bf16[4,2,160,256]{3,2,1,0:T(8,128)(2,1)}), bf16[4,2,160,256]{3,2,1,0:T(8,128)(2,1)S(1)}, u32[]{:S(2)}, u32[]{:S(2)}) %all-to-all-start.1) | async-done | bytes 655392 | tf_op jit(solution)/shard_map/all_to_all | solution.py:237
  73.0 2.2 %collective-permute-done.6.f0 = bf16[16,32,768]{2,1,0:T(8,128)(2,1)S(1)} collective-permute-done((bf16[16,32,768]{2,1,0:T(8,128)(2,1)S(1)}, bf16[16,32,768]{2,1,0:T(8,128)(2,1)S(1)}, u32[]{:S(2)}, u32[]{:S(2)}) %collective-permute-start.6) | collective-permute-done | bytes 786464 | tf_op jit(solution)/shard_map/ppermute | solution.py:285
  75.1 1.9 %collective-permute-start.8 = (bf16[16,32,768]{2,1,0:T(8,128)(2,1)S(1)}, bf16[16,32,768]{2,1,0:T(8,128)(2,1)}, u32[]{:S(2)}, u32[]{:S(2)}) collective-permute-start(bf16[16,32,768]{2,1,0:T(8,128)(2,1)S(1)} %collective-permute-done.6.f0), channel_id=1, source_target_pairs={{0,8},{8,0},{1,9},{9,1},{2,10},{10,2},{3,11},{11,3},{4,12},{12,4},... | collective-permute-start | bytes 2359304 | tf_op jit(solution)/shard_map/ppermute | solution.py:247
  77.3 2.1 %collective-permute-done.8.f1 = bf16[16,32,768]{2,1,0:T(8,128)(2,1)} collective-permute-done((bf16[16,32,768]{2,1,0:T(8,128)(2,1)S(1)}, bf16[16,32,768]{2,1,0:T(8,128)(2,1)}, u32[]{:S(2)}, u32[]{:S(2)}) %collective-permute-start.8) | collective-permute-done | bytes 786464 | tf_op jit(solution)/shard_map/ppermute | solution.py:247
  79.4 4.5 %shard_map.119 = (bf16[64,24,128]{2,1,0:T(8,128)(2,1)S(1)}, bf16[288,2048]{1,0:T(8,128)(2,1)S(1)}, bf16[2,128,640]{2,1,0:T(8,128)(2,1)S(1)}, f32[2,128,128]{2,1,0:T(8,128)S(1)}) custom-call(s32[5]{0:T(128)S(1)} %stack.47.place_ref, bf16[4,2,160,256]{3,2,1,0:T(8,128)(2,1)S(1)} %all-to-all-done.1.x_ref, bf16[16,32,768]{2,1,0:T(8,128)(2,1)S(1)} %all-to-all-done.n0, ...), custom_call_target="tpu_custom_call" | custom-call | tf_op jit(solution)/shard_map/pallas_call | solution.py:302
  84.0 1.1 copy-done
  86.4 23.9 %all_to_all.25.got_ref = bf16[64,24,128]{2,1,0:T(8,128)(2,1)S(1)} all-to-all(bf16[64,24,128]{2,1,0:T(8,128)(2,1)S(1)} %get-tuple-element.25), channel_id=1, replica_groups=mesh['y_pair'=2,'y_bit'=2,'z'=8,'core'=2,'y_hi'=2,'x'=4] {'y_pair','y_bi..., dimensions={0} | all-to-all | bytes 786432 | tf_op jit(solution)/shard_map/all_to_all | solution.py:315
  110.3 2.2 %collective-permute-start.9 = (bf16[8,4,32,1152]{3,2,1,0:T(8,128)(2,1)}, bf16[8,4,32,1152]{3,2,1,0:T(8,128)(2,1)S(1)}, u32[]{:S(2)}, u32[]{:S(2)}) collective-permute-start(bf16[8,4,32,1152]{3,2,1,0:T(8,128)(2,1)} %bitcast.25), channel_id=1, source_target_pairs={{0,8},{8,0},{1,9},{9,1},{2,10},{10,2},{3,11},{11,3},{4,12},{12,4},... | collective-permute-start | bytes 7077896 | tf_op jit(solution)/shard_map/ppermute | solution.py:247
  112.6 1.5 shard_map.120
  114.1 7.2 %all-to-all-start.3 = ((bf16[64,16,128]{2,1,0:T(8,128)(2,1)}), bf16[64,16,128]{2,1,0:T(8,128)(2,1)S(1)}, u32[]{:S(2)}, u32[]{:S(2)}) async-start(bf16[64,16,128]{2,1,0:T(8,128)(2,1)} %shard_map.120), calls=%async_computation.3 | async-start | bytes 524288 | tf_op jit(solution)/shard_map/all_to_all | solution.py:319
  122.1 1.4 copy-done.7
  123.5 7.5 %shard_map.121 = (bf16[2,128,128]{2,1,0:T(8,128)(2,1)}, f32[2,128,512]{2,1,0:T(8,128)}, f32[2,128,512]{2,1,0:T(8,128)}, bf16[2048,512]{1,0:T(8,128)(2,1)}) custom-call(s32[5]{0:T(128)} %copy-done.5, bf16[288,2048]{1,0:T(8,128)(2,1)} %copy-done, bf16[8,4,32,1152]{3,2,1,0:T(8,128)(2,1)} %bitcast.26, bf16[8,4,32,1152]{3,2,1,0:T(8,128)(2,1)} %copy-done.7, ...), custom_call_target="tpu_custom_call" | custom-call | tf_op jit(solution)/shard_map/pallas_call | solution.py:320
  131.1 2.2 %all-to-all-done.3 = bf16[64,16,128]{2,1,0:T(8,128)(2,1)S(1)} async-done(((bf16[64,16,128]{2,1,0:T(8,128)(2,1)}), bf16[64,16,128]{2,1,0:T(8,128)(2,1)S(1)}, u32[]{:S(2)}, u32[]{:S(2)}) %all-to-all-start.3) | async-done | bytes 262176 | tf_op jit(solution)/shard_map/all_to_all | solution.py:319
  134.0 5.9 %shard_map.122 = bf16[4,2,128,256]{3,2,1,0:T(8,128)(2,1)} custom-call(bf16[1024,128]{1,0:T(8,128)(2,1)} %bitcast.27, bf16[2,128,128]{2,1,0:T(8,128)(2,1)} %get-tuple-element.31.map_ref, f32[2,128,512]{2,1,0:T(8,128)} %get-tuple-element.32.inner_in, f32[2,128,512]{2,1,0:T(8,128)} %get-tuple-element.33.gate_in, ...), custom_call_target="tpu_custom_call" | custom-call | tf_op jit(solution)/shard_map/pallas_call | solution.py:333
  139.9 4.3 %all-to-all-start.4 = ((bf16[4,2,128,256]{3,2,1,0:T(8,128)(2,1)}), bf16[4,2,128,256]{3,2,1,0:T(8,128)(2,1)S(1)}, u32[]{:S(2)}, u32[]{:S(2)}) async-start(bf16[4,2,128,256]{3,2,1,0:T(8,128)(2,1)} %shard_map.122), calls=%async_computation.4 | async-start | bytes 1048576 | tf_op jit(solution)/shard_map/all_to_all | solution.py:345
  144.1 9.9 %all-to-all-done.4 = bf16[4,2,128,256]{3,2,1,0:T(8,128)(2,1)S(1)} async-done(((bf16[4,2,128,256]{3,2,1,0:T(8,128)(2,1)}), bf16[4,2,128,256]{3,2,1,0:T(8,128)(2,1)S(1)}, u32[]{:S(2)}, u32[]{:S(2)}) %all-to-all-start.4) | async-done | bytes 524320 | tf_op jit(solution)/shard_map/all_to_all | solution.py:345
  154.1 5.4 %collective-permute-start.10 = (bf16[128,256]{1,0:T(8,128)(2,1)S(1)}, bf16[128,256]{1,0:T(8,128)(2,1)S(1)}, u32[]{:S(2)}, u32[]{:S(2)}) collective-permute-start(bf16[128,256]{1,0:T(8,128)(2,1)S(1)} %fusion.1), channel_id=1, source_target_pairs={{0,4},{4,0},{1,5},{5,1},{2,6},{6,2},{3,7},{7,3},{8,12},{12,8},{9,1... | collective-permute-start | bytes 196616 | tf_op jit(solution)/shard_map/ppermute | solution.py:348
  159.5 4.9 %collective-permute-done.10 = bf16[128,256]{1,0:T(8,128)(2,1)S(1)} collective-permute-done((bf16[128,256]{1,0:T(8,128)(2,1)S(1)}, bf16[128,256]{1,0:T(8,128)(2,1)S(1)}, u32[]{:S(2)}, u32[]{:S(2)}) %collective-permute-start.10) | collective-permute-done | bytes 65568 | tf_op jit(solution)/shard_map/ppermute | solution.py:348
  (67 shorter events, 6.8 us)
Async XLA Ops:
  7.3 0.8 copy-start.4
  8.7 13.8 %copy-start.9 = (bf16[128,256]{1,0:T(8,128)(2,1)S(1)}, bf16[128,256]{1,0:T(8,128)(2,1)}, u32[]{:S(2)}) copy-start(bf16[128,256]{1,0:T(8,128)(2,1)} %param.12) | copy-start | bytes 196612
  8.7 15.7 %slice-start = ((bf16[32,256]{1,0:T(8,128)(2,1)}), bf16[32,128]{1,0:T(8,128)(2,1)S(1)}, s32[]{:S(2)}) async-start(bf16[32,256]{1,0:T(8,128)(2,1)} %maps_ref.1), calls=%async_computation.6 | async-start | bytes 16384 | tf_op jit(solution)/shard_map/slice | solution.py:276
  8.7 15.7 %copy-start.10 = (bf16[32,512]{1,0:T(8,128)(2,1)S(1)}, bf16[32,512]{1,0:T(8,128)(2,1)}, u32[]{:S(2)}) copy-start(bf16[32,512]{1,0:T(8,128)(2,1)} %param.14) | copy-start | bytes 98308
  8.7 15.7 %copy-start.11 = (bf16[512,32]{0,1:T(8,128)(2,1)S(1)}, bf16[512,32]{0,1:T(8,128)(2,1)}, u32[]{:S(2)}) copy-start(bf16[512,32]{0,1:T(8,128)(2,1)} %param.23) | copy-start | bytes 98308
  9.8 67.3 %copy-start.16 = (f32[8]{0:T(128)S(1)}, f32[8]{0:T(128)}, u32[]{:S(2)}) copy-start(f32[8]{0:T(128)} %param.17) | copy-start | bytes 100
  9.8 67.3 %copy-start.15 = (f32[8]{0:T(128)S(1)}, f32[8]{0:T(128)}, u32[]{:S(2)}) copy-start(f32[8]{0:T(128)} %param.18) | copy-start | bytes 100
  9.8 67.4 %copy-start.13 = (f32[4,256]{1,0:T(4,128)S(1)}, f32[4,256]{1,0:T(4,128)}, u32[]{:S(2)}) copy-start(f32[4,256]{1,0:T(4,128)} %param.21) | copy-start | bytes 12292
  9.8 67.4 %copy-start.12 = (f32[4,512]{1,0:T(4,128)S(1)}, f32[4,512]{1,0:T(4,128)}, u32[]{:S(2)}) copy-start(f32[4,512]{1,0:T(4,128)} %param.20) | copy-start | bytes 24580
  9.8 47.2 %all-to-all-start = ((bf16[16,32,768]{2,1,0:T(8,128)(2,1)}), bf16[16,32,768]{2,1,0:T(8,128)(2,1)S(1)}, u32[]{:S(2)}, u32[]{:S(2)}) async-start(bf16[16,32,768]{2,1,0:T(8,128)(2,1)} %shard_map.118), calls=%async_computation | async-start | bytes 1572864 | tf_op jit(solution)/shard_map/all_to_all | solution.py:277
  22.4 87.9 %all-gather.3.cloned.1.call-start = ((), (), s32[]{:S(2)}) async-start(), calls=%async_computation.5 | async-start | bytes 2654208 | tf_op jit(solution)/shard_map/all_gather | solution.py:284
  22.5 19.3 %collective-permute-start.3 = (bf16[16,256]{1,0:T(8,128)(2,1)S(1)}, bf16[16,256]{1,0:T(8,128)(2,1)S(1)}, u32[]{:S(2)}, u32[]{:S(2)}) collective-permute-start(bf16[16,256]{1,0:T(8,128)(2,1)S(1)} %get-tuple-element.38), channel_id=1, source_target_pairs={{0,8},{8,16},{16,24},{24,32},{32,40},{40,48},{48,56},{56,64},{64,7... | collective-permute-start | bytes 24584 | tf_op jit(solution)/shard_map/ppermute | solution.py:243
  24.5 30.1 %collective-permute-start.1 = (bf16[32,1152]{1,0:T(8,128)(2,1)S(1)}, bf16[32,1152]{1,0:T(8,128)(2,1)S(1)}, u32[]{:S(2)}, u32[]{:S(2)}) collective-permute-start(bf16[32,1152]{1,0:T(8,128)(2,1)S(1)} %get-tuple-element.36), channel_id=1, source_target_pairs={{0,256},{128,384},{256,0},{384,128},{1,257},{129,385},{257,1},{385... | collective-permute-start | bytes 221192 | tf_op jit(solution)/shard_map/ppermute | solution.py:253
  29.2 25.3 %collective-permute-start = (bf16[32,1152]{1,0:T(8,128)(2,1)S(1)}, bf16[32,1152]{1,0:T(8,128)(2,1)S(1)}, u32[]{:S(2)}, u32[]{:S(2)}) collective-permute-start(bf16[32,1152]{1,0:T(8,128)(2,1)S(1)} %get-tuple-element.36), channel_id=1, source_target_pairs={{0,128},{128,256},{256,384},{384,0},{1,129},{129,257},{257,385},{3... | collective-permute-start | bytes 221192 | tf_op jit(solution)/shard_map/ppermute | solution.py:253
  31.1 23.4 %collective-permute-start.2 = (bf16[32,1152]{1,0:T(8,128)(2,1)S(1)}, bf16[32,1152]{1,0:T(8,128)(2,1)S(1)}, u32[]{:S(2)}, u32[]{:S(2)}) collective-permute-start(bf16[32,1152]{1,0:T(8,128)(2,1)S(1)} %get-tuple-element.36), channel_id=1, source_target_pairs={{0,384},{128,0},{256,128},{384,256},{1,385},{129,1},{257,129},{385... | collective-permute-start | bytes 221192 | tf_op jit(solution)/shard_map/ppermute | solution.py:253
  35.1 11.7 %collective-permute-start.4 = (bf16[16,256]{1,0:T(8,128)(2,1)S(1)}, bf16[16,256]{1,0:T(8,128)(2,1)S(1)}, u32[]{:S(2)}, u32[]{:S(2)}) collective-permute-start(bf16[16,256]{1,0:T(8,128)(2,1)S(1)} %get-tuple-element.37), channel_id=1, source_target_pairs={{8,0},{16,8},{24,16},{32,24},{40,32},{48,40},{56,48},{64,56},{72,6... | collective-permute-start | bytes 24584 | tf_op jit(solution)/shard_map/ppermute | solution.py:243
  46.7 10.3 %collective-permute-start.5 = (bf16[160,256]{1,0:T(8,128)(2,1)S(1)}, bf16[160,256]{1,0:T(8,128)(2,1)S(1)}, u32[]{:S(2)}, u32[]{:S(2)}) collective-permute-start(bf16[160,256]{1,0:T(8,128)(2,1)S(1)} %constant_dynamic-update-slice_fusion), channel_id=1, source_target_pairs={{0,4},{4,0},{1,5},{5,1},{2,6},{6,2},{3,7},{7,3},{8,12},{12,8},{9,1... | collective-permute-start | bytes 245768 | tf_op jit(solution)/shard_map/ppermute | solution.py:281
  57.1 18.1 %collective-permute-start.6 = (bf16[16,32,768]{2,1,0:T(8,128)(2,1)S(1)}, bf16[16,32,768]{2,1,0:T(8,128)(2,1)S(1)}, u32[]{:S(2)}, u32[]{:S(2)}) collective-permute-start(bf16[16,32,768]{2,1,0:T(8,128)(2,1)S(1)} %all-to-all-done.n0), channel_id=1, source_target_pairs={{0,128},{128,0},{1,129},{129,1},{2,130},{130,2},{3,131},{131,3},{4... | collective-permute-start | bytes 2359304 | tf_op jit(solution)/shard_map/ppermute | solution.py:285
  59.9 13.1 %all-to-all-start.1 = ((bf16[4,2,160,256]{3,2,1,0:T(8,128)(2,1)}), bf16[4,2,160,256]{3,2,1,0:T(8,128)(2,1)S(1)}, u32[]{:S(2)}, u32[]{:S(2)}) async-start(bf16[4,2,160,256]{3,2,1,0:T(8,128)(2,1)} %broadcast_in_dim.21), calls=%async_computation.1 | async-start | bytes 1310720 | tf_op jit(solution)/shard_map/all_to_all | solution.py:237
  64.2 13.1 %collective-permute-start.7 = (bf16[16,32,768]{2,1,0:T(8,128)(2,1)S(1)}, bf16[16,32,768]{2,1,0:T(8,128)(2,1)S(1)}, u32[]{:S(2)}, u32[]{:S(2)}) collective-permute-start(bf16[16,32,768]{2,1,0:T(8,128)(2,1)S(1)} %all-to-all-done.n0), channel_id=1, source_target_pairs={{0,8},{8,0},{1,9},{9,1},{2,10},{10,2},{3,11},{11,3},{4,12},{12,4},... | collective-permute-start | bytes 2359304 | tf_op jit(solution)/shard_map/ppermute | solution.py:247
  75.1 4.3 %collective-permute-start.8 = (bf16[16,32,768]{2,1,0:T(8,128)(2,1)S(1)}, bf16[16,32,768]{2,1,0:T(8,128)(2,1)}, u32[]{:S(2)}, u32[]{:S(2)}) collective-permute-start(bf16[16,32,768]{2,1,0:T(8,128)(2,1)S(1)} %collective-permute-done.6.f0), channel_id=1, source_target_pairs={{0,8},{8,0},{1,9},{9,1},{2,10},{10,2},{3,11},{11,3},{4,12},{12,4},... | collective-permute-start | bytes 2359304 | tf_op jit(solution)/shard_map/ppermute | solution.py:247
  77.2 36.9 %copy-start.5 = (s32[5]{0:T(128)}, s32[5]{0:T(128)S(1)}, u32[]{:S(2)}) copy-start(s32[5]{0:T(128)S(1)} %stack.47.place_ref) | copy-start | bytes 64
  77.3 44.1 %copy-start.17 = (f32[8]{0:T(128)S(1)}, f32[8]{0:T(128)}, u32[]{:S(2)}) copy-start(f32[8]{0:T(128)} %param.19) | copy-start | bytes 100
  77.3 44.2 %copy-start.14 = (f32[512]{0:T(512)S(1)}, f32[512]{0:T(512)}, u32[]{:S(2)}) copy-start(f32[512]{0:T(512)} %param.22) | copy-start | bytes 6148
  84.0 1.1 copy-start
  85.1 0.7 copy-start.1
  110.3 11.8 %collective-permute-start.9 = (bf16[8,4,32,1152]{3,2,1,0:T(8,128)(2,1)}, bf16[8,4,32,1152]{3,2,1,0:T(8,128)(2,1)S(1)}, u32[]{:S(2)}, u32[]{:S(2)}) collective-permute-start(bf16[8,4,32,1152]{3,2,1,0:T(8,128)(2,1)} %bitcast.25), channel_id=1, source_target_pairs={{0,8},{8,0},{1,9},{9,1},{2,10},{10,2},{3,11},{11,3},{4,12},{12,4},... | collective-permute-start | bytes 7077896 | tf_op jit(solution)/shard_map/ppermute | solution.py:247
  114.1 19.2 %all-to-all-start.3 = ((bf16[64,16,128]{2,1,0:T(8,128)(2,1)}), bf16[64,16,128]{2,1,0:T(8,128)(2,1)S(1)}, u32[]{:S(2)}, u32[]{:S(2)}) async-start(bf16[64,16,128]{2,1,0:T(8,128)(2,1)} %shard_map.120), calls=%async_computation.3 | async-start | bytes 524288 | tf_op jit(solution)/shard_map/all_to_all | solution.py:319
  122.1 1.4 copy-start.7
  133.3 0.7 copy-start.8
  139.9 14.2 %all-to-all-start.4 = ((bf16[4,2,128,256]{3,2,1,0:T(8,128)(2,1)}), bf16[4,2,128,256]{3,2,1,0:T(8,128)(2,1)S(1)}, u32[]{:S(2)}, u32[]{:S(2)}) async-start(bf16[4,2,128,256]{3,2,1,0:T(8,128)(2,1)} %shard_map.122), calls=%async_computation.4 | async-start | bytes 1048576 | tf_op jit(solution)/shard_map/all_to_all | solution.py:345
  154.1 10.3 %collective-permute-start.10 = (bf16[128,256]{1,0:T(8,128)(2,1)S(1)}, bf16[128,256]{1,0:T(8,128)(2,1)S(1)}, u32[]{:S(2)}, u32[]{:S(2)}) collective-permute-start(bf16[128,256]{1,0:T(8,128)(2,1)S(1)} %fusion.1), channel_id=1, source_target_pairs={{0,4},{4,0},{1,5},{5,1},{2,6},{6,2},{3,7},{7,3},{8,12},{12,8},{9,1... | collective-permute-start | bytes 196616 | tf_op jit(solution)/shard_map/ppermute | solution.py:348
  (3 other events, 2.1 us)
Sparse Core Ops, SparseCore 0:
  57.2 51.9 all-gather.2

commit v5 on v4

--- a/solution.py
+++ b/solution.py
@@ -12,9 +12,9 @@
 STATE = 128
 HALO = 16
 EXT = SPAN + HALO
-AXES = ("y_pair", "y_bit", "z", "core", "y_hi", "x")
-SEQ = ("y_pair", "y_bit", "z", "core")
-Y_LO = ("y_pair", "y_bit")
+AXES = ("y_lo", "z_pair", "z_bit", "core", "y_hi", "x")
+SEQ = ("y_lo", "z_pair", "z_bit", "core")
+Z = ("z_pair", "z_bit")
 HEAD = ("y_hi", "x")
 F32 = jnp.float32
 BF16 = jnp.bfloat16
@@ -70,12 +70,13 @@
 def assemble(place_ref, pieces, full_ref):
     bit, core = place_ref[1], place_ref[2]
     for side in range(2):
-        near, far = pieces[2 * side : 2 * side + 2]
+        near, left, right = pieces[3 * side : 3 * side + 3]
         column = core + side - 2 * core * side
         for block in range(16):
-            start = 1024 * (block // 8) + 64 * (block % 8) + 32 * column
-            full_ref[pl.ds(pl.multiple_of(start + 512 * bit, 32), 32)] = near[block]
-            full_ref[pl.ds(pl.multiple_of(start + 512 * (1 - bit), 32), 32)] = far[block]
+            far = left.at[block] if block < 8 else right.at[block - 8]
+            start = 128 * block + 32 * column
+            full_ref[pl.ds(pl.multiple_of(start + 64 * bit, 32), 32)] = near[block]
+            full_ref[pl.ds(pl.multiple_of(start + 64 * (1 - bit), 32), 32)] = far[...]
 
 
 def pack_kernel(input_ref, maps_ref, step_ref, out_ref):
@@ -87,10 +88,10 @@
 
 
 def front_kernel(
-    place_ref, x_ref, n0, f0, n1, f1, small_ref,
+    place_ref, x_ref, n0, l0, r0, n1, l1, r1, small_ref,
     send_ref, stream_ref, conv_ref, step_ref, rows_ref, full_ref,
 ):
-    assemble(place_ref, (n0, f0, n1, f1), full_ref)
+    assemble(place_ref, (n0, l0, r0, n1, l1, r1), full_ref)
     y_hi = place_ref[4]
     flip_rows, flip_columns = reversal(EXT), reversal(256)
     for step in range(4):
@@ -247,6 +248,13 @@
     return lax.ppermute(block, "core", [(0, 1), (1, 0)])
 
 
+def neighbours(near):
+    count, half = lax.axis_size(Z), near.shape[0] // 2
+    left = lax.ppermute(near[:half], Z, [(z, (z + 1) % count) for z in range(count)])
+    right = lax.ppermute(near[half:], Z, [(z, (z - 1) % count) for z in range(count)])
+    return left, right
+
+
 def around(block, axis):
     count = lax.axis_size(axis)
     steps = [
@@ -266,7 +274,7 @@
     rows, features = layer_input.shape
     width, heads = w_input.shape[1], w_step.shape[1]
     wide = 128 - heads
-    place = jnp.stack([lax.axis_index(SEQ), lax.axis_index("y_bit"), lax.axis_index("core")] + [lax.axis_index(axis) for axis in (Y_LO, "y_hi")])
+    place = jnp.stack([lax.axis_index(SEQ), lax.axis_index("z_bit"), lax.axis_index("core")] + [lax.axis_index(axis) for axis in ("y_lo", "y_hi")])
     smem = pl.BlockSpec(memory_space=pltpu.SMEM)
     vmem = pl.BlockSpec(memory_space=pltpu.VMEM)
     struct = jax.ShapeDtypeStruct
@@ -274,18 +282,17 @@
         w_input, w_maps, w_step.T
     )
     second = jnp.concatenate([w_out.T, w_gate, w_maps[:, STATE:]], 1)
-    near = lax.all_to_all(first, ("y_pair", "z"), 0, 0, tiled=True)
+    near = lax.all_to_all(first, ("y_lo", "z_pair"), 0, 0, tiled=True)
     before = shifted(layer_input[rows - HALO :], 1)
     after = shifted(layer_input[:HALO], -1)
     extended = jnp.concatenate([before, layer_input, after])
     extended = jnp.stack([extended, lax.ppermute(extended, "y_hi", [(0, 1), (1, 0)])])
-    second_y = around(second, Y_LO)
+    second_y = around(second, "y_lo")
     near, second_y, extended = together(near, second_y, extended)
-    second_z = lax.all_gather(second_y, "z")
-    far = lax.ppermute(near, "y_bit", [(0, 1), (1, 0)])
+    second_z = lax.all_gather(second_y, Z)
+    left, right = neighbours(near)
     blocks = copies(extended, "x")
-    far, blocks = together(far, blocks)
-    first_pieces = (near, far, swapped(near), swapped(far))
+    first_pieces = (near, left, right, swapped(near), swapped(left), swapped(right))
     places = 2 * width // 16
     front_small = jnp.concatenate(
         [jnp.concatenate([conv_input, conv_maps[:, :STATE]], 1)]
@@ -308,7 +315,7 @@
             struct((2, SPAN, 128), F32),
         ),
         [pltpu.VMEM((2 * EXT, width + STATE), F32), pltpu.VMEM((8 * features, width + 2 * STATE), BF16)],
-        [smem] + [vmem] * 6,
+        [smem] + [vmem] * 8,
     )(
         place, blocks, *first_pieces, front_small,
     )
@@ -349,7 +356,7 @@
 
 
 def solution(mesh):
-    fine = Mesh(mesh.devices.reshape(2, 2, 8, 2, 2, 4), AXES)
+    fine = Mesh(mesh.devices.reshape(4, 4, 2, 2, 2, 4), AXES)
     placed = (
         P(SEQ, HEAD), P(SEQ, HEAD), P(SEQ, HEAD), P(SEQ, None), P(SEQ, HEAD), P(HEAD), P(HEAD), P(HEAD), P(None, HEAD), P(), P(HEAD), P(HEAD, SEQ),
     )

time: 173 us -> 172 us (level)
  starting transfers between devices: 68.8 us -> 76.9 us
  waiting for transfers between devices: 34.7 us -> 28.4 us
  blocking collectives: 23.9 us -> 20.5 us
    ppermute x3 -> x4, starting transfers between devices: 6.06 us -> 14.8 us  [swapped(): return lax.ppermute(block, 'core', [(0, 1), (1, 0)])]
    ppermute x1 -> x2, starting transfers between devices: 1.92 us -> 5.83 us  [the longest x1 3.07 us: neighbours(): lax.ppermute(near[half:], Z, [(z, (z - 1) % count) for z in range(count)])]
    ppermute x2, waiting for transfers between devices: 4.92 us -> 1.31 us  [shifted(): return lax.ppermute(value, SEQ, route)]
    all_to_all x1, blocking collectives: 23.9 us -> 20.5 us  [local(): got = lax.all_to_all(send, SEQ, 0, 0, tiled=True)]
    ppermute x1, waiting for transfers between devices: 1.67 us -> 4.55 us  [local(): lax.ppermute(extended, 'y_hi', [(0, 1), (1, 0)])]
    ppermute x1, starting transfers between devices: 7.78 us -> 5.02 us  [local(): lax.ppermute(extended, 'y_hi', [(0, 1), (1, 0)])]
    all_to_all x1, waiting for transfers between devices: 6.87 us -> 4.67 us  [copies(): lax.all_to_all(jnp.broadcast_to(block[None], (count, *block.shape)), axis...]
    ppermute x1 -> x2, waiting for transfers between devices: 2.17 us -> 0.01 us  [the longest x1 0.01 us: neighbours(): lax.ppermute(near[half:], Z, [(z, (z - 1) % count) for z in range(count)])]
  transfers between devices with their start and end apart: 16 -> 18, of which waited for: 8 -> 6; matrix products, arithmetic and copies ran while one was open for 2% -> 2% of each run, Pallas kernels for 8% -> 8%
where the time goes in v5:
time: 172 us; the launch traced here: 171 us
  starting transfers between devices  76.9 us (45%)
  waiting for transfers between devices  28.4 us (17%)
  blocking collectives  20.5 us (12%)
  Pallas kernels  20.4 us (12%)
  between operations  13.8 us (8%)
  local copies, waits for them, and re-layouts  8.8 us (5%)
  other arithmetic  2.17 us (1%)
    all_to_all x1, blocking collectives, local(): got = lax.all_to_all(send, SEQ, 0, 0, tiled=True)  20.5 us
    ppermute x4, starting transfers between devices, swapped(): return lax.ppermute(block, 'core', [(0, 1), (1, 0)])  14.8 us
    all_to_all x1, starting transfers between devices, local(): near = lax.all_to_all(first, ('y_lo', 'z_pair'), 0, 0, tiled=True)  13.8 us
    all_to_all x1, waiting for transfers between devices, local(): lax.all_to_all(partial, 'x', 0, 0, tiled=True).astype(F32)  10.1 us
    ppermute x3, starting transfers between devices, around(): lax.ppermute(block, axis, [(place, (place + step) % count) for place in r...  10.1 us
    ppermute x2, starting transfers between devices, shifted(): return lax.ppermute(value, SEQ, route)  8.63 us
    pallas_call x1, Pallas kernels, local(): kernel_call(inner_kernel, (struct((2, SPAN, STATE), BF16), struct((2, SPA...  7.56 us
    unnamed x38, local copies, waits for them, and re-layouts  6.85 us
  transfers between devices with their start and end apart: 18, of which 6 were waited for; matrix products, arithmetic and copies ran while one was open for 2% of the time, Pallas kernels for 8%

profile of v5, /device:TPU:8, one launch (start us, length us, event | category | flops | bytes accessed | tf_op | source)
XLA Modules:
  0.0 171.0 jit_solution(7371011151781002338)
XLA Ops:
  8.7 1.1 shard_map.118
  9.8 13.8 %all-to-all-start = ((bf16[16,32,768]{2,1,0:T(8,128)(2,1)}), bf16[16,32,768]{2,1,0:T(8,128)(2,1)S(1)}, u32[]{:S(2)}, u32[]{:S(2)}) async-start(bf16[16,32,768]{2,1,0:T(8,128)(2,1)} %shard_map.118), calls=%async_computation | async-start | bytes 1572864 | tf_op jit(solution)/shard_map/all_to_all | solution.py:285
  23.7 1.9 %collective-permute-start.3 = (bf16[16,256]{1,0:T(8,128)(2,1)S(1)}, bf16[16,256]{1,0:T(8,128)(2,1)S(1)}, u32[]{:S(2)}, u32[]{:S(2)}) collective-permute-start(bf16[16,256]{1,0:T(8,128)(2,1)S(1)} %get-tuple-element.36), channel_id=1, source_target_pairs={{0,8},{8,16},{16,24},{24,32},{32,40},{40,48},{48,56},{56,64},{64,7... | collective-permute-start | bytes 24584 | tf_op jit(solution)/shard_map/ppermute | solution.py:244
  25.7 4.3 %collective-permute-start.1 = (bf16[32,1152]{1,0:T(8,128)(2,1)S(1)}, bf16[32,1152]{1,0:T(8,128)(2,1)S(1)}, u32[]{:S(2)}, u32[]{:S(2)}) collective-permute-start(bf16[32,1152]{1,0:T(8,128)(2,1)S(1)} %get-tuple-element.34), channel_id=1, source_target_pairs={{0,256},{128,384},{256,0},{384,128},{1,257},{129,385},{257,1},{385... | collective-permute-start | bytes 221192 | tf_op jit(solution)/shard_map/ppermute | solution.py:261
  29.9 1.9 %collective-permute-start = (bf16[32,1152]{1,0:T(8,128)(2,1)S(1)}, bf16[32,1152]{1,0:T(8,128)(2,1)S(1)}, u32[]{:S(2)}, u32[]{:S(2)}) collective-permute-start(bf16[32,1152]{1,0:T(8,128)(2,1)S(1)} %get-tuple-element.34), channel_id=1, source_target_pairs={{0,128},{128,256},{256,384},{384,0},{1,129},{129,257},{257,385},{3... | collective-permute-start | bytes 221192 | tf_op jit(solution)/shard_map/ppermute | solution.py:261
  31.9 3.9 %collective-permute-start.2 = (bf16[32,1152]{1,0:T(8,128)(2,1)S(1)}, bf16[32,1152]{1,0:T(8,128)(2,1)S(1)}, u32[]{:S(2)}, u32[]{:S(2)}) collective-permute-start(bf16[32,1152]{1,0:T(8,128)(2,1)S(1)} %get-tuple-element.34), channel_id=1, source_target_pairs={{0,384},{128,0},{256,128},{384,256},{1,385},{129,1},{257,129},{385... | collective-permute-start | bytes 221192 | tf_op jit(solution)/shard_map/ppermute | solution.py:261
  35.8 6.7 %collective-permute-start.4 = (bf16[16,256]{1,0:T(8,128)(2,1)S(1)}, bf16[16,256]{1,0:T(8,128)(2,1)S(1)}, u32[]{:S(2)}, u32[]{:S(2)}) collective-permute-start(bf16[16,256]{1,0:T(8,128)(2,1)S(1)} %get-tuple-element.35), channel_id=1, source_target_pairs={{8,0},{16,8},{24,16},{32,24},{40,32},{48,40},{56,48},{64,56},{72,6... | collective-permute-start | bytes 24584 | tf_op jit(solution)/shard_map/ppermute | solution.py:244
  42.6 1.3 collective-permute-done.4
  43.9 5.0 %collective-permute-start.5 = (bf16[160,256]{1,0:T(8,128)(2,1)S(1)}, bf16[160,256]{1,0:T(8,128)(2,1)S(1)}, u32[]{:S(2)}, u32[]{:S(2)}) collective-permute-start(bf16[160,256]{1,0:T(8,128)(2,1)S(1)} %constant_dynamic-update-slice_fusion), channel_id=1, source_target_pairs={{0,4},{4,0},{1,5},{5,1},{2,6},{6,2},{3,7},{7,3},{8,12},{12,8},{9,1... | collective-permute-start | bytes 245768 | tf_op jit(solution)/shard_map/ppermute | solution.py:289
  49.7 4.6 %collective-permute-done.5 = bf16[160,256]{1,0:T(8,128)(2,1)S(1)} collective-permute-done((bf16[160,256]{1,0:T(8,128)(2,1)S(1)}, bf16[160,256]{1,0:T(8,128)(2,1)S(1)}, u32[]{:S(2)}, u32[]{:S(2)}) %collective-permute-start.5) | collective-permute-done | bytes 81952 | tf_op jit(solution)/shard_map/ppermute | solution.py:289
  55.2 3.1 %collective-permute-start.7 = (bf16[8,32,768]{2,1,0:T(8,128)(2,1)S(1)}, bf16[8,32,768]{2,1,0:T(8,128)(2,1)S(1)}, u32[]{:S(2)}, u32[]{:S(2)}) collective-permute-start(bf16[8,32,768]{2,1,0:T(8,128)(2,1)S(1)} %get-tuple-element.31), channel_id=1, source_target_pairs={{0,112},{16,0},{32,16},{48,32},{64,48},{80,64},{96,80},{112,96},{1... | collective-permute-start | bytes 1179656 | tf_op jit(solution)/shard_map/ppermute | solution.py:254
  58.3 2.8 %collective-permute-start.6 = (bf16[8,32,768]{2,1,0:T(8,128)(2,1)}, bf16[8,32,768]{2,1,0:T(8,128)(2,1)S(1)}, u32[]{:S(2)}, u32[]{:S(2)}) collective-permute-start(bf16[8,32,768]{2,1,0:T(8,128)(2,1)} %get-tuple-element.32), channel_id=1, source_target_pairs={{0,16},{16,32},{32,48},{48,64},{64,80},{80,96},{96,112},{112,0},{1... | collective-permute-start | bytes 1179656 | tf_op jit(solution)/shard_map/ppermute | solution.py:253
  61.0 6.5 %collective-permute-start.8 = (bf16[16,32,768]{2,1,0:T(8,128)(2,1)S(1)}, bf16[16,32,768]{2,1,0:T(8,128)(2,1)S(1)}, u32[]{:S(2)}, u32[]{:S(2)}) collective-permute-start(bf16[16,32,768]{2,1,0:T(8,128)(2,1)S(1)} %all-to-all-done.n0), channel_id=1, source_target_pairs={{0,8},{8,0},{1,9},{9,1},{2,10},{10,2},{3,11},{11,3},{4,12},{12,4},... | collective-permute-start | bytes 2359304 | tf_op jit(solution)/shard_map/ppermute | solution.py:248
  67.5 0.9 broadcast_in_dim.21
  68.4 4.3 %all-to-all-start.1 = ((bf16[4,2,160,256]{3,2,1,0:T(8,128)(2,1)}), bf16[4,2,160,256]{3,2,1,0:T(8,128)(2,1)S(1)}, u32[]{:S(2)}, u32[]{:S(2)}) async-start(bf16[4,2,160,256]{3,2,1,0:T(8,128)(2,1)} %broadcast_in_dim.21), calls=%async_computation.1 | async-start | bytes 1310720 | tf_op jit(solution)/shard_map/all_to_all | solution.py:238
  72.7 1.9 %collective-permute-start.10 = (bf16[8,32,768]{2,1,0:T(8,128)(2,1)S(1)}, bf16[8,32,768]{2,1,0:T(8,128)(2,1)S(1)}, u32[]{:S(2)}, u32[]{:S(2)}) collective-permute-start(bf16[8,32,768]{2,1,0:T(8,128)(2,1)S(1)} %collective-permute-done.7.r0), channel_id=1, source_target_pairs={{0,8},{8,0},{1,9},{9,1},{2,10},{10,2},{3,11},{11,3},{4,12},{12,4},... | collective-permute-start | bytes 1179656 | tf_op jit(solution)/shard_map/ppermute | solution.py:248
  74.6 4.2 %collective-permute-start.9 = (bf16[8,32,768]{2,1,0:T(8,128)(2,1)S(1)}, bf16[8,32,768]{2,1,0:T(8,128)(2,1)}, u32[]{:S(2)}, u32[]{:S(2)}) collective-permute-start(bf16[8,32,768]{2,1,0:T(8,128)(2,1)S(1)} %collective-permute-done.6.l0), channel_id=1, source_target_pairs={{0,8},{8,0},{1,9},{9,1},{2,10},{10,2},{3,11},{11,3},{4,12},{12,4},... | collective-permute-start | bytes 1179656 | tf_op jit(solution)/shard_map/ppermute | solution.py:248
  79.1 4.7 %all-to-all-done.1.x_ref = bf16[4,2,160,256]{3,2,1,0:T(8,128)(2,1)S(1)} async-done(((bf16[4,2,160,256]{3,2,1,0:T(8,128)(2,1)}), bf16[4,2,160,256]{3,2,1,0:T(8,128)(2,1)S(1)}, u32[]{:S(2)}, u32[]{:S(2)}) %all-to-all-start.1) | async-done | bytes 655392 | tf_op jit(solution)/shard_map/all_to_all | solution.py:238
  83.8 4.4 %shard_map.119 = (bf16[64,24,128]{2,1,0:T(8,128)(2,1)S(1)}, bf16[288,2048]{1,0:T(8,128)(2,1)S(1)}, bf16[2,128,640]{2,1,0:T(8,128)(2,1)S(1)}, f32[2,128,128]{2,1,0:T(8,128)S(1)}) custom-call(s32[5]{0:T(128)S(1)} %stack.47.place_ref, bf16[4,2,160,256]{3,2,1,0:T(8,128)(2,1)S(1)} %all-to-all-done.1.x_ref, bf16[16,32,768]{2,1,0:T(8,128)(2,1)S(1)} %all-to-all-done.n0, ...), custom_call_target="tpu_custom_call" | custom-call | tf_op jit(solution)/shard_map/pallas_call | solution.py:309
  88.2 1.1 copy-done
  90.6 20.5 %all_to_all.25.got_ref = bf16[64,24,128]{2,1,0:T(8,128)(2,1)S(1)} all-to-all(bf16[64,24,128]{2,1,0:T(8,128)(2,1)S(1)} %get-tuple-element.21), channel_id=1, replica_groups=mesh['y_lo'=4,'z_pair'=4,'z_bit'=2,'core'=2,'y_hi'=2,'x'=4] {'y_lo','z_p..., dimensions={0} | all-to-all | bytes 786432 | tf_op jit(solution)/shard_map/all_to_all | solution.py:322
  111.1 2.2 %collective-permute-start.11 = (bf16[8,4,32,1152]{3,2,1,0:T(8,128)(2,1)}, bf16[8,4,32,1152]{3,2,1,0:T(8,128)(2,1)S(1)}, u32[]{:S(2)}, u32[]{:S(2)}) collective-permute-start(bf16[8,4,32,1152]{3,2,1,0:T(8,128)(2,1)} %bitcast.25), channel_id=1, source_target_pairs={{0,8},{8,0},{1,9},{9,1},{2,10},{10,2},{3,11},{11,3},{4,12},{12,4},... | collective-permute-start | bytes 7077896 | tf_op jit(solution)/shard_map/ppermute | solution.py:248
  113.4 1.5 shard_map.120
  114.9 5.8 %all-to-all-start.3 = ((bf16[64,16,128]{2,1,0:T(8,128)(2,1)}), bf16[64,16,128]{2,1,0:T(8,128)(2,1)S(1)}, u32[]{:S(2)}, u32[]{:S(2)}) async-start(bf16[64,16,128]{2,1,0:T(8,128)(2,1)} %shard_map.120), calls=%async_computation.3 | async-start | bytes 524288 | tf_op jit(solution)/shard_map/all_to_all | solution.py:326
  121.5 1.4 copy-done.7
  122.9 7.6 %shard_map.121 = (bf16[2,128,128]{2,1,0:T(8,128)(2,1)}, f32[2,128,512]{2,1,0:T(8,128)}, f32[2,128,512]{2,1,0:T(8,128)}, bf16[2048,512]{1,0:T(8,128)(2,1)}) custom-call(s32[5]{0:T(128)} %copy-done.5, bf16[288,2048]{1,0:T(8,128)(2,1)} %copy-done, bf16[8,4,32,1152]{3,2,1,0:T(8,128)(2,1)} %bitcast.26, bf16[8,4,32,1152]{3,2,1,0:T(8,128)(2,1)} %copy-done.7, ...), custom_call_target="tpu_custom_call" | custom-call | tf_op jit(solution)/shard_map/pallas_call | solution.py:327
  130.5 2.2 %all-to-all-done.3 = bf16[64,16,128]{2,1,0:T(8,128)(2,1)S(1)} async-done(((bf16[64,16,128]{2,1,0:T(8,128)(2,1)}), bf16[64,16,128]{2,1,0:T(8,128)(2,1)S(1)}, u32[]{:S(2)}, u32[]{:S(2)}) %all-to-all-start.3) | async-done | bytes 262176 | tf_op jit(solution)/shard_map/all_to_all | solution.py:326
  133.3 5.9 %shard_map.122 = bf16[4,2,128,256]{3,2,1,0:T(8,128)(2,1)} custom-call(bf16[1024,128]{1,0:T(8,128)(2,1)} %bitcast.27, bf16[2,128,128]{2,1,0:T(8,128)(2,1)} %get-tuple-element.27.map_ref, f32[2,128,512]{2,1,0:T(8,128)} %get-tuple-element.28.inner_in, f32[2,128,512]{2,1,0:T(8,128)} %get-tuple-element.29.gate_in, ...), custom_call_target="tpu_custom_call" | custom-call | tf_op jit(solution)/shard_map/pallas_call | solution.py:340
  139.2 3.5 %all-to-all-start.4 = ((bf16[4,2,128,256]{3,2,1,0:T(8,128)(2,1)}), bf16[4,2,128,256]{3,2,1,0:T(8,128)(2,1)S(1)}, u32[]{:S(2)}, u32[]{:S(2)}) async-start(bf16[4,2,128,256]{3,2,1,0:T(8,128)(2,1)} %shard_map.122), calls=%async_computation.4 | async-start | bytes 1048576 | tf_op jit(solution)/shard_map/all_to_all | solution.py:352
  142.7 10.1 %all-to-all-done.4 = bf16[4,2,128,256]{3,2,1,0:T(8,128)(2,1)S(1)} async-done(((bf16[4,2,128,256]{3,2,1,0:T(8,128)(2,1)}), bf16[4,2,128,256]{3,2,1,0:T(8,128)(2,1)S(1)}, u32[]{:S(2)}, u32[]{:S(2)}) %all-to-all-start.4) | async-done | bytes 524320 | tf_op jit(solution)/shard_map/all_to_all | solution.py:352
  152.9 5.0 %collective-permute-start.12 = (bf16[128,256]{1,0:T(8,128)(2,1)S(1)}, bf16[128,256]{1,0:T(8,128)(2,1)S(1)}, u32[]{:S(2)}, u32[]{:S(2)}) collective-permute-start(bf16[128,256]{1,0:T(8,128)(2,1)S(1)} %fusion.1), channel_id=1, source_target_pairs={{0,4},{4,0},{1,5},{5,1},{2,6},{6,2},{3,7},{7,3},{8,12},{12,8},{9,1... | collective-permute-start | bytes 196616 | tf_op jit(solution)/shard_map/ppermute | solution.py:355
  158.0 5.5 %collective-permute-done.12 = bf16[128,256]{1,0:T(8,128)(2,1)S(1)} collective-permute-done((bf16[128,256]{1,0:T(8,128)(2,1)S(1)}, bf16[128,256]{1,0:T(8,128)(2,1)S(1)}, u32[]{:S(2)}, u32[]{:S(2)}) %collective-permute-start.12) | collective-permute-done | bytes 65568 | tf_op jit(solution)/shard_map/ppermute | solution.py:355
  (72 shorter events, 7.7 us)
Async XLA Ops:
  7.3 0.8 copy-start.4
  8.7 15.0 %copy-start.9 = (bf16[128,256]{1,0:T(8,128)(2,1)S(1)}, bf16[128,256]{1,0:T(8,128)(2,1)}, u32[]{:S(2)}) copy-start(bf16[128,256]{1,0:T(8,128)(2,1)} %param.12) | copy-start | bytes 196612
  8.7 16.9 %slice-start = ((bf16[32,256]{1,0:T(8,128)(2,1)}), bf16[32,128]{1,0:T(8,128)(2,1)S(1)}, s32[]{:S(2)}) async-start(bf16[32,256]{1,0:T(8,128)(2,1)} %maps_ref.1), calls=%async_computation.6 | async-start | bytes 16384 | tf_op jit(solution)/shard_map/slice | solution.py:284
  8.7 16.9 %copy-start.10 = (bf16[32,512]{1,0:T(8,128)(2,1)S(1)}, bf16[32,512]{1,0:T(8,128)(2,1)}, u32[]{:S(2)}) copy-start(bf16[32,512]{1,0:T(8,128)(2,1)} %param.14) | copy-start | bytes 98308
  8.7 16.9 %copy-start.11 = (bf16[512,32]{0,1:T(8,128)(2,1)S(1)}, bf16[512,32]{0,1:T(8,128)(2,1)}, u32[]{:S(2)}) copy-start(bf16[512,32]{0,1:T(8,128)(2,1)} %param.23) | copy-start | bytes 98308
  9.8 44.5 %all-to-all-start = ((bf16[16,32,768]{2,1,0:T(8,128)(2,1)}), bf16[16,32,768]{2,1,0:T(8,128)(2,1)S(1)}, u32[]{:S(2)}, u32[]{:S(2)}) async-start(bf16[16,32,768]{2,1,0:T(8,128)(2,1)} %shard_map.118), calls=%async_computation | async-start | bytes 1572864 | tf_op jit(solution)/shard_map/all_to_all | solution.py:285
  23.6 87.5 %all-gather.3.cloned.1.call-start = ((), (), s32[]{:S(2)}) async-start(), calls=%async_computation.5 | async-start | bytes 2654208 | tf_op jit(solution)/shard_map/all_gather | solution.py:292
  23.7 18.8 %collective-permute-start.3 = (bf16[16,256]{1,0:T(8,128)(2,1)S(1)}, bf16[16,256]{1,0:T(8,128)(2,1)S(1)}, u32[]{:S(2)}, u32[]{:S(2)}) collective-permute-start(bf16[16,256]{1,0:T(8,128)(2,1)S(1)} %get-tuple-element.36), channel_id=1, source_target_pairs={{0,8},{8,16},{16,24},{24,32},{32,40},{40,48},{48,56},{56,64},{64,7... | collective-permute-start | bytes 24584 | tf_op jit(solution)/shard_map/ppermute | solution.py:244
  25.7 23.2 %collective-permute-start.1 = (bf16[32,1152]{1,0:T(8,128)(2,1)S(1)}, bf16[32,1152]{1,0:T(8,128)(2,1)S(1)}, u32[]{:S(2)}, u32[]{:S(2)}) collective-permute-start(bf16[32,1152]{1,0:T(8,128)(2,1)S(1)} %get-tuple-element.34), channel_id=1, source_target_pairs={{0,256},{128,384},{256,0},{384,128},{1,257},{129,385},{257,1},{385... | collective-permute-start | bytes 221192 | tf_op jit(solution)/shard_map/ppermute | solution.py:261
  29.9 19.0 %collective-permute-start = (bf16[32,1152]{1,0:T(8,128)(2,1)S(1)}, bf16[32,1152]{1,0:T(8,128)(2,1)S(1)}, u32[]{:S(2)}, u32[]{:S(2)}) collective-permute-start(bf16[32,1152]{1,0:T(8,128)(2,1)S(1)} %get-tuple-element.34), channel_id=1, source_target_pairs={{0,128},{128,256},{256,384},{384,0},{1,129},{129,257},{257,385},{3... | collective-permute-start | bytes 221192 | tf_op jit(solution)/shard_map/ppermute | solution.py:261
  31.9 17.1 %collective-permute-start.2 = (bf16[32,1152]{1,0:T(8,128)(2,1)S(1)}, bf16[32,1152]{1,0:T(8,128)(2,1)S(1)}, u32[]{:S(2)}, u32[]{:S(2)}) collective-permute-start(bf16[32,1152]{1,0:T(8,128)(2,1)S(1)} %get-tuple-element.34), channel_id=1, source_target_pairs={{0,384},{128,0},{256,128},{384,256},{1,385},{129,1},{257,129},{385... | collective-permute-start | bytes 221192 | tf_op jit(solution)/shard_map/ppermute | solution.py:261
  35.8 8.1 %collective-permute-start.4 = (bf16[16,256]{1,0:T(8,128)(2,1)S(1)}, bf16[16,256]{1,0:T(8,128)(2,1)S(1)}, u32[]{:S(2)}, u32[]{:S(2)}) collective-permute-start(bf16[16,256]{1,0:T(8,128)(2,1)S(1)} %get-tuple-element.35), channel_id=1, source_target_pairs={{8,0},{16,8},{24,16},{32,24},{40,32},{48,40},{56,48},{64,56},{72,6... | collective-permute-start | bytes 24584 | tf_op jit(solution)/shard_map/ppermute | solution.py:244
  43.9 10.4 %collective-permute-start.5 = (bf16[160,256]{1,0:T(8,128)(2,1)S(1)}, bf16[160,256]{1,0:T(8,128)(2,1)S(1)}, u32[]{:S(2)}, u32[]{:S(2)}) collective-permute-start(bf16[160,256]{1,0:T(8,128)(2,1)S(1)} %constant_dynamic-update-slice_fusion), channel_id=1, source_target_pairs={{0,4},{4,0},{1,5},{5,1},{2,6},{6,2},{3,7},{7,3},{8,12},{12,8},{9,1... | collective-permute-start | bytes 245768 | tf_op jit(solution)/shard_map/ppermute | solution.py:289
  48.9 29.9 %copy-start.16 = (f32[8]{0:T(128)S(1)}, f32[8]{0:T(128)}, u32[]{:S(2)}) copy-start(f32[8]{0:T(128)} %param.17) | copy-start | bytes 100
  48.9 29.9 %copy-start.15 = (f32[8]{0:T(128)S(1)}, f32[8]{0:T(128)}, u32[]{:S(2)}) copy-start(f32[8]{0:T(128)} %param.18) | copy-start | bytes 100
  49.0 30.1 %copy-start.13 = (f32[4,256]{1,0:T(4,128)S(1)}, f32[4,256]{1,0:T(4,128)}, u32[]{:S(2)}) copy-start(f32[4,256]{1,0:T(4,128)} %param.21) | copy-start | bytes 12292
  49.7 29.3 %copy-start.12 = (f32[4,512]{1,0:T(4,128)S(1)}, f32[4,512]{1,0:T(4,128)}, u32[]{:S(2)}) copy-start(f32[4,512]{1,0:T(4,128)} %param.20) | copy-start | bytes 24580
  55.2 17.5 %collective-permute-start.7 = (bf16[8,32,768]{2,1,0:T(8,128)(2,1)S(1)}, bf16[8,32,768]{2,1,0:T(8,128)(2,1)S(1)}, u32[]{:S(2)}, u32[]{:S(2)}) collective-permute-start(bf16[8,32,768]{2,1,0:T(8,128)(2,1)S(1)} %get-tuple-element.31), channel_id=1, source_target_pairs={{0,112},{16,0},{32,16},{48,32},{64,48},{80,64},{96,80},{112,96},{1... | collective-permute-start | bytes 1179656 | tf_op jit(solution)/shard_map/ppermute | solution.py:254
  58.3 16.3 %collective-permute-start.6 = (bf16[8,32,768]{2,1,0:T(8,128)(2,1)}, bf16[8,32,768]{2,1,0:T(8,128)(2,1)S(1)}, u32[]{:S(2)}, u32[]{:S(2)}) collective-permute-start(bf16[8,32,768]{2,1,0:T(8,128)(2,1)} %get-tuple-element.32), channel_id=1, source_target_pairs={{0,16},{16,32},{32,48},{48,64},{64,80},{80,96},{96,112},{112,0},{1... | collective-permute-start | bytes 1179656 | tf_op jit(solution)/shard_map/ppermute | solution.py:253
  61.0 22.7 %collective-permute-start.8 = (bf16[16,32,768]{2,1,0:T(8,128)(2,1)S(1)}, bf16[16,32,768]{2,1,0:T(8,128)(2,1)S(1)}, u32[]{:S(2)}, u32[]{:S(2)}) collective-permute-start(bf16[16,32,768]{2,1,0:T(8,128)(2,1)S(1)} %all-to-all-done.n0), channel_id=1, source_target_pairs={{0,8},{8,0},{1,9},{9,1},{2,10},{10,2},{3,11},{11,3},{4,12},{12,4},... | collective-permute-start | bytes 2359304 | tf_op jit(solution)/shard_map/ppermute | solution.py:248
  68.4 15.4 %all-to-all-start.1 = ((bf16[4,2,160,256]{3,2,1,0:T(8,128)(2,1)}), bf16[4,2,160,256]{3,2,1,0:T(8,128)(2,1)S(1)}, u32[]{:S(2)}, u32[]{:S(2)}) async-start(bf16[4,2,160,256]{3,2,1,0:T(8,128)(2,1)} %broadcast_in_dim.21), calls=%async_computation.1 | async-start | bytes 1310720 | tf_op jit(solution)/shard_map/all_to_all | solution.py:238
  72.7 11.1 %collective-permute-start.10 = (bf16[8,32,768]{2,1,0:T(8,128)(2,1)S(1)}, bf16[8,32,768]{2,1,0:T(8,128)(2,1)S(1)}, u32[]{:S(2)}, u32[]{:S(2)}) collective-permute-start(bf16[8,32,768]{2,1,0:T(8,128)(2,1)S(1)} %collective-permute-done.7.r0), channel_id=1, source_target_pairs={{0,8},{8,0},{1,9},{9,1},{2,10},{10,2},{3,11},{11,3},{4,12},{12,4},... | collective-permute-start | bytes 1179656 | tf_op jit(solution)/shard_map/ppermute | solution.py:248
  74.6 9.1 %collective-permute-start.9 = (bf16[8,32,768]{2,1,0:T(8,128)(2,1)S(1)}, bf16[8,32,768]{2,1,0:T(8,128)(2,1)}, u32[]{:S(2)}, u32[]{:S(2)}) collective-permute-start(bf16[8,32,768]{2,1,0:T(8,128)(2,1)S(1)} %collective-permute-done.6.l0), channel_id=1, source_target_pairs={{0,8},{8,0},{1,9},{9,1},{2,10},{10,2},{3,11},{11,3},{4,12},{12,4},... | collective-permute-start | bytes 1179656 | tf_op jit(solution)/shard_map/ppermute | solution.py:248
  79.0 35.9 %copy-start.5 = (s32[5]{0:T(128)}, s32[5]{0:T(128)S(1)}, u32[]{:S(2)}) copy-start(s32[5]{0:T(128)S(1)} %stack.47.place_ref) | copy-start | bytes 64
  79.0 41.6 %copy-start.17 = (f32[8]{0:T(128)S(1)}, f32[8]{0:T(128)}, u32[]{:S(2)}) copy-start(f32[8]{0:T(128)} %param.19) | copy-start | bytes 100
  79.1 41.8 %copy-start.14 = (f32[512]{0:T(512)S(1)}, f32[512]{0:T(512)}, u32[]{:S(2)}) copy-start(f32[512]{0:T(512)} %param.22) | copy-start | bytes 6148
  88.1 1.1 copy-start
  111.1 10.3 %collective-permute-start.11 = (bf16[8,4,32,1152]{3,2,1,0:T(8,128)(2,1)}, bf16[8,4,32,1152]{3,2,1,0:T(8,128)(2,1)S(1)}, u32[]{:S(2)}, u32[]{:S(2)}) collective-permute-start(bf16[8,4,32,1152]{3,2,1,0:T(8,128)(2,1)} %bitcast.25), channel_id=1, source_target_pairs={{0,8},{8,0},{1,9},{9,1},{2,10},{10,2},{3,11},{11,3},{4,12},{12,4},... | collective-permute-start | bytes 7077896 | tf_op jit(solution)/shard_map/ppermute | solution.py:248
  114.9 17.7 %all-to-all-start.3 = ((bf16[64,16,128]{2,1,0:T(8,128)(2,1)}), bf16[64,16,128]{2,1,0:T(8,128)(2,1)S(1)}, u32[]{:S(2)}, u32[]{:S(2)}) async-start(bf16[64,16,128]{2,1,0:T(8,128)(2,1)} %shard_map.120), calls=%async_computation.3 | async-start | bytes 524288 | tf_op jit(solution)/shard_map/all_to_all | solution.py:326
  121.5 1.4 copy-start.7
  139.2 13.6 %all-to-all-start.4 = ((bf16[4,2,128,256]{3,2,1,0:T(8,128)(2,1)}), bf16[4,2,128,256]{3,2,1,0:T(8,128)(2,1)S(1)}, u32[]{:S(2)}, u32[]{:S(2)}) async-start(bf16[4,2,128,256]{3,2,1,0:T(8,128)(2,1)} %shard_map.122), calls=%async_computation.4 | async-start | bytes 1048576 | tf_op jit(solution)/shard_map/all_to_all | solution.py:352
  152.9 10.5 %collective-permute-start.12 = (bf16[128,256]{1,0:T(8,128)(2,1)S(1)}, bf16[128,256]{1,0:T(8,128)(2,1)S(1)}, u32[]{:S(2)}, u32[]{:S(2)}) collective-permute-start(bf16[128,256]{1,0:T(8,128)(2,1)S(1)} %fusion.1), channel_id=1, source_target_pairs={{0,4},{4,0},{1,5},{5,1},{2,6},{6,2},{3,7},{7,3},{8,12},{12,8},{9,1... | collective-permute-start | bytes 196616 | tf_op jit(solution)/shard_map/ppermute | solution.py:355
  (5 other events, 3.5 us)
Sparse Core Ops, SparseCore 0:
  54.5 44.8 all-gather.2
